TPU v7x, 256 devices: a whole 4x4x8 slice. The times are simulated.
256 devices in a mesh: tmpl: 2 (over x_hi), row: 16 (over z, core), col: 8 (over x_lo, y).
Axes of the slice: x: 4 (x_hi: 2, x_lo: 2; x = x_hi * 2 + x_lo), y: 4, z: 8, core: 2. Of those that a mesh axis runs over, the one named last changes fastest.
Arguments:
- template_pair: bfloat16 [4, 256, 256, 64], P('tmpl', 'row', 'col'), may hold values from -6 to 6
- template_mask: int32 [4], P('tmpl'), may hold values from 0 to 1, as said below
- pair_mask: int32 [256, 256], P('row', 'col'), may hold values 0 or 1
- main_pair: bfloat16 [256, 256, 128], P('row', 'col'), may hold values from -6 to 6
- update_cotangent: bfloat16 [256, 256, 128], P('row', 'col'), may hold values from -2.390625 to 2.390625
- gain_in: float32 [64], replicated, may hold values from 0.1 to 1.9
- proj_a: bfloat16 [64, 64], replicated, may hold values from -0.75 to 0.75
- gate_a: bfloat16 [64, 64], replicated, may hold values from -0.75 to 0.75
- proj_b: bfloat16 [64, 64], replicated, may hold values from -0.75 to 0.75
- gate_b: bfloat16 [64, 64], replicated, may hold values from -0.75 to 0.75
- gain_mid: float32 [64], replicated, may hold values from 0.1 to 1.9
- proj_out: bfloat16 [64, 64], replicated, may hold values from -0.75 to 0.75
- gate_out: bfloat16 [64, 64], replicated, may hold values from -0.75 to 0.75
- gain_final: float32 [64], replicated, may hold values from 0.1 to 1.9
- key_weight: bfloat16 [64, 64], replicated, may hold values from -0.75 to 0.75
- value_weight: bfloat16 [64, 64], replicated, may hold values from -0.75 to 0.75
- query_weight: bfloat16 [128, 64], replicated, may hold values from -0.5 to 0.5
- output_weight: bfloat16 [64, 128], replicated, may hold values from -0.75 to 0.75
Outputs:
- pair_grad: bfloat16 [4, 256, 256, 64], P('tmpl', 'row', 'col')
- main_grad: bfloat16 [256, 256, 128], P('row', 'col')
Inputs may be any that keep to these rules, and one draw needn't show every extreme that they name: `template_mask`: exactly one of the 4 templates is absent (0); all others are present (1).
All inputs are finite; a program needn't handle non-finite values. No bound on the sum of `pair_mask` on one device may be relied on, other than what follows from the above.
Results may differ from a plain program's by a relative error of at most 0.027.
Values may be sent and summed in bfloat16 or wider, within the bound.
No kernel may reach another device: no remote copies, remote signals or barrier semaphores. Data moves between devices by JAX's collectives and lax.ppermute only.
A program may use at most 128 MiB of HBM per device.

v0:
```python
import math

import jax
import jax.numpy as jnp
from jax import lax
from jax.sharding import PartitionSpec as P

HEADS = 4
HEAD_DIM = 16


EPS = 1e-05


def normalize(inputs, gain_vec):
    mean_val = jnp.mean(inputs, axis=-1, keepdims=True)
    centered = inputs - mean_val
    variance = jnp.mean(centered * centered, axis=-1, keepdims=True)
    return centered * lax.rsqrt(variance + EPS) * gain_vec


def project(normed, weight):
    return jnp.dot(normed, weight, preferred_element_type=jnp.float32)


def front(pair_in, mask_cells, gain_in, proj_a, gate_a, proj_b, gate_b):
    normed = normalize(pair_in.astype(jnp.float32), gain_in).astype(jnp.bfloat16)
    keep_mask = mask_cells.astype(jnp.float32)[..., None]
    left_proj = (
        keep_mask * jax.nn.sigmoid(project(normed, gate_a)) * project(normed, proj_a)
    ).astype(jnp.bfloat16)
    right_proj = (
        keep_mask * jax.nn.sigmoid(project(normed, gate_b)) * project(normed, proj_b)
    ).astype(jnp.bfloat16)
    return (left_proj, right_proj)


def back(
    pair_in, product, gain_in, gain_mid, proj_out, gate_out, gain_final, key_weight, value_weight
):
    normed = normalize(pair_in.astype(jnp.float32), gain_in).astype(jnp.bfloat16)
    gating = jax.nn.sigmoid(project(normed, gate_out))
    mixed_norm = normalize(product.astype(jnp.float32), gain_mid).astype(jnp.bfloat16)
    updated = pair_in.astype(jnp.float32) + gating * project(mixed_norm, proj_out)
    final_norm = normalize(updated, gain_final).astype(jnp.bfloat16)
    return (
        project(final_norm, key_weight).astype(jnp.bfloat16),
        project(final_norm, value_weight).astype(jnp.bfloat16),
    )


def split_heads(array_in):
    return array_in.reshape(array_in.shape[:-1] + (HEADS, array_in.shape[-1] // HEADS))


def sum_query(term_in):
    return lax.psum(term_in, "tmpl")


def body(
    template_pair,
    template_mask,
    pair_mask,
    main_pair,
    update_cotangent,
    gain_in,
    proj_a,
    gate_a,
    proj_b,
    gate_b,
    gain_mid,
    proj_out,
    gate_out,
    gain_final,
    key_weight,
    value_weight,
    query_weight,
    output_weight,
):

    def front_of(pair_in):
        return front(pair_in, pair_mask, gain_in, proj_a, gate_a, proj_b, gate_b)

    (left_proj, right_proj), front_vjp = jax.vjp(front_of, template_pair)
    right_rows = lax.all_gather(right_proj, "row", axis=1, tiled=True)
    mixed_sum = lax.psum_scatter(
        jnp.einsum("sikc,sjkc->jsic", left_proj, right_rows, preferred_element_type=jnp.float32),
        "col",
        scatter_dimension=0,
        tiled=True,
    )
    product = jnp.transpose(mixed_sum, (1, 2, 0, 3)).astype(jnp.bfloat16)

    def back_of(pair_in, product_in):
        return back(
            pair_in,
            product_in,
            gain_in,
            gain_mid,
            proj_out,
            gate_out,
            gain_final,
            key_weight,
            value_weight,
        )

    (key_proj, value_proj), back_vjp = jax.vjp(back_of, template_pair, product)
    query_proj = project(main_pair, query_weight).astype(jnp.bfloat16)
    grad_out = project(update_cotangent, output_weight.T)
    present = template_mask.astype(jnp.float32)[:, None, None, None]
    score_scale = 1.0 / math.sqrt(HEAD_DIM)
    query_heads = split_heads(query_proj.astype(jnp.float32))[None]
    key_heads = split_heads(key_proj.astype(jnp.float32))
    value_heads = split_heads(value_proj.astype(jnp.float32))
    out_heads = split_heads(grad_out)[None]
    exp_terms = present * jnp.exp(jnp.sum(query_heads * key_heads, -1) * score_scale)
    along_heads = jnp.sum(out_heads * value_heads, -1)
    weight_sum = lax.psum(jnp.sum(exp_terms, 0), "tmpl")
    weights = exp_terms / weight_sum
    average = lax.psum(jnp.sum(weights * along_heads, 0), "tmpl")
    slope_term = weights * (along_heads - average)
    query_sum = sum_query(jnp.sum(slope_term[..., None] * key_heads, 0) * score_scale)
    query_grad = query_sum.reshape(query_proj.shape).astype(jnp.bfloat16)
    main_grad = project(query_grad, query_weight.T).astype(jnp.bfloat16)
    key_grad = (
        (slope_term[..., None] * query_heads * score_scale)
        .reshape(key_proj.shape)
        .astype(jnp.bfloat16)
    )
    value_grad = (weights[..., None] * out_heads).reshape(value_proj.shape).astype(jnp.bfloat16)
    back_grad, product_grad = back_vjp((key_grad, value_grad))
    product_cols = lax.all_gather(product_grad, "col", axis=2, tiled=True)
    left_grad = jnp.einsum(
        "sijc,sjkc->sikc", product_cols, right_rows, preferred_element_type=jnp.float32
    ).astype(jnp.bfloat16)
    summed = lax.psum_scatter(
        jnp.einsum("sijc,sikc->jskc", product_cols, left_proj, preferred_element_type=jnp.float32),
        "row",
        scatter_dimension=0,
        tiled=True,
    )
    right_grad = jnp.transpose(summed, (1, 0, 2, 3)).astype(jnp.bfloat16)
    (front_grad,) = front_vjp((left_grad, right_grad))
    pair_grad = (front_grad.astype(jnp.float32) + back_grad.astype(jnp.float32)).astype(
        jnp.bfloat16
    )
    return (pair_grad, main_grad)


def solution(mesh):
    placed = (
        P("tmpl", "row", "col", None),
        P("tmpl"),
        P("row", "col"),
        P("row", "col", None),
        P("row", "col", None),
        P(),
        P(),
        P(),
        P(),
        P(),
        P(),
        P(),
        P(),
        P(),
        P(),
        P(),
        P(),
        P(),
    )
    return jax.shard_map(
        body,
        mesh=mesh,
        in_specs=placed,
        out_specs=(P("tmpl", "row", "col", None), P("row", "col", None)),
        check_vma=False,
    )
```

profile of v0, /device:TPU:6, one launch (start us, length us, event | category | flops | bytes accessed | tf_op | source)
XLA Modules:
  0.0 330.0 jit_solution(5352120777696271654)
XLA Ops:
  11.1 1.4 fusion.5
  12.5 1.6 fusion.87
  14.2 1.6 fusion.8
  16.6 2.3 multiply_convert_fusion.4
  19.4 44.7 %all-gather.3.cloned.1.call-done = bf16[2,256,32,64]{3,2,1,0:T(8,128)(2,1)} async-done(((bf16[2,16,32,64]{3,2,1,0:T(8,128)(2,1)}), bf16[2,256,32,64]{3,2,1,0:T(8,128)(2,1)}) %all-gather.3.cloned.1.call-update) | async-done | bytes 2097168 | tf_op jit(solution)/shard_map/all_gather | solution.py:85
  64.1 13.4 %copy.47 = bf16[2,256,32,64]{2,1,3,0:T(8,128)(2,1)} copy(bf16[2,256,32,64]{3,2,1,0:T(8,128)(2,1)} %all-gather.3.cloned.1.call-done) | data formatting | bytes 4194304 | tf_op jit(solution)/shard_map/all_gather | solution.py:85
  77.5 5.7 %convolution_bitcast_fusion.1 = f32[256,2,16,64]{0,2,3,1:T(8,128)S(1)} fusion(bf16[2,256,32,64]{2,1,3,0:T(8,128)(2,1)} %copy.47, bf16[2,16,32,64]{2,1,3,0:T(8,128)(2,1)S(1)} %copy.59), kind=kOutput, calls=%fused_computation.1 | convolution fusion | flops 33554432 | bytes 4325376 | tf_op jit(solution)/shard_map/sikc,sjkc->jsic/dot_general | solution.py:87
  83.3 4.4 %copy.49 = f32[256,2,16,64]{3,2,1,0:T(8,128)} copy(f32[256,2,16,64]{0,2,3,1:T(8,128)S(1)} %convolution_bitcast_fusion.1) | data formatting | bytes 4194304 | tf_op jit(solution)/shard_map/sikc,sjkc->jsic/transpose | solution.py:87
  88.6 52.9 %reduce-scatter.5.cloned.1.call-done = f32[32,2,16,64]{3,2,1,0:T(8,128)} async-done(((f32[256,2,16,64]{3,2,1,0:T(8,128)}), f32[32,2,16,64]{3,2,1,0:T(8,128)}) %reduce-scatter.5.cloned.1.call-update) | async-done | bytes 262160 | tf_op jit(solution)/shard_map/reduce_scatter | solution.py:86
  141.5 1.5 bitcast_reduce_fusion
  146.2 1.4 copy.55
  149.4 1.5 multiply_reduce_fusion.1
  151.0 9.5 %psum.21 = f32[16,32,4]{1,2,0:T(4,128)S(1)} all-reduce(f32[16,32,4]{1,2,0:T(4,128)S(1)} %fusion.83), channel_id=1, replica_groups=mesh['tmpl'=2,'row'=16,'col'=8] {'tmpl'}, use_global_device_ids=true, to_apply=%region_9.0 | all-reduce | flops 2048 | bytes 16384 | tf_op jit(solution)/shard_map/psum | solution.py:118
  160.6 1.5 multiply_reduce_fusion
  162.9 10.9 %psum.22 = f32[16,32,4]{1,2,0:T(4,128)S(1)} all-reduce(f32[16,32,4]{1,2,0:T(4,128)S(1)} %get-tuple-element.8), channel_id=1, replica_groups=mesh['tmpl'=2,'row'=16,'col'=8] {'tmpl'}, use_global_device_ids=true, to_apply=%region_12.0 | all-reduce | flops 2048 | bytes 16384 | tf_op jit(solution)/shard_map/psum | solution.py:120
  176.4 1.4 fusion.118
  177.8 1.6 fusion.53
  182.3 42.8 %all-gather.5.cloned.1.call-done = bf16[2,16,256,64]{3,1,0,2:T(8,128)(2,1)} async-done(((bf16[2,16,32,64]{3,1,0,2:T(8,128)(2,1)}), bf16[2,16,256,64]{3,1,0,2:T(8,128)(2,1)}) %all-gather.5.cloned.1.call-update) | async-done | bytes 1048592 | tf_op jit(solution)/shard_map/all_gather | solution.py:132
  225.1 4.1 %copy.60 = bf16[2,16,256,64]{2,1,3,0:T(8,128)(2,1)S(1)} copy(bf16[2,16,256,64]{3,1,0,2:T(8,128)(2,1)} %all-gather.5.cloned.1.call-done) | data formatting | bytes 2097152 | tf_op jit(solution)/shard_map/all_gather | solution.py:132
  229.2 3.7 %convolution_bitcast_fusion = f32[256,2,32,64]{0,2,3,1:T(8,128)} fusion(bf16[2,16,32,64]{2,1,3,0:T(8,128)(2,1)} %copy-done.9, bf16[2,16,256,64]{2,1,3,0:T(8,128)(2,1)S(1)} %copy.60), kind=kOutput, calls=%fused_computation | convolution fusion | flops 33554432 | bytes 5373952 | tf_op jit(solution)/shard_map/sijc,sikc->jskc/dot_general | solution.py:137
  233.0 9.2 %copy.80 = f32[256,2,32,64]{3,2,1,0:T(8,128)} copy(f32[256,2,32,64]{0,2,3,1:T(8,128)} %convolution_bitcast_fusion) | data formatting | bytes 8388608
  242.1 8.0 %reshape.145 = f32[256,4096]{1,0:T(8,128)} reshape(f32[256,2,32,64]{3,2,1,0:T(8,128)} %copy.80) | data formatting | bytes 8388608
  254.4 18.5 %all-reduce.1 = bf16[16,32,4,16]{1,3,2,0:T(8,128)(2,1)} all-reduce(f32[16,32,4,16]{1,3,2,0:T(8,128)S(1)} %bitcast.159), channel_id=1, replica_groups=mesh['tmpl'=2,'row'=16,'col'=8] {'tmpl'}, use_global_device_ids=true, to_apply=%region_23.0 | all-reduce | flops 32768 | bytes 196608 | tf_op jit(solution)/shard_map/psum | solution.py:57
  272.9 1.8 convolution_convert_fusion.10
  274.7 1.6 fusion.10
  276.3 5.5 %fusion.121 = bf16[2,64,32,16]{2,3,1,0:T(8,128)(2,1)} fusion(bf16[2,16,256,64]{2,1,3,0:T(8,128)(2,1)S(1)} %copy.60, bf16[2,256,32,64]{2,1,3,0:T(8,128)(2,1)} %copy.47), kind=kOutput, calls=%fused_computation.178 | convolution fusion | flops 33554432 | bytes 3276800 | tf_op jit(solution)/shard_map/sijc,sjkc->sikc/dot_general | solution.py:133
  281.8 1.5 copy.64
  283.2 1.7 convolution_convert_fusion.2
  285.0 28.0 %reduce-scatter.7.cloned.1.call-done = f32[16,4096]{1,0:T(8,128)} async-done(((f32[256,4096]{1,0:T(8,128)}), f32[16,4096]{1,0:T(8,128)}) %reduce-scatter.7.cloned.1.call-update) | async-done | bytes 262160
  316.9 1.7 fusion.34
  319.3 1.7 fusion.78
  321.0 2.5 add_convert_fusion
  (122 shorter events, 26.0 us)
Async XLA Ops:
  7.2 80.7 %copy-start = (bf16[16,32,128]{2,1,0:T(8,128)(2,1)S(1)}, bf16[16,32,128]{2,1,0:T(8,128)(2,1)}, u32[]{:S(2)}) copy-start(bf16[16,32,128]{2,1,0:T(8,128)(2,1)} %param.21) | copy-start | bytes 393220
  7.2 56.9 %all-gather.3.cloned.1.call-start = ((), (), s32[]{:S(2)}) async-start(), calls=%async_computation.2 | async-start | bytes 4456448 | tf_op jit(solution)/shard_map/all_gather | solution.py:85
  10.4 133.5 %copy-start.14 = (f32[2,16,32]{2,1,0:T(8,128)}, f32[2,16,32]{2,1,0:T(8,128)S(1)}, u32[]{:S(2)}) copy-start(f32[2,16,32]{2,1,0:T(8,128)S(1)} %fusion.106) | copy-start | bytes 12292
  11.1 66.4 %copy-start.15 = (f32[16,32]{1,0:T(8,128)}, f32[16,32]{1,0:T(8,128)S(1)}, u32[]{:S(2)}) copy-start(f32[16,32]{1,0:T(8,128)S(1)} %convert_element_type.147) | copy-start | bytes 6148
  12.5 6.4 %copy-start.4 = (f32[2,16,32,64]{3,2,1,0:T(8,128)}, f32[2,16,32,64]{3,2,1,0:T(8,128)S(1)}, u32[]{:S(2)}) copy-start(f32[2,16,32,64]{3,2,1,0:T(8,128)S(1)} %fusion.5) | copy-start | bytes 786436
  14.2 4.8 %copy-start.6 = (f32[2,16,32,64]{3,2,1,0:T(8,128)}, f32[2,16,32,64]{3,2,1,0:T(8,128)S(1)}, u32[]{:S(2)}) copy-start(f32[2,16,32,64]{3,2,1,0:T(8,128)S(1)} %fusion.87) | copy-start | bytes 786436
  18.9 122.6 %reduce-scatter.5.cloned.1.call-start = ((), (), s32[]{:S(2)}) async-start(), calls=%async_computation.3 | async-start | bytes 4718592 | tf_op jit(solution)/shard_map/reduce_scatter | solution.py:86
  19.4 63.7 %copy-start.9 = (bf16[2,16,32,64]{2,1,3,0:T(8,128)(2,1)}, bf16[2,16,32,64]{2,1,3,0:T(8,128)(2,1)S(1)}, u32[]{:S(2)}) copy-start(bf16[2,16,32,64]{2,1,3,0:T(8,128)(2,1)S(1)} %copy.59) | copy-start | bytes 393220
  77.5 10.3 %copy-start.27 = (bf16[128,64]{0,1:T(8,128)(2,1)S(1)}, bf16[128,64]{0,1:T(8,128)(2,1)}, u32[]{:S(2)}) copy-start(bf16[128,64]{0,1:T(8,128)(2,1)} %param.34) | copy-start | bytes 49156
  83.2 5.1 %copy-start.34 = (s32[2]{0:T(128)S(1)}, s32[2]{0:T(128)}, u32[]{:S(2)}) copy-start(s32[2]{0:T(128)} %param.19) | copy-start | bytes 28
  83.2 5.1 %copy-start.23 = (bf16[16,32,128]{2,1,0:T(8,128)(2,1)S(1)}, bf16[16,32,128]{2,1,0:T(8,128)(2,1)}, u32[]{:S(2)}) copy-start(bf16[16,32,128]{2,1,0:T(8,128)(2,1)} %param.22) | copy-start | bytes 393220
  83.2 5.1 %copy-start.29 = (bf16[64,128]{1,0:T(8,128)(2,1)S(1)}, bf16[64,128]{1,0:T(8,128)(2,1)}, u32[]{:S(2)}) copy-start(bf16[64,128]{1,0:T(8,128)(2,1)} %param.35) | copy-start | bytes 49156
  83.2 60.2 %copy-start.26 = (bf16[64,64]{1,0:T(8,128)(2,1)S(1)}, bf16[64,64]{1,0:T(8,128)(2,1)}, u32[]{:S(2)}) copy-start(bf16[64,64]{1,0:T(8,128)(2,1)} %param.29) | copy-start | bytes 24580
  83.2 60.2 %copy-start.33 = (f32[64]{0:T(128)S(1)}, f32[64]{0:T(128)}, u32[]{:S(2)}) copy-start(f32[64]{0:T(128)} %param.28) | copy-start | bytes 772
  83.2 60.7 %copy-start.1 = (bf16[2,16,32,64]{3,2,1,0:T(8,128)(2,1)S(1)}, bf16[2,16,32,64]{3,2,1,0:T(8,128)(2,1)}, u32[]{:S(2)}) copy-start(bf16[2,16,32,64]{3,2,1,0:T(8,128)(2,1)} %param.18) | copy-start | bytes 393220
  83.3 60.7 %copy-start.28 = (bf16[64,64]{1,0:T(8,128)(2,1)S(1)}, bf16[64,64]{1,0:T(8,128)(2,1)}, u32[]{:S(2)}) copy-start(bf16[64,64]{1,0:T(8,128)(2,1)} %param.30) | copy-start | bytes 24580
  83.3 60.7 %copy-start.30 = (f32[64]{0:T(128)S(1)}, f32[64]{0:T(128)}, u32[]{:S(2)}) copy-start(f32[64]{0:T(128)} %param.23) | copy-start | bytes 772
  83.3 62.4 %copy-start.25 = (bf16[64,64]{1,0:T(8,128)(2,1)S(1)}, bf16[64,64]{1,0:T(8,128)(2,1)}, u32[]{:S(2)}) copy-start(bf16[64,64]{1,0:T(8,128)(2,1)} %param.33) | copy-start | bytes 24580
  83.3 62.4 %copy-start.31 = (f32[64]{0:T(128)S(1)}, f32[64]{0:T(128)}, u32[]{:S(2)}) copy-start(f32[64]{0:T(128)} %param.31) | copy-start | bytes 772
  87.8 59.8 %copy-start.24 = (bf16[64,64]{1,0:T(8,128)(2,1)S(1)}, bf16[64,64]{1,0:T(8,128)(2,1)}, u32[]{:S(2)}) copy-start(bf16[64,64]{1,0:T(8,128)(2,1)} %param.32) | copy-start | bytes 24580
  87.8 137.4 %all-gather.5.cloned.1.call-start = ((), (), s32[]{:S(2)}) async-start(), calls=%async_computation.4 | async-start | bytes 2359296 | tf_op jit(solution)/shard_map/all_gather | solution.py:132
  88.3 72.3 %copy-start.32 = (f32[2]{0:T(128)}, f32[2]{0:T(128)S(1)}, u32[]{:S(2)}) copy-start(f32[2]{0:T(128)S(1)} %convert_element_type.151) | copy-start | bytes 28
  145.2 31.1 %copy-start.11 = (f32[2,16,32]{2,1,0:T(8,128)}, f32[2,16,32]{2,1,0:T(8,128)S(1)}, u32[]{:S(2)}) copy-start(f32[2,16,32]{2,1,0:T(8,128)S(1)} %broadcast_multiply_fusion.1) | copy-start | bytes 12292
  145.7 14.9 %copy-start.17 = (f32[2,16,32]{2,1,0:T(8,128)}, f32[2,16,32]{2,1,0:T(8,128)S(1)}, u32[]{:S(2)}) copy-start(f32[2,16,32]{2,1,0:T(8,128)S(1)} %fusion.108) | copy-start | bytes 12292
  147.6 30.2 %copy-start.13 = (f32[2,16,32]{2,1,0:T(8,128)S(1)}, f32[2,16,32]{2,1,0:T(8,128)}, u32[]{:S(2)}) copy-start(f32[2,16,32]{2,1,0:T(8,128)} %copy-done.12) | copy-start | bytes 12292
  147.6 31.8 %copy-start.22 = (f32[2,16,32]{2,1,0:T(8,128)S(1)}, f32[2,16,32]{2,1,0:T(8,128)}, u32[]{:S(2)}) copy-start(f32[2,16,32]{2,1,0:T(8,128)} %copy-done.21) | copy-start | bytes 12292
  147.6 31.8 %copy-start.19 = (f32[2,16,32]{2,1,0:T(8,128)S(1)}, f32[2,16,32]{2,1,0:T(8,128)}, u32[]{:S(2)}) copy-start(f32[2,16,32]{2,1,0:T(8,128)} %copy-done.18) | copy-start | bytes 12292
  148.1 25.9 %copy-start.7 = (f32[2,16,32,64]{3,2,1,0:T(8,128)}, f32[2,16,32,64]{3,2,1,0:T(8,128)S(1)}, u32[]{:S(2)}) copy-start(f32[2,16,32,64]{3,2,1,0:T(8,128)S(1)} %fusion.14) | copy-start | bytes 786436
  182.3 130.8 %reduce-scatter.7.cloned.1.call-start = ((), (), s32[]{:S(2)}) async-start(), calls=%async_computation.5 | async-start | bytes 4456448
  242.1 9.2 %copy-start.8 = (f32[2,16,32,64]{3,2,1,0:T(8,128)S(1)}, f32[2,16,32,64]{3,2,1,0:T(8,128)}, u32[]{:S(2)}) copy-start(f32[2,16,32,64]{3,2,1,0:T(8,128)} %copy-done.7) | copy-start | bytes 786436
  251.3 31.9 %copy-start.5 = (f32[2,16,32,64]{3,2,1,0:T(8,128)S(1)}, f32[2,16,32,64]{3,2,1,0:T(8,128)}, u32[]{:S(2)}) copy-start(f32[2,16,32,64]{3,2,1,0:T(8,128)} %copy-done.4) | copy-start | bytes 786436
  252.5 61.7 %copy-start.3 = (f32[2,16,32,64]{3,2,1,0:T(8,128)S(1)}, f32[2,16,32,64]{3,2,1,0:T(8,128)}, u32[]{:S(2)}) copy-start(f32[2,16,32,64]{3,2,1,0:T(8,128)} %copy-done.2) | copy-start | bytes 786436
  (7 other events, 13.0 us)
Sparse Core Ops, SparseCore 0:
  19.1 45.0 all-gather.2
  87.9 53.5 reduce-scatter.4
  182.4 42.7 all-gather.4
  250.2 62.7 reduce-scatter.6
where the time goes:
time: 332 us; the launch traced here: 330 us
  waiting for transfers between devices  169 us (51%)
  local copies, waits for them, and re-layouts  49.9 us (15%)
  blocking collectives  38.9 us (12%)
  matrix products  38.2 us (12%)
  other arithmetic  19.9 us (6%)
  between operations  14.4 us (4%)
    reduce_scatter x1, waiting for transfers between devices, body(): lax.psum_scatter(jnp.einsum('sikc,sjkc->jsic', left_proj, right_rows, pre...  52.9 us
    all_gather x1, waiting for transfers between devices, body(): right_rows = lax.all_gather(right_proj, 'row', axis=1, tiled=True)  44.7 us
    all_gather x1, waiting for transfers between devices, body(): product_cols = lax.all_gather(product_grad, 'col', axis=2, tiled=True)  42.8 us
    unnamed x5, waiting for transfers between devices  28.1 us
    dot_general x19, matrix products, project(): return jnp.dot(normed, weight, preferred_element_type=jnp.float32)  23.4 us
    unnamed x73, local copies, waits for them, and re-layouts  19.9 us
    psum x1, blocking collectives, sum_query(): return lax.psum(term_in, 'tmpl')  18.5 us
    all_gather x1, local copies, waits for them, and re-layouts, body(): right_rows = lax.all_gather(right_proj, 'row', axis=1, tiled=True)  13.4 us
  transfers between devices with their start and end apart: 4, of which 4 were waited for; matrix products, arithmetic and copies ran while one was open for 5% of the time, Pallas kernels for 0%

commit v1 on v0

v1 whole, which is shorter than its diff:
```python
import functools
import math

import jax
import jax.numpy as jnp
from jax import lax
from jax.experimental import pallas as pl
from jax.experimental.pallas import tpu as pltpu
from jax.sharding import PartitionSpec as P

EPS = 1e-05
F32 = jnp.float32
BF16 = jnp.bfloat16
HEADS = 4
HEAD_DIM = 16
SCALE = 1.0 / math.sqrt(HEAD_DIM)
GROUP = ("col", "row")


def iota(shape, axis):
    return lax.broadcasted_iota(jnp.int32, shape, axis)


def onehot(cond):
    return jnp.where(cond, 1.0, 0.0).astype(BF16)


def dot(a, b):
    return lax.dot_general(a, b, (((1,), (0,)), ((), ())), preferred_element_type=F32)


def dot_nt(a, b):
    return lax.dot_general(a, b, (((1,), (1,)), ((), ())), preferred_element_type=F32)


def dot_tn(a, b):
    return lax.dot_general(a, b, (((0,), (0,)), ((), ())), preferred_element_type=F32)


def eye64():
    return onehot(iota((64, 64), 0) == iota((64, 64), 1))


def c_to_rc(v):
    return jnp.concatenate(
        [
            jnp.concatenate([v[:, s * 512 + r * 128 : s * 512 + r * 128 + 128] for s in range(2)], axis=1)
            for r in range(4)
        ],
        axis=0,
    )


def rc_to_c(v):
    return jnp.concatenate(
        [v[r * 64 : r * 64 + 64, s * 128 : s * 128 + 128] for s in range(2) for r in range(4)], axis=1
    )


def both(v):
    return jnp.concatenate([v, v], axis=1)


def column(gain_row, repeat):
    pick = iota((64 * repeat, 64), 0) // repeat == iota((64 * repeat, 64), 1)
    return jnp.sum(jnp.where(pick, gain_row, 0.0), axis=1, keepdims=True)


def mean_c(v):
    return jnp.mean(v, axis=0, keepdims=True)


def mean_cr(v):
    part = jnp.sum(v.reshape(32, 8, 256), axis=0)
    return (part + pltpu.roll(part, 4, 0)) * (1.0 / 64.0)


def spread_cr(v):
    return jnp.broadcast_to(v[None], (32, 8, 256)).reshape(256, 256)


def hat_c(v):
    centered = v - mean_c(v)
    rstd = lax.rsqrt(mean_c(centered * centered) + EPS)
    return centered * rstd, rstd


def norm_grad_c(grad, gain, hat, rstd):
    scaled = grad * gain
    return rstd * (scaled - mean_c(scaled) - hat * mean_c(scaled * hat))


def hat_cr(v):
    centered = v - spread_cr(mean_cr(v))
    rstd = spread_cr(lax.rsqrt(mean_cr(centered * centered) + EPS))
    return centered * rstd, rstd


def norm_grad_cr(grad, gain, hat, rstd):
    scaled = grad * gain
    return rstd * (scaled - spread_cr(mean_cr(scaled)) - hat * spread_cr(mean_cr(scaled * hat)))


def wide_pair(wa, wb):
    row, lane = iota((64, 512), 0), iota((64, 512), 1)
    own = row == lane // 8
    base = dot(wa, onehot(own & (lane % 8 < 4))) + dot(wb, onehot(own & (lane % 8 >= 4)))
    return jnp.concatenate([jnp.where(lane % 4 == r, base, 0.0) for r in range(4)], axis=0).astype(BF16)


def wide_out(w):
    row, lane = iota((64, 256), 0), iota((64, 256), 1)
    base = dot_tn(w, onehot(row == lane // 4))
    return jnp.concatenate([jnp.where(lane % 4 == r, base, 0.0) for r in range(4)], axis=0).astype(BF16)


def wide_mask(mask):
    tiled = dot(mask.astype(F32).astype(BF16), onehot(iota((32, 256), 0) == iota((32, 256), 1) % 32))
    i, lane = iota((16, 256), 0), iota((16, 256), 1)
    tiled = jnp.where(i % 4 == (lane % 128) // 32, tiled, 0.0).astype(BF16)
    return dot(onehot(iota((8, 16), 0) % 4 == iota((8, 16), 1) // 4), tiled)


def spread8(v):
    return jnp.broadcast_to(v[None], (64, 8, 256)).reshape(512, 256)


def swap_groups(four):
    lane = iota(four[0].shape, 1) // 32
    for bit in (1, 2):
        low = (lane & bit) == 0
        out = []
        for a in range(4):
            if a & bit == 0:
                out.append(jnp.where(low, four[a], pltpu.roll(four[a ^ bit], 32 * bit, 1)))
            else:
                out.append(jnp.where(low, pltpu.roll(four[a ^ bit], 128 - 32 * bit, 1), four[a]))
        four = out
    return four


def swap_in(blocks):
    lo, hi = swap_groups(blocks[:4]), swap_groups(blocks[4:])
    return [jnp.concatenate([lo[q], hi[q]], axis=1) for q in range(4)]


def swap_out(rows):
    return swap_groups([v[:, :128] for v in rows]) + swap_groups([v[:, 128:] for v in rows])


def sides_first():
    a, b = iota((128, 128), 0), iota((128, 128), 1)
    return onehot((a // 64 == (b // 4) % 2) & ((a % 64) // 4 == b // 8) & (a % 4 == b % 4))


def natural_rows():
    a, b = iota((256, 256), 0), iota((256, 256), 1)
    return onehot((a % 4 == b // 64) & (a // 4 == b % 64))


def front_kernel(x_ref, mask_ref, gain_ref, pa_ref, ga_ref, pb_ref, gb_ref, out_ref, x_out, n_out):
    x = dot_nt(eye64(), x_ref[...].reshape(1024, 64))
    hat, _ = hat_c(x)
    normed = (hat * column(gain_ref[...], 1)).astype(BF16)
    x_out[...] = x.astype(BF16)
    n_out[...] = normed
    rc = c_to_rc(normed)
    gate = dot_tn(wide_pair(ga_ref[...], gb_ref[...]), rc)
    proj = dot_tn(wide_pair(pa_ref[...], pb_ref[...]), rc)
    mask = spread8(wide_mask(mask_ref[...]))
    both_sides = (mask * jax.nn.sigmoid(gate) * proj).astype(BF16)
    out_ref[:512, :] = both_sides[:, :128]
    out_ref[512:, :] = both_sides[:, 128:]


def side_kernel(n_ref, main_ref, cot_ref, go_ref, wq_ref, wo_ref, gat_out, q_out, g_out):
    gat_out[...] = jax.nn.sigmoid(dot_tn(go_ref[...], n_ref[...]))
    q_out[...] = dot_nt(wq_ref[...].T, main_ref[...].reshape(512, 128)).astype(BF16)
    g_out[...] = dot_nt(wo_ref[...], cot_ref[...].reshape(512, 128))


def product_kernel(x_ref, out_ref, a_out, b_out):
    blocks = [x_ref[c * 128 : c * 128 + 128, :].astype(F32) for c in range(8)]
    order = sides_first()
    parts = [dot(order, v.astype(BF16)).astype(BF16) for v in swap_in(blocks)]
    a = jnp.concatenate([v[:64] for v in parts], axis=0)
    b = jnp.concatenate([v[64:] for v in parts], axis=0)
    b = dot(natural_rows(), b).astype(BF16)
    a_out[...] = a
    b_out[...] = b
    prod = dot_nt(a, b)
    for c, v in enumerate(swap_out([prod[q * 64 : q * 64 + 64] for q in range(4)])):
        out_ref[c * 64 : c * 64 + 64, :] = v.astype(BF16)


def heads_sum(v):
    return jnp.sum(v.reshape(HEADS, HEAD_DIM, v.shape[-1]), axis=1)


def heads_spread(v):
    return jnp.broadcast_to(v[:, None, :], (HEADS, HEAD_DIM, v.shape[-1])).reshape(64, v.shape[-1])


def middle(x_ref, prod_ref, gat_ref, gm, gf, po_ref):
    prod = jnp.concatenate([prod_ref[:256, :], prod_ref[256:, :]], axis=1).astype(F32)
    hat_m, rstd_m = hat_cr(prod)
    wide = wide_out(po_ref[...])
    out = rc_to_c(dot(wide, (hat_m * gm).astype(BF16)))
    updated = x_ref[...].astype(F32) + gat_ref[...] * out
    hat_f, rstd_f = hat_c(updated)
    return hat_m, rstd_m, wide, out, hat_f, rstd_f


def score_kernel(
    x_ref, prod_ref, gat_ref, q_ref, g_ref, present_ref, gm_ref, gf_ref, po_ref, kw_ref, vw_ref,
    stat_out, w_out, along_out, key_out,
):
    gm, gf = column(gm_ref[...], 4), column(gf_ref[...], 1)
    _, _, _, _, hat_f, _ = middle(x_ref, prod_ref, gat_ref, gm, gf, po_ref)
    final = (hat_f * gf).astype(BF16)
    key = dot_tn(kw_ref[...], final).astype(BF16)
    val = dot_tn(vw_ref[...], final).astype(BF16)
    key_out[...] = key
    score = heads_sum(both(q_ref[...].astype(F32)) * key.astype(F32)) * SCALE
    along = heads_sum(both(g_ref[...]) * val.astype(F32))
    s0 = jnp.where(present_ref[0] > 0, score[:, :512], -1e30)
    s1 = jnp.where(present_ref[1] > 0, score[:, 512:], -1e30)
    top = jnp.maximum(s0, s1)
    e0, e1 = jnp.exp(s0 - top), jnp.exp(s1 - top)
    total = e0 + e1
    w0, w1 = e0 / total, e1 / total
    w_out[...] = jnp.concatenate([w0, w1], axis=1)
    along_out[...] = along
    stat_out[0] = top + jnp.log(total)
    stat_out[1] = w0 * along[:, :512] + w1 * along[:, 512:]


def grad_kernel(
    x_ref, prod_ref, gat_ref, q_ref, g_ref, key_ref, w_ref, along_ref, mine_ref, other_ref,
    gm_ref, gf_ref, po_ref, kw_ref, vw_ref,
    pg_out, qsum_out, du_out, dgate_out,
):
    gm, gf = column(gm_ref[...], 4), column(gf_ref[...], 1)
    hat_m, rstd_m, wide, out, hat_f, rstd_f = middle(x_ref, prod_ref, gat_ref, gm, gf, po_ref)
    share = jax.nn.sigmoid(mine_ref[0] - other_ref[0])
    average = share * mine_ref[1] + jax.nn.sigmoid(other_ref[0] - mine_ref[0]) * other_ref[1]
    weights = w_ref[...] * both(share)
    slope = weights * (along_ref[...] - both(average))
    slope_wide = heads_spread(slope)
    part = slope_wide * key_ref[...].astype(F32)
    qsum_out[...] = (part[:, :512] + part[:, 512:]) * SCALE
    key_grad = (slope_wide * both(q_ref[...].astype(F32)) * SCALE).astype(BF16)
    value_grad = (heads_spread(weights) * both(g_ref[...])).astype(BF16)
    d_final = dot(kw_ref[...], key_grad) + dot(vw_ref[...], value_grad)
    d_updated = norm_grad_c(d_final, gf, hat_f, rstd_f)
    gat = gat_ref[...]
    du_out[...] = d_updated
    d_out = (d_updated * gat).astype(BF16)
    dgate_out[...] = (d_updated * out * gat * (1.0 - gat)).astype(BF16)
    d_mixed = dot_tn(wide, c_to_rc(d_out))
    pg = norm_grad_cr(d_mixed, gm, hat_m, rstd_m).astype(BF16)
    pg_out[:256, :] = pg[:, :128]
    pg_out[256:, :] = pg[:, 128:]


def coef_kernel(
    n_ref, mask_ref, dgate_ref, go_ref, pa_ref, ga_ref, pb_ref, gb_ref,
    cg_out, cp_out, wg_out, wp_out, dn_out,
):
    wg = wide_pair(ga_ref[...], gb_ref[...])
    wp = wide_pair(pa_ref[...], pb_ref[...])
    rc = c_to_rc(n_ref[...])
    gate = jax.nn.sigmoid(dot_tn(wg, rc))
    proj = dot_tn(wp, rc)
    scaled = spread8(wide_mask(mask_ref[...])) * gate
    cp_out[...] = scaled
    cg_out[...] = scaled * (1.0 - gate) * proj
    wg_out[...] = wg
    wp_out[...] = wp
    dn_out[...] = dot(go_ref[...], dgate_ref[...])


def triangle_kernel(pg_ref, a_ref, b_ref, out_ref):
    blocks = [pg_ref[c * 64 : c * 64 + 64, :].astype(F32) for c in range(8)]
    pg = jnp.concatenate(swap_in(blocks), axis=0).astype(BF16)
    left = dot(pg, b_ref[...]).astype(BF16)
    right = dot_tn(dot(pg, natural_rows()).astype(BF16), a_ref[...]).astype(BF16)
    order = sides_first()
    rows = [
        dot_tn(order, jnp.concatenate([left[q * 64 : q * 64 + 64], right[q * 64 : q * 64 + 64]], axis=0))
        for q in range(4)
    ]
    for c, v in enumerate(swap_out(rows)):
        out_ref[c * 128 : c * 128 + 128, :] = v.astype(BF16)


def finish_kernel(lr_ref, cg_ref, cp_ref, wg_ref, wp_ref, dn_ref, x_ref, du_ref, gain_ref, out_ref):
    grad = jnp.concatenate([lr_ref[:512, :], lr_ref[512:, :]], axis=1).astype(F32)
    d_gate = (grad * cg_ref[...]).astype(BF16)
    d_proj = (grad * cp_ref[...]).astype(BF16)
    d_normed = rc_to_c(dot(wg_ref[...], d_gate) + dot(wp_ref[...], d_proj)) + dn_ref[...]
    hat, rstd = hat_c(x_ref[...].astype(F32))
    grad_x = norm_grad_c(d_normed, column(gain_ref[...], 1), hat, rstd) + du_ref[...]
    out_ref[...] = dot_tn(grad_x.astype(BF16), eye64()).astype(BF16).reshape(2, 16, 32, 64)


def main_kernel(mine_ref, other_ref, wq_ref, out_ref):
    grad = (mine_ref[...] + other_ref[...]).astype(BF16)
    out_ref[...] = dot_tn(grad, wq_ref[...].T).astype(BF16).reshape(16, 32, 128)


def call(kernel, outs, *args, smem=(), flops=0):
    specs = [
        pl.BlockSpec(memory_space=pltpu.SMEM if n in smem else pltpu.VMEM) for n in range(len(args))
    ]
    shapes = [jax.ShapeDtypeStruct(s, t) for s, t in outs]
    nbytes = sum(a.size * a.dtype.itemsize for a in args)
    return pl.pallas_call(
        kernel,
        out_shape=shapes,
        in_specs=specs,
        out_specs=[pl.BlockSpec(memory_space=pltpu.VMEM)] * len(shapes),
        compiler_params=pltpu.CompilerParams(vmem_limit_bytes=24 * 1024 * 1024),
        cost_estimate=pl.CostEstimate(flops=flops, bytes_accessed=nbytes, transcendentals=0),
    )(*args)


def exchange(v):
    return lax.ppermute(v, "tmpl", [(0, 1), (1, 0)])


def spread_chunks(v, rows):
    return lax.all_to_all(v.reshape(128, rows, 128), GROUP, 0, 0, tiled=True).reshape(128 * rows, 128)


def body(
    template_pair, template_mask, pair_mask, main_pair, update_cotangent,
    gain_in, proj_a, gate_a, proj_b, gate_b, gain_mid, proj_out, gate_out, gain_final,
    key_weight, value_weight, query_weight, output_weight,
):
    gi, gm, gf = gain_in.reshape(1, 64), gain_mid.reshape(1, 64), gain_final.reshape(1, 64)
    sides, x, normed = call(
        front_kernel,
        [((1024, 128), BF16), ((64, 1024), BF16), ((64, 1024), BF16)],
        template_pair, pair_mask, gi, proj_a, gate_a, proj_b, gate_b,
    )
    gat, query, grad_out = call(
        side_kernel,
        [((64, 1024), F32), ((64, 512), BF16), ((64, 512), F32)],
        normed, main_pair, update_cotangent, gate_out, query_weight, output_weight,
    )
    sides = spread_chunks(sides, 8)
    prod, a, b = call(
        product_kernel, [((512, 128), BF16), ((256, 256), BF16), ((256, 256), BF16)], sides
    )
    prod = spread_chunks(prod, 4)
    stat, weights, along, key = call(
        score_kernel,
        [((2, 4, 512), F32), ((4, 1024), F32), ((4, 1024), F32), ((64, 1024), BF16)],
        x, prod, gat, query, grad_out, template_mask, gm, gf, proj_out, key_weight, value_weight,
        smem=(5,),
    )
    other = exchange(stat)
    pg, query_sum, d_updated, d_gate = call(
        grad_kernel,
        [((512, 128), BF16), ((64, 512), F32), ((64, 1024), F32), ((64, 1024), BF16)],
        x, prod, gat, query, grad_out, key, weights, along, stat, other,
        gm, gf, proj_out, key_weight, value_weight,
    )
    cg, cp, wg, wp, dn = call(
        coef_kernel,
        [
            ((512, 256), F32), ((512, 256), F32), ((256, 512), BF16), ((256, 512), BF16),
            ((64, 1024), F32),
        ],
        normed, pair_mask, d_gate, gate_out, proj_a, gate_a, proj_b, gate_b,
    )
    pg = spread_chunks(pg, 4)
    (grads,) = call(triangle_kernel, [((1024, 128), BF16)], pg, a, b)
    query_other = exchange(query_sum)
    (main_grad,) = call(main_kernel, [((16, 32, 128), BF16)], query_sum, query_other, query_weight)
    grads = spread_chunks(grads, 8)
    (pair_grad,) = call(
        finish_kernel, [((2, 16, 32, 64), BF16)], grads, cg, cp, wg, wp, dn, x, d_updated, gi
    )
    return (pair_grad, main_grad)


def solution(mesh):
    pixel = P("row", "col", None)
    placed = (
        P("tmpl", "row", "col", None), P("tmpl"), P("row", "col"), pixel, pixel,
    ) + (P(),) * 13
    return jax.shard_map(
        body,
        mesh=mesh,
        in_specs=placed,
        out_specs=(P("tmpl", "row", "col", None), pixel),
        check_vma=False,
    )
```

time: 332 us -> 103 us (0.31)
  the two profiles are of different devices: /device:TPU:6 before, /device:TPU:1 now
where the time goes in v1:
time: 103 us; the launch traced here: 102 us
  blocking collectives  46.1 us (45%)
  waiting for transfers between devices  21.7 us (21%)
  starting transfers between devices  17.1 us (17%)
  Pallas kernels  9.32 us (9%)
  local copies, waits for them, and re-layouts  6.56 us (6%)
    all_to_all x2, blocking collectives, spread_chunks(): lax.all_to_all(v.reshape(128, rows, 128), GROUP, 0, 0, tiled=True)  46.1 us
    all_to_all x2, waiting for transfers between devices, spread_chunks(): lax.all_to_all(v.reshape(128, rows, 128), GROUP, 0, 0, tiled=True)  16.5 us
    all_to_all x2, starting transfers between devices, spread_chunks(): lax.all_to_all(v.reshape(128, rows, 128), GROUP, 0, 0, tiled=True)  12 us
    pallas_call x9, Pallas kernels, call(): pl.pallas_call(kernel, out_shape=shapes, in_specs=specs, out_specs=[pl.Bl...  9.32 us
    unnamed x47, local copies, waits for them, and re-layouts  6.56 us
    ppermute x2, waiting for transfers between devices, exchange(): return lax.ppermute(v, 'tmpl', [(0, 1), (1, 0)])  5.25 us
    ppermute x2, starting transfers between devices, exchange(): return lax.ppermute(v, 'tmpl', [(0, 1), (1, 0)])  5.06 us
  transfers between devices with their start and end apart: 4, of which 4 were waited for; matrix products, arithmetic and copies ran while one was open for 0% of the time, Pallas kernels for 2%

profile of v1, /device:TPU:1, one launch (start us, length us, event | category | flops | bytes accessed | tf_op | source)
XLA Modules:
  0.0 101.6 jit_solution(7572219348362065447)
XLA Ops:
  0.6 0.6 copy-done.18
  1.3 0.9 copy-done
  2.2 0.7 copy-done.7
  3.0 0.7 copy-done.9
  3.7 0.7 copy-done.11
  4.4 0.7 copy-done.13
  5.1 0.7 copy-done.15
  5.8 0.8 shard_map.185
  6.6 28.2 %all_to_all.20 = bf16[128,8,128]{2,1,0:T(8,128)(2,1)S(1)} all-to-all(bf16[128,8,128]{2,1,0:T(8,128)(2,1)S(1)} %bitcast.16), channel_id=1, replica_groups=mesh['tmpl'=2,'row'=16,'col'=8] {'col','row'}, dimensions={0} | all-to-all | bytes 524288 | tf_op jit(solution)/shard_map/all_to_all | solution.py:333
  34.8 1.6 %shard_map.186 = (bf16[512,128]{1,0:T(8,128)(2,1)}, bf16[256,256]{1,0:T(8,128)(2,1)S(1)}, bf16[256,256]{1,0:T(8,128)(2,1)S(1)}) custom-call(bf16[1024,128]{1,0:T(8,128)(2,1)S(1)} %bitcast.14), custom_call_target="tpu_custom_call" | custom-call | bytes 262144 | tf_op jit(solution)/shard_map/pallas_call | solution.py:318
  36.4 6.3 %all-to-all-start.1 = ((bf16[128,4,128]{2,1,0:T(4,128)(2,1)}), bf16[128,4,128]{2,1,0:T(4,128)(2,1)S(1)}, u32[]{:S(2)}, u32[]{:S(2)}) async-start(bf16[128,4,128]{2,1,0:T(4,128)(2,1)} %bitcast.3), calls=%async_computation.1 | async-start | bytes 262144 | tf_op jit(solution)/shard_map/all_to_all | solution.py:333
  42.7 0.1 copy.20.wq_ref
  42.9 0.6 copy-done.6
  43.4 0.0 copy-done.17
  43.5 0.3 shard_map.187
  43.7 10.7 %all-to-all-done.1 = bf16[128,4,128]{2,1,0:T(4,128)(2,1)S(1)} async-done(((bf16[128,4,128]{2,1,0:T(4,128)(2,1)}), bf16[128,4,128]{2,1,0:T(4,128)(2,1)S(1)}, u32[]{:S(2)}, u32[]{:S(2)}) %all-to-all-start.1) | async-done | bytes 131104 | tf_op jit(solution)/shard_map/all_to_all | solution.py:333
  54.4 0.6 copy-done.19
  55.1 0.0 copy-done.20
  55.1 0.0 copy-done.21
  55.1 1.2 %shard_map.188 = (f32[2,4,512]{2,1,0:T(4,128)S(1)}, f32[4,1024]{1,0:T(4,128)S(1)}, f32[4,1024]{1,0:T(4,128)S(1)}, bf16[64,1024]{1,0:T(8,128)(2,1)S(1)}) custom-call(bf16[64,1024]{1,0:T(8,128)(2,1)S(1)} %get-tuple-element.24.x_ref, bf16[512,128]{1,0:T(8,128)(2,1)S(1)} %bitcast.11, f32[64,1024]{1,0:T(8,128)S(1)} %get-tuple-element.28.gat_ref, ...), custom_call_target="tpu_custom_call" | custom-call | bytes 745992 | tf_op jit(solution)/shard_map/pallas_call | solution.py:318
  56.3 2.5 %collective-permute-start = (f32[2,4,512]{2,1,0:T(4,128)S(1)}, f32[2,4,512]{2,1,0:T(4,128)S(1)}, u32[]{:S(2)}, u32[]{:S(2)}) collective-permute-start(f32[2,4,512]{2,1,0:T(4,128)S(1)} %get-tuple-element.34.mine_ref), channel_id=1, source_target_pairs={{0,128},{128,0},{1,129},{129,1},{2,130},{130,2},{3,131},{131,3},{4... | collective-permute-start | bytes 49160 | tf_op jit(solution)/shard_map/ppermute | solution.py:329
  58.9 1.6 %collective-permute-done.other_ref = f32[2,4,512]{2,1,0:T(4,128)S(1)} collective-permute-done((f32[2,4,512]{2,1,0:T(4,128)S(1)}, f32[2,4,512]{2,1,0:T(4,128)S(1)}, u32[]{:S(2)}, u32[]{:S(2)}) %collective-permute-start) | collective-permute-done | bytes 16416 | tf_op jit(solution)/shard_map/ppermute | solution.py:329
  60.5 0.8 shard_map.189
  61.3 17.9 %all_to_all.21 = bf16[128,4,128]{2,1,0:T(4,128)(2,1)S(1)} all-to-all(bf16[128,4,128]{2,1,0:T(4,128)(2,1)S(1)} %bitcast.17), channel_id=1, replica_groups=mesh['tmpl'=2,'row'=16,'col'=8] {'col','row'}, dimensions={0} | all-to-all | bytes 262144 | tf_op jit(solution)/shard_map/all_to_all | solution.py:333
  79.3 1.6 %shard_map.190 = bf16[1024,128]{1,0:T(8,128)(2,1)} custom-call(bf16[512,128]{1,0:T(8,128)(2,1)S(1)} %bitcast.15, bf16[256,256]{1,0:T(8,128)(2,1)S(1)} %get-tuple-element.36.a_ref, bf16[256,256]{1,0:T(8,128)(2,1)S(1)} %get-tuple-element.37.b_ref), custom_call_target="tpu_custom_call" | custom-call | bytes 393216 | tf_op jit(solution)/shard_map/pallas_call | solution.py:318
  80.9 5.7 %all-to-all-start.3 = ((bf16[128,8,128]{2,1,0:T(8,128)(2,1)}), bf16[128,8,128]{2,1,0:T(8,128)(2,1)S(1)}, u32[]{:S(2)}, u32[]{:S(2)}) async-start(bf16[128,8,128]{2,1,0:T(8,128)(2,1)} %bitcast.9), calls=%async_computation.3 | async-start | bytes 524288 | tf_op jit(solution)/shard_map/all_to_all | solution.py:333
  86.6 2.5 %collective-permute-start.1 = (f32[64,512]{1,0:T(8,128)S(1)}, f32[64,512]{1,0:T(8,128)S(1)}, u32[]{:S(2)}, u32[]{:S(2)}) collective-permute-start(f32[64,512]{1,0:T(8,128)S(1)} %get-tuple-element.45.mine_ref), channel_id=1, source_target_pairs={{0,128},{128,0},{1,129},{129,1},{2,130},{130,2},{3,131},{131,3},{4... | collective-permute-start | bytes 393224 | tf_op jit(solution)/shard_map/ppermute | solution.py:329
  89.2 0.8 shard_map.191
  90.0 3.6 %collective-permute-done.1.other_ref = f32[64,512]{1,0:T(8,128)S(1)} collective-permute-done((f32[64,512]{1,0:T(8,128)S(1)}, f32[64,512]{1,0:T(8,128)S(1)}, u32[]{:S(2)}, u32[]{:S(2)}) %collective-permute-start.1) | collective-permute-done | bytes 131104 | tf_op jit(solution)/shard_map/ppermute | solution.py:329
  93.6 0.9 shard_map.193
  94.4 5.8 %all-to-all-done.3 = bf16[128,8,128]{2,1,0:T(8,128)(2,1)S(1)} async-done(((bf16[128,8,128]{2,1,0:T(8,128)(2,1)}), bf16[128,8,128]{2,1,0:T(8,128)(2,1)S(1)}, u32[]{:S(2)}, u32[]{:S(2)}) %all-to-all-start.3) | async-done | bytes 262176 | tf_op jit(solution)/shard_map/all_to_all | solution.py:333
  100.2 1.4 %shard_map.192 = bf16[2,16,32,64]{3,2,1,0:T(8,128)(2,1)} custom-call(bf16[1024,128]{1,0:T(8,128)(2,1)S(1)} %bitcast.13, f32[512,256]{1,0:T(8,128)S(1)} %get-tuple-element.39.cg_ref, f32[512,256]{1,0:T(8,128)S(1)} %get-tuple-element.40.cp_ref, bf16[256,512]{1,0:T(8,128)(2,1)S(1)} %get-tuple-element.41.wg_ref, bf16[256,512]{1,0:T(8,128)(2,1)S(1)} %get-tuple-element.42.wp_ref, ...), custom_call_target="tpu_custom_call" | custom-call | bytes 2490624 | tf_op jit(solution)/shard_map/pallas_call | solution.py:318
  (34 shorter events, 0.1 us)
Async XLA Ops:
  0.6 0.7 copy-start.18
  1.3 0.9 copy-start
  2.2 0.7 copy-start.7
  3.0 0.7 copy-start.9
  3.7 0.7 copy-start.11
  4.4 0.7 copy-start.13
  5.1 0.7 copy-start.15
  34.8 7.9 %copy-start.22 = (bf16[128,64]{0,1:T(8,128)(2,1)S(1)}, bf16[128,64]{0,1:T(8,128)(2,1)}, u32[]{:S(2)}) copy-start(bf16[128,64]{0,1:T(8,128)(2,1)} %param.34) | copy-start | bytes 49156
  36.4 6.5 %copy-start.1 = (bf16[16,32,128]{2,1,0:T(8,128)(2,1)S(1)}, bf16[16,32,128]{2,1,0:T(8,128)(2,1)}, u32[]{:S(2)}) copy-start(bf16[16,32,128]{2,1,0:T(8,128)(2,1)} %main_ref.1) | copy-start | bytes 393220
  36.4 6.5 %copy-start.2 = (bf16[16,32,128]{2,1,0:T(8,128)(2,1)S(1)}, bf16[16,32,128]{2,1,0:T(8,128)(2,1)}, u32[]{:S(2)}) copy-start(bf16[16,32,128]{2,1,0:T(8,128)(2,1)} %cot_ref.1) | copy-start | bytes 393220
  36.4 18.0 %all-to-all-start.1 = ((bf16[128,4,128]{2,1,0:T(4,128)(2,1)}), bf16[128,4,128]{2,1,0:T(4,128)(2,1)S(1)}, u32[]{:S(2)}, u32[]{:S(2)}) async-start(bf16[128,4,128]{2,1,0:T(4,128)(2,1)} %bitcast.3), calls=%async_computation.1 | async-start | bytes 262144 | tf_op jit(solution)/shard_map/all_to_all | solution.py:333
  42.7 0.7 copy-start.6
  42.7 0.7 copy-start.17
  43.5 11.0 %copy-start.3 = (bf16[64,64]{1,0:T(8,128)(2,1)S(1)}, bf16[64,64]{1,0:T(8,128)(2,1)}, u32[]{:S(2)}) copy-start(bf16[64,64]{1,0:T(8,128)(2,1)} %po_ref.3) | copy-start | bytes 24580
  43.5 11.0 %copy-start.4 = (bf16[64,64]{1,0:T(8,128)(2,1)S(1)}, bf16[64,64]{1,0:T(8,128)(2,1)}, u32[]{:S(2)}) copy-start(bf16[64,64]{1,0:T(8,128)(2,1)} %kw_ref.3) | copy-start | bytes 24580
  43.5 11.0 %copy-start.5 = (bf16[64,64]{1,0:T(8,128)(2,1)S(1)}, bf16[64,64]{1,0:T(8,128)(2,1)}, u32[]{:S(2)}) copy-start(bf16[64,64]{1,0:T(8,128)(2,1)} %vw_ref.3) | copy-start | bytes 24580
  54.4 0.7 copy-start.19
  54.4 0.7 copy-start.20
  54.4 0.7 copy-start.21
  56.3 4.2 %collective-permute-start = (f32[2,4,512]{2,1,0:T(4,128)S(1)}, f32[2,4,512]{2,1,0:T(4,128)S(1)}, u32[]{:S(2)}, u32[]{:S(2)}) collective-permute-start(f32[2,4,512]{2,1,0:T(4,128)S(1)} %get-tuple-element.34.mine_ref), channel_id=1, source_target_pairs={{0,128},{128,0},{1,129},{129,1},{2,130},{130,2},{3,131},{131,3},{4... | collective-permute-start | bytes 49160 | tf_op jit(solution)/shard_map/ppermute | solution.py:329
  80.9 8.3 %copy-start.8 = (bf16[64,64]{1,0:T(8,128)(2,1)S(1)}, bf16[64,64]{1,0:T(8,128)(2,1)}, u32[]{:S(2)}) copy-start(bf16[64,64]{1,0:T(8,128)(2,1)} %pa_ref.3) | copy-start | bytes 24580
  80.9 8.3 %copy-start.10 = (bf16[64,64]{1,0:T(8,128)(2,1)S(1)}, bf16[64,64]{1,0:T(8,128)(2,1)}, u32[]{:S(2)}) copy-start(bf16[64,64]{1,0:T(8,128)(2,1)} %ga_ref.3) | copy-start | bytes 24580
  80.9 8.3 %copy-start.12 = (bf16[64,64]{1,0:T(8,128)(2,1)S(1)}, bf16[64,64]{1,0:T(8,128)(2,1)}, u32[]{:S(2)}) copy-start(bf16[64,64]{1,0:T(8,128)(2,1)} %pb_ref.3) | copy-start | bytes 24580
  80.9 8.3 %copy-start.14 = (bf16[64,64]{1,0:T(8,128)(2,1)S(1)}, bf16[64,64]{1,0:T(8,128)(2,1)}, u32[]{:S(2)}) copy-start(bf16[64,64]{1,0:T(8,128)(2,1)} %gb_ref.3) | copy-start | bytes 24580
  80.9 8.3 %copy-start.16 = (s32[16,32]{1,0:T(8,128)S(1)}, s32[16,32]{1,0:T(8,128)}, u32[]{:S(2)}) copy-start(s32[16,32]{1,0:T(8,128)} %mask_ref.3) | copy-start | bytes 6148
  80.9 19.3 %all-to-all-start.3 = ((bf16[128,8,128]{2,1,0:T(8,128)(2,1)}), bf16[128,8,128]{2,1,0:T(8,128)(2,1)S(1)}, u32[]{:S(2)}, u32[]{:S(2)}) async-start(bf16[128,8,128]{2,1,0:T(8,128)(2,1)} %bitcast.9), calls=%async_computation.3 | async-start | bytes 524288 | tf_op jit(solution)/shard_map/all_to_all | solution.py:333
  86.6 6.9 %collective-permute-start.1 = (f32[64,512]{1,0:T(8,128)S(1)}, f32[64,512]{1,0:T(8,128)S(1)}, u32[]{:S(2)}, u32[]{:S(2)}) collective-permute-start(f32[64,512]{1,0:T(8,128)S(1)} %get-tuple-element.45.mine_ref), channel_id=1, source_target_pairs={{0,128},{128,0},{1,129},{129,1},{2,130},{130,2},{3,131},{131,3},{4... | collective-permute-start | bytes 393224 | tf_op jit(solution)/shard_map/ppermute | solution.py:329

commit v2 on v1

--- a/solution.py
+++ b/solution.py
@@ -14,7 +14,9 @@
 HEADS = 4
 HEAD_DIM = 16
 SCALE = 1.0 / math.sqrt(HEAD_DIM)
-GROUP = ("col", "row")
+GROUP = ("row", "col")
+TURN = 12
+ORDER = [p ^ (8 * TURN) for p in range(128)]
 
 
 def iota(shape, axis):
@@ -148,6 +150,12 @@
     return swap_groups([v[:, :128] for v in rows]) + swap_groups([v[:, 128:] for v in rows])
 
 
+def pair_up(even, odd):
+    even, odd = even.reshape(8, 8, 128), odd.reshape(8, 8, 128)
+    top = iota(even.shape, 1) < 4
+    return jnp.where(top, even, pltpu.roll(odd, 4, 1)), jnp.where(top, pltpu.roll(even, 4, 1), odd)
+
+
 def sides_first():
     a, b = iota((128, 128), 0), iota((128, 128), 1)
     return onehot((a // 64 == (b // 4) % 2) & ((a % 64) // 4 == b // 8) & (a % 4 == b % 4))
@@ -155,13 +163,31 @@
 
 def natural_rows():
     a, b = iota((256, 256), 0), iota((256, 256), 1)
-    return onehot((a % 4 == b // 64) & (a // 4 == b % 64))
-
-
-def front_kernel(x_ref, mask_ref, gain_ref, pa_ref, ga_ref, pb_ref, gb_ref, out_ref, x_out, n_out):
+    return onehot((a % 4 == b // 64) & ((a // 4) ^ (4 * TURN) == b % 64))
+
+
+def front_kernel(
+    x_hbm, mask_hbm, gi_hbm, pa_hbm, ga_hbm, pb_hbm, gb_hbm, go_hbm, main_hbm, cot_hbm, wq_hbm, wo_hbm,
+    po_hbm, kw_hbm, vw_hbm, gm_hbm, gf_hbm, present_hbm,
+    out_ref, x_out, n_out, gat_out, q_out, g_out, wide_out_ref, kv_out, gm_out, gf_out, gi_out, absent_out,
+    x_ref, mask_ref, gi_ref, pa_ref, ga_ref, pb_ref, gb_ref, go_ref, main_ref, cot_ref, wq_ref, wo_ref,
+    po_ref, kw_ref, vw_ref, gm_ref, gf_ref, present_ref, sems,
+):
+    pairs = [
+        (x_hbm, x_ref), (gi_hbm, gi_ref), (pa_hbm, pa_ref), (ga_hbm, ga_ref), (pb_hbm, pb_ref),
+        (gb_hbm, gb_ref), (mask_hbm, mask_ref), (go_hbm, go_ref), (main_hbm, main_ref), (cot_hbm, cot_ref),
+        (wq_hbm, wq_ref), (wo_hbm, wo_ref), (po_hbm, po_ref), (kw_hbm, kw_ref), (vw_hbm, vw_ref),
+        (gm_hbm, gm_ref), (gf_hbm, gf_ref), (present_hbm, present_ref),
+    ]
+    copies = [pltpu.make_async_copy(a, b, sems.at[n]) for n, (a, b) in enumerate(pairs)]
+    for copy in copies:
+        copy.start()
+    for copy in copies[:7]:
+        copy.wait()
     x = dot_nt(eye64(), x_ref[...].reshape(1024, 64))
     hat, _ = hat_c(x)
-    normed = (hat * column(gain_ref[...], 1)).astype(BF16)
+    gi = column(gi_ref[...], 1)
+    normed = (hat * gi).astype(BF16)
     x_out[...] = x.astype(BF16)
     n_out[...] = normed
     rc = c_to_rc(normed)
@@ -171,16 +197,25 @@
     both_sides = (mask * jax.nn.sigmoid(gate) * proj).astype(BF16)
     out_ref[:512, :] = both_sides[:, :128]
     out_ref[512:, :] = both_sides[:, 128:]
-
-
-def side_kernel(n_ref, main_ref, cot_ref, go_ref, wq_ref, wo_ref, gat_out, q_out, g_out):
-    gat_out[...] = jax.nn.sigmoid(dot_tn(go_ref[...], n_ref[...]))
-    q_out[...] = dot_nt(wq_ref[...].T, main_ref[...].reshape(512, 128)).astype(BF16)
+    gi_out[...] = jnp.broadcast_to(gi, (64, 128))
+    for copy in copies[7:]:
+        copy.wait()
+    gat_out[...] = jax.nn.sigmoid(dot_tn(go_ref[...], normed))
+    q_out[...] = dot_nt(wq_ref[...], main_ref[...].reshape(512, 128)).astype(BF16)
     g_out[...] = dot_nt(wo_ref[...], cot_ref[...].reshape(512, 128))
+    wide_out_ref[...] = wide_out(po_ref[...])
+    kv_out[...] = jnp.concatenate([kw_ref[...], vw_ref[...]], axis=1)
+    gm_out[...] = jnp.broadcast_to(column(gm_ref[...], 4), (256, 128))
+    gf_out[...] = jnp.broadcast_to(column(gf_ref[...], 1), (64, 128))
+    absent_out[...] = jnp.where(
+        jnp.concatenate([jnp.broadcast_to(present_ref[:, s : s + 1], (8, 512)) for s in range(2)], axis=1) > 0,
+        0.0, -1e30,
+    )
 
 
 def product_kernel(x_ref, out_ref, a_out, b_out):
-    blocks = [x_ref[c * 128 : c * 128 + 128, :].astype(F32) for c in range(8)]
+    tiles = x_ref[...].astype(F32).reshape(16, 8, 8, 128)
+    blocks = [tiles[:, c].reshape(128, 128) for c in range(8)]
     order = sides_first()
     parts = [dot(order, v.astype(BF16)).astype(BF16) for v in swap_in(blocks)]
     a = jnp.concatenate([v[:64] for v in parts], axis=0)
@@ -189,8 +224,9 @@
     a_out[...] = a
     b_out[...] = b
     prod = dot_nt(a, b)
-    for c, v in enumerate(swap_out([prod[q * 64 : q * 64 + 64] for q in range(4)])):
-        out_ref[c * 64 : c * 64 + 64, :] = v.astype(BF16)
+    cols = swap_out([prod[q * 64 : q * 64 + 64] for q in range(4)])
+    pairs = [jnp.stack(pair_up(cols[c], cols[c + 1]), axis=1) for c in range(0, 8, 2)]
+    out_ref[...] = jnp.stack(pairs, axis=2).reshape(512, 128).astype(BF16)
 
 
 def heads_sum(v):
@@ -201,30 +237,33 @@
     return jnp.broadcast_to(v[:, None, :], (HEADS, HEAD_DIM, v.shape[-1])).reshape(64, v.shape[-1])
 
 
-def middle(x_ref, prod_ref, gat_ref, gm, gf, po_ref):
+def tile_lanes(v, n):
+    return jnp.concatenate([v] * n, axis=1)
+
+
+def score_kernel(
+    x_ref, prod_ref, gat_ref, q_ref, g_ref, absent_ref, gm_ref, gf_ref, wide_ref, kv_ref,
+    stat_out, w_out, along_out, key_out, hat_m_out, rstd_m_out, out_out, hat_f_out, rstd_f_out,
+):
     prod = jnp.concatenate([prod_ref[:256, :], prod_ref[256:, :]], axis=1).astype(F32)
-    hat_m, rstd_m = hat_cr(prod)
-    wide = wide_out(po_ref[...])
-    out = rc_to_c(dot(wide, (hat_m * gm).astype(BF16)))
-    updated = x_ref[...].astype(F32) + gat_ref[...] * out
-    hat_f, rstd_f = hat_c(updated)
-    return hat_m, rstd_m, wide, out, hat_f, rstd_f
-
-
-def score_kernel(
-    x_ref, prod_ref, gat_ref, q_ref, g_ref, present_ref, gm_ref, gf_ref, po_ref, kw_ref, vw_ref,
-    stat_out, w_out, along_out, key_out,
-):
-    gm, gf = column(gm_ref[...], 4), column(gf_ref[...], 1)
-    _, _, _, _, hat_f, _ = middle(x_ref, prod_ref, gat_ref, gm, gf, po_ref)
-    final = (hat_f * gf).astype(BF16)
-    key = dot_tn(kw_ref[...], final).astype(BF16)
-    val = dot_tn(vw_ref[...], final).astype(BF16)
+    centered = prod - spread_cr(mean_cr(prod))
+    rstd_m = lax.rsqrt(mean_cr(centered * centered) + EPS)
+    hat_m = centered * spread_cr(rstd_m)
+    out = rc_to_c(dot(wide_ref[...], (hat_m * tile_lanes(gm_ref[...], 2)).astype(BF16)))
+    hat_f, rstd_f = hat_c(x_ref[...].astype(F32) + gat_ref[...] * out)
+    hat_m_out[...] = hat_m
+    rstd_m_out[...] = rstd_m
+    out_out[...] = out
+    hat_f_out[...] = hat_f
+    rstd_f_out[...] = rstd_f
+    final = (hat_f * tile_lanes(gf_ref[...], 8)).astype(BF16)
+    key_val = dot_tn(kv_ref[...], final).astype(BF16)
+    key, val = key_val[:64], key_val[64:]
     key_out[...] = key
     score = heads_sum(both(q_ref[...].astype(F32)) * key.astype(F32)) * SCALE
     along = heads_sum(both(g_ref[...]) * val.astype(F32))
-    s0 = jnp.where(present_ref[0] > 0, score[:, :512], -1e30)
-    s1 = jnp.where(present_ref[1] > 0, score[:, 512:], -1e30)
+    score = jnp.where(absent_ref[:4, :] < 0.0, -1e30, score)
+    s0, s1 = score[:, :512], score[:, 512:]
     top = jnp.maximum(s0, s1)
     e0, e1 = jnp.exp(s0 - top), jnp.exp(s1 - top)
     total = e0 + e1
@@ -236,12 +275,10 @@
 
 
 def grad_kernel(
-    x_ref, prod_ref, gat_ref, q_ref, g_ref, key_ref, w_ref, along_ref, mine_ref, other_ref,
-    gm_ref, gf_ref, po_ref, kw_ref, vw_ref,
+    gat_ref, q_ref, g_ref, key_ref, w_ref, along_ref, mine_ref, other_ref,
+    gm_ref, gf_ref, wide_ref, kv_ref, hat_m_ref, rstd_m_ref, out_ref, hat_f_ref, rstd_f_ref,
     pg_out, qsum_out, du_out, dgate_out,
 ):
-    gm, gf = column(gm_ref[...], 4), column(gf_ref[...], 1)
-    hat_m, rstd_m, wide, out, hat_f, rstd_f = middle(x_ref, prod_ref, gat_ref, gm, gf, po_ref)
     share = jax.nn.sigmoid(mine_ref[0] - other_ref[0])
     average = share * mine_ref[1] + jax.nn.sigmoid(other_ref[0] - mine_ref[0]) * other_ref[1]
     weights = w_ref[...] * both(share)
@@ -249,16 +286,18 @@
     slope_wide = heads_spread(slope)
     part = slope_wide * key_ref[...].astype(F32)
     qsum_out[...] = (part[:, :512] + part[:, 512:]) * SCALE
-    key_grad = (slope_wide * both(q_ref[...].astype(F32)) * SCALE).astype(BF16)
+    key_grad = (slope_wide * both(q_ref[...].astype(F32) * SCALE)).astype(BF16)
     value_grad = (heads_spread(weights) * both(g_ref[...])).astype(BF16)
-    d_final = dot(kw_ref[...], key_grad) + dot(vw_ref[...], value_grad)
-    d_updated = norm_grad_c(d_final, gf, hat_f, rstd_f)
+    d_final = dot(kv_ref[...], jnp.concatenate([key_grad, value_grad], axis=0))
+    d_updated = norm_grad_c(d_final, tile_lanes(gf_ref[...], 8), hat_f_ref[...], rstd_f_ref[...])
     gat = gat_ref[...]
     du_out[...] = d_updated
-    d_out = (d_updated * gat).astype(BF16)
-    dgate_out[...] = (d_updated * out * gat * (1.0 - gat)).astype(BF16)
-    d_mixed = dot_tn(wide, c_to_rc(d_out))
-    pg = norm_grad_cr(d_mixed, gm, hat_m, rstd_m).astype(BF16)
+    d_out = d_updated * gat
+    dgate_out[...] = (d_out * out_ref[...] * (1.0 - gat)).astype(BF16)
+    d_mixed = dot_tn(wide_ref[...], c_to_rc(d_out.astype(BF16)))
+    pg = norm_grad_cr(
+        d_mixed, tile_lanes(gm_ref[...], 2), hat_m_ref[...], spread_cr(rstd_m_ref[...])
+    ).astype(BF16)
     pg_out[:256, :] = pg[:, :128]
     pg_out[256:, :] = pg[:, 128:]
 
@@ -281,7 +320,12 @@
 
 
 def triangle_kernel(pg_ref, a_ref, b_ref, out_ref):
-    blocks = [pg_ref[c * 64 : c * 64 + 64, :].astype(F32) for c in range(8)]
+    tiles = pg_ref[...].astype(F32).reshape(8, 2, 4, 8, 128)
+    blocks = [
+        v.reshape(64, 128)
+        for m in range(4)
+        for v in pair_up(tiles[:, 0, m].reshape(64, 128), tiles[:, 1, m].reshape(64, 128))
+    ]
     pg = jnp.concatenate(swap_in(blocks), axis=0).astype(BF16)
     left = dot(pg, b_ref[...]).astype(BF16)
     right = dot_tn(dot(pg, natural_rows()).astype(BF16), a_ref[...]).astype(BF16)
@@ -290,8 +334,8 @@
         dot_tn(order, jnp.concatenate([left[q * 64 : q * 64 + 64], right[q * 64 : q * 64 + 64]], axis=0))
         for q in range(4)
     ]
-    for c, v in enumerate(swap_out(rows)):
-        out_ref[c * 128 : c * 128 + 128, :] = v.astype(BF16)
+    cols = [v.reshape(16, 8, 128) for v in swap_out(rows)]
+    out_ref[...] = jnp.stack(cols, axis=1).reshape(1024, 128).astype(BF16)
 
 
 def finish_kernel(lr_ref, cg_ref, cp_ref, wg_ref, wp_ref, dn_ref, x_ref, du_ref, gain_ref, out_ref):
@@ -300,37 +344,48 @@
     d_proj = (grad * cp_ref[...]).astype(BF16)
     d_normed = rc_to_c(dot(wg_ref[...], d_gate) + dot(wp_ref[...], d_proj)) + dn_ref[...]
     hat, rstd = hat_c(x_ref[...].astype(F32))
-    grad_x = norm_grad_c(d_normed, column(gain_ref[...], 1), hat, rstd) + du_ref[...]
+    grad_x = norm_grad_c(d_normed, tile_lanes(gain_ref[...], 8), hat, rstd) + du_ref[...]
     out_ref[...] = dot_tn(grad_x.astype(BF16), eye64()).astype(BF16).reshape(2, 16, 32, 64)
 
 
 def main_kernel(mine_ref, other_ref, wq_ref, out_ref):
     grad = (mine_ref[...] + other_ref[...]).astype(BF16)
-    out_ref[...] = dot_tn(grad, wq_ref[...].T).astype(BF16).reshape(16, 32, 128)
-
-
-def call(kernel, outs, *args, smem=(), flops=0):
-    specs = [
-        pl.BlockSpec(memory_space=pltpu.SMEM if n in smem else pltpu.VMEM) for n in range(len(args))
-    ]
+    out_ref[...] = dot_tn(grad, wq_ref[...]).astype(BF16).reshape(16, 32, 128)
+
+
+def call(kernel, outs, *args, flops=0):
     shapes = [jax.ShapeDtypeStruct(s, t) for s, t in outs]
     nbytes = sum(a.size * a.dtype.itemsize for a in args)
     return pl.pallas_call(
         kernel,
         out_shape=shapes,
-        in_specs=specs,
+        in_specs=[pl.BlockSpec(memory_space=pltpu.VMEM)] * len(args),
         out_specs=[pl.BlockSpec(memory_space=pltpu.VMEM)] * len(shapes),
         compiler_params=pltpu.CompilerParams(vmem_limit_bytes=24 * 1024 * 1024),
         cost_estimate=pl.CostEstimate(flops=flops, bytes_accessed=nbytes, transcendentals=0),
     )(*args)
 
 
+def call_copying(kernel, outs, *args):
+    shapes = [jax.ShapeDtypeStruct(s, t) for s, t in outs]
+    return pl.pallas_call(
+        kernel,
+        out_shape=shapes,
+        in_specs=[pl.BlockSpec(memory_space=pl.ANY)] * len(args),
+        out_specs=[pl.BlockSpec(memory_space=pltpu.VMEM)] * len(shapes),
+        scratch_shapes=[pltpu.VMEM(a.shape, a.dtype) for a in args]
+        + [pltpu.SemaphoreType.DMA((len(args),))],
+        compiler_params=pltpu.CompilerParams(vmem_limit_bytes=24 * 1024 * 1024),
+    )(*[pltpu.with_memory_space_constraint(a, pltpu.HBM) for a in args])
+
+
 def exchange(v):
     return lax.ppermute(v, "tmpl", [(0, 1), (1, 0)])
 
 
 def spread_chunks(v, rows):
-    return lax.all_to_all(v.reshape(128, rows, 128), GROUP, 0, 0, tiled=True).reshape(128 * rows, 128)
+    v = lax.all_to_all(v.reshape(128, rows, 128), GROUP, 0, 0, axis_index_groups=[ORDER], tiled=True)
+    return v.reshape(128 * rows, 128)
 
 
 def body(
@@ -339,33 +394,36 @@
     key_weight, value_weight, query_weight, output_weight,
 ):
     gi, gm, gf = gain_in.reshape(1, 64), gain_mid.reshape(1, 64), gain_final.reshape(1, 64)
-    sides, x, normed = call(
+    sides, x, normed, gat, query, grad_out, wide, kv, gm_wide, gf_wide, gi_wide, absent = call_copying(
         front_kernel,
-        [((1024, 128), BF16), ((64, 1024), BF16), ((64, 1024), BF16)],
-        template_pair, pair_mask, gi, proj_a, gate_a, proj_b, gate_b,
-    )
-    gat, query, grad_out = call(
-        side_kernel,
-        [((64, 1024), F32), ((64, 512), BF16), ((64, 512), F32)],
-        normed, main_pair, update_cotangent, gate_out, query_weight, output_weight,
+        [
+            ((1024, 128), BF16), ((64, 1024), BF16), ((64, 1024), BF16), ((64, 1024), F32),
+            ((64, 512), BF16), ((64, 512), F32), ((256, 256), BF16), ((64, 128), BF16),
+            ((256, 128), F32), ((64, 128), F32), ((64, 128), F32), ((8, 1024), F32),
+        ],
+        template_pair, pair_mask, gi, proj_a, gate_a, proj_b, gate_b, gate_out, main_pair,
+        update_cotangent, query_weight.T, output_weight, proj_out, key_weight, value_weight, gm, gf,
+        template_mask.reshape(1, 2),
     )
     sides = spread_chunks(sides, 8)
     prod, a, b = call(
         product_kernel, [((512, 128), BF16), ((256, 256), BF16), ((256, 256), BF16)], sides
     )
     prod = spread_chunks(prod, 4)
-    stat, weights, along, key = call(
+    stat, weights, along, key, hat_m, rstd_m, out, hat_f, rstd_f = call(
         score_kernel,
-        [((2, 4, 512), F32), ((4, 1024), F32), ((4, 1024), F32), ((64, 1024), BF16)],
-        x, prod, gat, query, grad_out, template_mask, gm, gf, proj_out, key_weight, value_weight,
-        smem=(5,),
+        [
+            ((2, 4, 512), F32), ((4, 1024), F32), ((4, 1024), F32), ((64, 1024), BF16),
+            ((256, 256), F32), ((8, 256), F32), ((64, 1024), F32), ((64, 1024), F32), ((1, 1024), F32),
+        ],
+        x, prod, gat, query, grad_out, absent, gm_wide, gf_wide, wide, kv,
     )
     other = exchange(stat)
     pg, query_sum, d_updated, d_gate = call(
         grad_kernel,
         [((512, 128), BF16), ((64, 512), F32), ((64, 1024), F32), ((64, 1024), BF16)],
-        x, prod, gat, query, grad_out, key, weights, along, stat, other,
-        gm, gf, proj_out, key_weight, value_weight,
+        gat, query, grad_out, key, weights, along, stat, other,
+        gm_wide, gf_wide, wide, kv, hat_m, rstd_m, out, hat_f, rstd_f,
     )
     cg, cp, wg, wp, dn = call(
         coef_kernel,
@@ -378,10 +436,10 @@
     pg = spread_chunks(pg, 4)
     (grads,) = call(triangle_kernel, [((1024, 128), BF16)], pg, a, b)
     query_other = exchange(query_sum)
-    (main_grad,) = call(main_kernel, [((16, 32, 128), BF16)], query_sum, query_other, query_weight)
+    (main_grad,) = call(main_kernel, [((16, 32, 128), BF16)], query_sum, query_other, query_weight.T)
     grads = spread_chunks(grads, 8)
     (pair_grad,) = call(
-        finish_kernel, [((2, 16, 32, 64), BF16)], grads, cg, cp, wg, wp, dn, x, d_updated, gi
+        finish_kernel, [((2, 16, 32, 64), BF16)], grads, cg, cp, wg, wp, dn, x, d_updated, gi_wide
     )
     return (pair_grad, main_grad)
 

time: 103 us -> 91 us (0.88)
  the two profiles are of different devices: /device:TPU:1 before, /device:TPU:6 now
where the time goes in v2:
time: 91 us; the launch traced here: 90.2 us
  blocking collectives  57.3 us (63%)
  starting transfers between devices  12.2 us (13%)
  waiting for transfers between devices  10.8 us (12%)
  Pallas kernels  9.05 us (10%)
    all_to_all x3, blocking collectives, spread_chunks(): lax.all_to_all(v.reshape(128, rows, 128), GROUP, 0, 0, axis_index_groups=...  57.3 us
    ppermute x2, waiting for transfers between devices, exchange(): return lax.ppermute(v, 'tmpl', [(0, 1), (1, 0)])  10.1 us
    all_to_all x1, starting transfers between devices, spread_chunks(): lax.all_to_all(v.reshape(128, rows, 128), GROUP, 0, 0, axis_index_groups=...  9.26 us
    pallas_call x7, Pallas kernels, call(): pl.pallas_call(kernel, out_shape=shapes, in_specs=[pl.BlockSpec(memory_sp...  6.77 us
    ppermute x2, starting transfers between devices, exchange(): return lax.ppermute(v, 'tmpl', [(0, 1), (1, 0)])  2.96 us
    pallas_call x1, Pallas kernels, call_copying(): pl.pallas_call(kernel, out_shape=shapes, in_specs=[pl.BlockSpec(memory_sp...  2.28 us
  transfers between devices with their start and end apart: 3, of which 3 were waited for; matrix products, arithmetic and copies ran while one was open for 0% of the time, Pallas kernels for 2%

profile of v2, /device:TPU:6, one launch (start us, length us, event | category | flops | bytes accessed | tf_op | source)
XLA Modules:
  0.0 90.2 jit_solution(47232450537630757)
XLA Ops:
  0.6 2.3 %shard_map.185 = (bf16[1024,128]{1,0:T(8,128)(2,1)S(1)}, bf16[64,1024]{1,0:T(8,128)(2,1)S(1)}, bf16[64,1024]{1,0:T(8,128)(2,1)S(1)}, f32[64,1024]{1,0:T(8,128)S(...) custom-call(bf16[2,16,32,64]{3,2,1,0:T(8,128)(2,1)} %x_hbm.1, ...), custom_call_target="tpu_custom_call" | custom-call | tf_op jit(solution)/shard_map/pallas_call | solution.py:371
  2.9 24.3 %all_to_all.20 = bf16[128,8,128]{2,1,0:T(8,128)(2,1)S(1)} all-to-all(bf16[128,8,128]{2,1,0:T(8,128)(2,1)S(1)} %bitcast.17), channel_id=1, replica_groups={{96,97,98,99,100,101,102,103,104,105,106,107,108,109,110,111,112,113,11..., dimensions={0} | all-to-all | bytes 524288 | tf_op jit(solution)/shard_map/all_to_all | solution.py:387
  27.3 0.9 %shard_map.186 = (bf16[512,128]{1,0:T(8,128)(2,1)S(1)}, bf16[256,256]{1,0:T(8,128)(2,1)S(1)}, bf16[256,256]{1,0:T(8,128)(2,1)S(1)}) custom-call(bf16[1024,128]{1,0:T(8,128)(2,1)S(1)} %bitcast.13), custom_call_target="tpu_custom_call" | custom-call | bytes 262144 | tf_op jit(solution)/shard_map/pallas_call | solution.py:359
  28.2 16.6 %all_to_all.21 = bf16[128,4,128]{2,1,0:T(4,128)(2,1)S(1)} all-to-all(bf16[128,4,128]{2,1,0:T(4,128)(2,1)S(1)} %bitcast.19), channel_id=1, replica_groups={{96,97,98,99,100,101,102,103,104,105,106,107,108,109,110,111,112,113,11..., dimensions={0} | all-to-all | bytes 262144 | tf_op jit(solution)/shard_map/all_to_all | solution.py:387
  44.8 0.6 shard_map.187
  45.4 1.5 %collective-permute-start = (f32[2,4,512]{2,1,0:T(4,128)S(1)}, f32[2,4,512]{2,1,0:T(4,128)S(1)}, u32[]{:S(2)}, u32[]{:S(2)}) collective-permute-start(f32[2,4,512]{2,1,0:T(4,128)S(1)} %get-tuple-element.49.mine_ref), channel_id=1, source_target_pairs={{0,128},{128,0},{1,129},{129,1},{2,130},{130,2},{3,131},{131,3},{4... | collective-permute-start | bytes 49160 | tf_op jit(solution)/shard_map/ppermute | solution.py:383
  46.9 3.8 %collective-permute-done.other_ref = f32[2,4,512]{2,1,0:T(4,128)S(1)} collective-permute-done((f32[2,4,512]{2,1,0:T(4,128)S(1)}, f32[2,4,512]{2,1,0:T(4,128)S(1)}, u32[]{:S(2)}, u32[]{:S(2)}) %collective-permute-start) | collective-permute-done | bytes 16416 | tf_op jit(solution)/shard_map/ppermute | solution.py:383
  50.7 0.6 shard_map.188
  51.3 16.4 %all_to_all.22 = bf16[128,4,128]{2,1,0:T(4,128)(2,1)S(1)} all-to-all(bf16[128,4,128]{2,1,0:T(4,128)(2,1)S(1)} %bitcast.18), channel_id=1, replica_groups={{96,97,98,99,100,101,102,103,104,105,106,107,108,109,110,111,112,113,11..., dimensions={0} | all-to-all | bytes 262144 | tf_op jit(solution)/shard_map/all_to_all | solution.py:387
  67.7 1.6 %shard_map.189 = bf16[1024,128]{1,0:T(8,128)(2,1)} custom-call(bf16[512,128]{1,0:T(8,128)(2,1)S(1)} %bitcast.15, bf16[256,256]{1,0:T(8,128)(2,1)S(1)} %get-tuple-element.56.a_ref, bf16[256,256]{1,0:T(8,128)(2,1)S(1)} %get-tuple-element.57.b_ref), custom_call_target="tpu_custom_call" | custom-call | bytes 393216 | tf_op jit(solution)/shard_map/pallas_call | solution.py:359
  69.3 0.0 copy-start
  69.3 0.0 copy-start.1
  69.3 0.0 copy-start.2
  69.3 0.0 copy-start.3
  69.3 0.0 copy-start.4
  69.4 0.0 copy-start.6
  69.4 9.3 %all-to-all-start.3 = ((bf16[128,8,128]{2,1,0:T(8,128)(2,1)}), bf16[128,8,128]{2,1,0:T(8,128)(2,1)S(1)}, u32[]{:S(2)}, u32[]{:S(2)}) async-start(bf16[128,8,128]{2,1,0:T(8,128)(2,1)} %bitcast.11), calls=%async_computation.3 | async-start | bytes 524288 | tf_op jit(solution)/shard_map/all_to_all | solution.py:387
  78.6 1.5 %collective-permute-start.1 = (f32[64,512]{1,0:T(8,128)S(1)}, f32[64,512]{1,0:T(8,128)S(1)}, u32[]{:S(2)}, u32[]{:S(2)}) collective-permute-start(f32[64,512]{1,0:T(8,128)S(1)} %get-tuple-element.67.mine_ref), channel_id=1, source_target_pairs={{0,128},{128,0},{1,129},{129,1},{2,130},{130,2},{3,131},{131,3},{4... | collective-permute-start | bytes 393224 | tf_op jit(solution)/shard_map/ppermute | solution.py:383
  80.1 0.0 copy-done
  80.1 0.0 copy-done.1
  80.1 0.0 copy-done.2
  80.1 0.0 copy-done.3
  80.1 0.0 copy-done.4
  80.1 0.0 copy-done.6
  80.2 0.0 copy-start.5
  80.2 0.8 shard_map.190
  80.9 6.2 %collective-permute-done.1.other_ref = f32[64,512]{1,0:T(8,128)S(1)} collective-permute-done((f32[64,512]{1,0:T(8,128)S(1)}, f32[64,512]{1,0:T(8,128)S(1)}, u32[]{:S(2)}, u32[]{:S(2)}) %collective-permute-start.1) | collective-permute-done | bytes 131104 | tf_op jit(solution)/shard_map/ppermute | solution.py:383
  87.2 0.0 copy-done.5
  87.2 0.9 shard_map.192
  88.0 0.7 all-to-all-done.3
  88.8 1.4 %shard_map.191 = bf16[2,16,32,64]{3,2,1,0:T(8,128)(2,1)} custom-call(bf16[1024,128]{1,0:T(8,128)(2,1)S(1)} %bitcast.14, f32[512,256]{1,0:T(8,128)S(1)} %get-tuple-element.60.cg_ref, f32[512,256]{1,0:T(8,128)S(1)} %get-tuple-element.61.cp_ref, bf16[256,512]{1,0:T(8,128)(2,1)S(1)} %get-tuple-element.62.wg_ref, bf16[256,512]{1,0:T(8,128)(2,1)S(1)} %get-tuple-element.63.wp_ref, ...), custom_call_target="tpu_custom_call" | custom-call | bytes 2523136 | tf_op jit(solution)/shard_map/pallas_call | solution.py:359
Async XLA Ops:
  45.4 5.3 %collective-permute-start = (f32[2,4,512]{2,1,0:T(4,128)S(1)}, f32[2,4,512]{2,1,0:T(4,128)S(1)}, u32[]{:S(2)}, u32[]{:S(2)}) collective-permute-start(f32[2,4,512]{2,1,0:T(4,128)S(1)} %get-tuple-element.49.mine_ref), channel_id=1, source_target_pairs={{0,128},{128,0},{1,129},{129,1},{2,130},{130,2},{3,131},{131,3},{4... | collective-permute-start | bytes 49160 | tf_op jit(solution)/shard_map/ppermute | solution.py:383
  69.3 10.8 %copy-start = (bf16[64,64]{1,0:T(8,128)(2,1)S(1)}, bf16[64,64]{1,0:T(8,128)(2,1)}, u32[]{:S(2)}) copy-start(bf16[64,64]{1,0:T(8,128)(2,1)} %pa_ref.1) | copy-start | bytes 24580
  69.3 10.8 %copy-start.1 = (bf16[64,64]{1,0:T(8,128)(2,1)S(1)}, bf16[64,64]{1,0:T(8,128)(2,1)}, u32[]{:S(2)}) copy-start(bf16[64,64]{1,0:T(8,128)(2,1)} %ga_ref.1) | copy-start | bytes 24580
  69.3 10.8 %copy-start.2 = (bf16[64,64]{1,0:T(8,128)(2,1)S(1)}, bf16[64,64]{1,0:T(8,128)(2,1)}, u32[]{:S(2)}) copy-start(bf16[64,64]{1,0:T(8,128)(2,1)} %pb_ref.1) | copy-start | bytes 24580
  69.3 10.8 %copy-start.3 = (bf16[64,64]{1,0:T(8,128)(2,1)S(1)}, bf16[64,64]{1,0:T(8,128)(2,1)}, u32[]{:S(2)}) copy-start(bf16[64,64]{1,0:T(8,128)(2,1)} %gb_ref.1) | copy-start | bytes 24580
  69.3 10.8 %copy-start.4 = (bf16[64,64]{1,0:T(8,128)(2,1)S(1)}, bf16[64,64]{1,0:T(8,128)(2,1)}, u32[]{:S(2)}) copy-start(bf16[64,64]{1,0:T(8,128)(2,1)} %go_ref.1) | copy-start | bytes 24580
  69.4 10.8 %copy-start.6 = (s32[16,32]{1,0:T(8,128)S(1)}, s32[16,32]{1,0:T(8,128)}, u32[]{:S(2)}) copy-start(s32[16,32]{1,0:T(8,128)} %mask_ref.1) | copy-start | bytes 6148
  69.4 19.4 %all-to-all-start.3 = ((bf16[128,8,128]{2,1,0:T(8,128)(2,1)}), bf16[128,8,128]{2,1,0:T(8,128)(2,1)S(1)}, u32[]{:S(2)}, u32[]{:S(2)}) async-start(bf16[128,8,128]{2,1,0:T(8,128)(2,1)} %bitcast.11), calls=%async_computation.3 | async-start | bytes 524288 | tf_op jit(solution)/shard_map/all_to_all | solution.py:387
  78.6 8.5 %collective-permute-start.1 = (f32[64,512]{1,0:T(8,128)S(1)}, f32[64,512]{1,0:T(8,128)S(1)}, u32[]{:S(2)}, u32[]{:S(2)}) collective-permute-start(f32[64,512]{1,0:T(8,128)S(1)} %get-tuple-element.67.mine_ref), channel_id=1, source_target_pairs={{0,128},{128,0},{1,129},{129,1},{2,130},{130,2},{3,131},{131,3},{4... | collective-permute-start | bytes 393224 | tf_op jit(solution)/shard_map/ppermute | solution.py:383
  80.2 7.0 %copy-start.5 = (bf16[128,64]{0,1:T(8,128)(2,1)S(1)}, bf16[128,64]{0,1:T(8,128)(2,1)}, u32[]{:S(2)}) copy-start(bf16[128,64]{0,1:T(8,128)(2,1)} %param.34) | copy-start | bytes 49156

commit v3 on v2

--- a/solution.py
+++ b/solution.py
@@ -16,11 +16,17 @@
 SCALE = 1.0 / math.sqrt(HEAD_DIM)
 GROUP = ("row", "col")
 TURN = 12
+SIDE_BLOCKS = [(s, side, r) for s in range(2) for side in range(2) for r in range(4)]
+PIXEL_ROWS = [4 * q + r for r in range(4) for q in range(4)]
 ORDER = [p ^ (8 * TURN) for p in range(128)]
 
 
 def iota(shape, axis):
     return lax.broadcasted_iota(jnp.int32, shape, axis)
+
+
+def shr(v, n):
+    return lax.shift_right_logical(v, jnp.full(v.shape, n, jnp.int32))
 
 
 def onehot(cond):
@@ -64,7 +70,7 @@
 
 
 def column(gain_row, repeat):
-    pick = iota((64 * repeat, 64), 0) // repeat == iota((64 * repeat, 64), 1)
+    pick = shr(iota((64 * repeat, 64), 0), repeat // 2) == iota((64 * repeat, 64), 1)
     return jnp.sum(jnp.where(pick, gain_row, 0.0), axis=1, keepdims=True)
 
 
@@ -103,34 +109,24 @@
     return rstd * (scaled - spread_cr(mean_cr(scaled)) - hat * spread_cr(mean_cr(scaled * hat)))
 
 
-def wide_pair(wa, wb):
-    row, lane = iota((64, 512), 0), iota((64, 512), 1)
-    own = row == lane // 8
-    base = dot(wa, onehot(own & (lane % 8 < 4))) + dot(wb, onehot(own & (lane % 8 >= 4)))
-    return jnp.concatenate([jnp.where(lane % 4 == r, base, 0.0) for r in range(4)], axis=0).astype(BF16)
-
-
 def wide_out(w):
     row, lane = iota((64, 256), 0), iota((64, 256), 1)
-    base = dot_tn(w, onehot(row == lane // 4))
-    return jnp.concatenate([jnp.where(lane % 4 == r, base, 0.0) for r in range(4)], axis=0).astype(BF16)
-
-
-def wide_mask(mask):
-    tiled = dot(mask.astype(F32).astype(BF16), onehot(iota((32, 256), 0) == iota((32, 256), 1) % 32))
-    i, lane = iota((16, 256), 0), iota((16, 256), 1)
-    tiled = jnp.where(i % 4 == (lane % 128) // 32, tiled, 0.0).astype(BF16)
-    return dot(onehot(iota((8, 16), 0) % 4 == iota((8, 16), 1) // 4), tiled)
-
-
-def spread8(v):
-    return jnp.broadcast_to(v[None], (64, 8, 256)).reshape(512, 256)
+    base = dot_tn(w, onehot(row == shr(lane, 2)))
+    return jnp.concatenate([jnp.where((lane & 3) == r, base, 0.0) for r in range(4)], axis=0).astype(BF16)
+
+
+def mask_row(mask):
+    tiled = dot(mask.astype(F32).astype(BF16), onehot(iota((32, 128), 0) == (iota((32, 128), 1) & 31)))
+    i, lane = iota((16, 128), 0), iota((16, 128), 1)
+    tiled = jnp.where(shr(i, 2) == shr(lane, 5), tiled, 0.0).astype(BF16)
+    rows = dot(onehot((iota((8, 16), 0) & 3) == (iota((8, 16), 1) & 3)), tiled)
+    return both(jnp.concatenate([rows[r : r + 1] for r in range(4)], axis=1))
 
 
 def swap_groups(four):
-    lane = iota(four[0].shape, 1) // 32
+    lane = iota(four[0].shape, 1)
     for bit in (1, 2):
-        low = (lane & bit) == 0
+        low = (lane & (32 * bit)) == 0
         out = []
         for a in range(4):
             if a & bit == 0:
@@ -156,22 +152,16 @@
     return jnp.where(top, even, pltpu.roll(odd, 4, 1)), jnp.where(top, pltpu.roll(even, 4, 1), odd)
 
 
-def sides_first():
-    a, b = iota((128, 128), 0), iota((128, 128), 1)
-    return onehot((a // 64 == (b // 4) % 2) & ((a % 64) // 4 == b // 8) & (a % 4 == b % 4))
-
-
-def natural_rows():
-    a, b = iota((256, 256), 0), iota((256, 256), 1)
-    return onehot((a % 4 == b // 64) & ((a // 4) ^ (4 * TURN) == b % 64))
+def turn(v):
+    return jnp.concatenate([v[n ^ TURN : (n ^ TURN) + 4] for n in range(0, 16, 4)], axis=0)
 
 
 def front_kernel(
     x_hbm, mask_hbm, gi_hbm, pa_hbm, ga_hbm, pb_hbm, gb_hbm, go_hbm, main_hbm, cot_hbm, wq_hbm, wo_hbm,
     po_hbm, kw_hbm, vw_hbm, gm_hbm, gf_hbm, present_hbm,
-    out_ref, x_out, n_out, gat_out, q_out, g_out, wide_out_ref, kv_out, gm_out, gf_out, gi_out, absent_out,
+    out_ref, x_out, n_out, gat_out, q_out, g_out, wide_out_ref, kv_out, gm_out, gf_out, gi_out, absent_out, sides_out, mask_out,
     x_ref, mask_ref, gi_ref, pa_ref, ga_ref, pb_ref, gb_ref, go_ref, main_ref, cot_ref, wq_ref, wo_ref,
-    po_ref, kw_ref, vw_ref, gm_ref, gf_ref, present_ref, sems,
+    po_ref, kw_ref, vw_ref, gm_ref, gf_ref, present_ref, tiles_ref, sems,
 ):
     pairs = [
         (x_hbm, x_ref), (gi_hbm, gi_ref), (pa_hbm, pa_ref), (ga_hbm, ga_ref), (pb_hbm, pb_ref),
@@ -182,27 +172,32 @@
     copies = [pltpu.make_async_copy(a, b, sems.at[n]) for n, (a, b) in enumerate(pairs)]
     for copy in copies:
         copy.start()
-    for copy in copies[:7]:
+    for copy in copies[1:7]:
         copy.wait()
-    x = dot_nt(eye64(), x_ref[...].reshape(1024, 64))
+    weights = jnp.concatenate([ga_ref[...], gb_ref[...], pa_ref[...], pb_ref[...]], axis=1)
+    sides_out[...] = weights
+    mask = mask_row(mask_ref[...])
+    mask_out[...] = jnp.broadcast_to(mask, (8, 1024))
+    copies[0].wait()
+    x = dot_nt(eye64(), jnp.concatenate([x_ref[s, i] for s in range(2) for i in PIXEL_ROWS], axis=0))
     hat, _ = hat_c(x)
     gi = column(gi_ref[...], 1)
     normed = (hat * gi).astype(BF16)
     x_out[...] = x.astype(BF16)
     n_out[...] = normed
-    rc = c_to_rc(normed)
-    gate = dot_tn(wide_pair(ga_ref[...], gb_ref[...]), rc)
-    proj = dot_tn(wide_pair(pa_ref[...], pb_ref[...]), rc)
-    mask = spread8(wide_mask(mask_ref[...]))
-    both_sides = (mask * jax.nn.sigmoid(gate) * proj).astype(BF16)
-    out_ref[:512, :] = both_sides[:, :128]
-    out_ref[512:, :] = both_sides[:, 128:]
+    both_sides = dot_tn(weights, normed)
+    both_sides = mask * jax.nn.sigmoid(both_sides[:128]) * both_sides[128:]
+    for s, side, r in SIDE_BLOCKS:
+        tiles_ref[pl.ds(s * 512 + side * 4 + r, 64, stride=8), :] = both_sides[
+            side * 64 : side * 64 + 64, s * 512 + r * 128 : s * 512 + r * 128 + 128
+        ]
+    out_ref[...] = tiles_ref[...].astype(BF16)
     gi_out[...] = jnp.broadcast_to(gi, (64, 128))
     for copy in copies[7:]:
         copy.wait()
     gat_out[...] = jax.nn.sigmoid(dot_tn(go_ref[...], normed))
-    q_out[...] = dot_nt(wq_ref[...], main_ref[...].reshape(512, 128)).astype(BF16)
-    g_out[...] = dot_nt(wo_ref[...], cot_ref[...].reshape(512, 128))
+    q_out[...] = dot_nt(wq_ref[...], jnp.concatenate([main_ref[i] for i in PIXEL_ROWS], axis=0)).astype(BF16)
+    g_out[...] = dot_nt(wo_ref[...], jnp.concatenate([cot_ref[i] for i in PIXEL_ROWS], axis=0))
     wide_out_ref[...] = wide_out(po_ref[...])
     kv_out[...] = jnp.concatenate([kw_ref[...], vw_ref[...]], axis=1)
     gm_out[...] = jnp.broadcast_to(column(gm_ref[...], 4), (256, 128))
@@ -215,12 +210,16 @@
 
 def product_kernel(x_ref, out_ref, a_out, b_out):
     tiles = x_ref[...].astype(F32).reshape(16, 8, 8, 128)
-    blocks = [tiles[:, c].reshape(128, 128) for c in range(8)]
-    order = sides_first()
-    parts = [dot(order, v.astype(BF16)).astype(BF16) for v in swap_in(blocks)]
-    a = jnp.concatenate([v[:64] for v in parts], axis=0)
-    b = jnp.concatenate([v[64:] for v in parts], axis=0)
-    b = dot(natural_rows(), b).astype(BF16)
+    parts = [v.reshape(16, 8, 256) for v in swap_in([tiles[:, c].reshape(128, 128) for c in range(8)])]
+    rolled = [pltpu.roll(v, 4, 1) for v in parts]
+    top = iota((16, 8, 256), 1) < 4
+    a = [
+        jnp.where(top[:8], v.reshape(8, 2, 8, 256)[:, 0], w.reshape(8, 2, 8, 256)[:, 1]).reshape(64, 256)
+        for v, w in zip(parts, rolled)
+    ]
+    b = [turn(jnp.where(top, rolled[q], parts[q + 1])) for q in (0, 2)]
+    a = jnp.concatenate(a, axis=0).astype(BF16)
+    b = jnp.stack(b, axis=1).reshape(256, 256).astype(BF16)
     a_out[...] = a
     b_out[...] = b
     prod = dot_nt(a, b)
@@ -303,19 +302,14 @@
 
 
 def coef_kernel(
-    n_ref, mask_ref, dgate_ref, go_ref, pa_ref, ga_ref, pb_ref, gb_ref,
-    cg_out, cp_out, wg_out, wp_out, dn_out,
-):
-    wg = wide_pair(ga_ref[...], gb_ref[...])
-    wp = wide_pair(pa_ref[...], pb_ref[...])
-    rc = c_to_rc(n_ref[...])
-    gate = jax.nn.sigmoid(dot_tn(wg, rc))
-    proj = dot_tn(wp, rc)
-    scaled = spread8(wide_mask(mask_ref[...])) * gate
+    n_ref, x_ref, mask_ref, dgate_ref, go_ref, sides_ref, cg_out, cp_out, hat_out, rstd_out, dn_out
+):
+    both_sides = dot_tn(sides_ref[...], n_ref[...])
+    gate = jax.nn.sigmoid(both_sides[:128])
+    scaled = mask_ref[:1, :] * gate
     cp_out[...] = scaled
-    cg_out[...] = scaled * (1.0 - gate) * proj
-    wg_out[...] = wg
-    wp_out[...] = wp
+    cg_out[...] = scaled * (1.0 - gate) * both_sides[128:]
+    hat_out[...], rstd_out[...] = hat_c(x_ref[...].astype(F32))
     dn_out[...] = dot(go_ref[...], dgate_ref[...])
 
 
@@ -327,33 +321,48 @@
         for v in pair_up(tiles[:, 0, m].reshape(64, 128), tiles[:, 1, m].reshape(64, 128))
     ]
     pg = jnp.concatenate(swap_in(blocks), axis=0).astype(BF16)
-    left = dot(pg, b_ref[...]).astype(BF16)
-    right = dot_tn(dot(pg, natural_rows()).astype(BF16), a_ref[...]).astype(BF16)
-    order = sides_first()
-    rows = [
-        dot_tn(order, jnp.concatenate([left[q * 64 : q * 64 + 64], right[q * 64 : q * 64 + 64]], axis=0))
-        for q in range(4)
-    ]
+    left = dot(pg, b_ref[...]).reshape(4, 8, 8, 256)
+    right = dot_tn(pg, a_ref[...]).reshape(16, 2, 8, 256)
+    top = iota((16, 8, 256), 1) < 4
+    rows = []
+    for q in range(4):
+        upper = jnp.stack([left[q], pltpu.roll(left[q], 4, 1)], axis=1).reshape(16, 8, 256)
+        lower = turn(right[:, q // 2])
+        lower = lower if q & 1 else pltpu.roll(lower, 4, 1)
+        rows.append(jnp.where(top, upper, lower).reshape(128, 256))
     cols = [v.reshape(16, 8, 128) for v in swap_out(rows)]
     out_ref[...] = jnp.stack(cols, axis=1).reshape(1024, 128).astype(BF16)
 
 
-def finish_kernel(lr_ref, cg_ref, cp_ref, wg_ref, wp_ref, dn_ref, x_ref, du_ref, gain_ref, out_ref):
-    grad = jnp.concatenate([lr_ref[:512, :], lr_ref[512:, :]], axis=1).astype(F32)
-    d_gate = (grad * cg_ref[...]).astype(BF16)
-    d_proj = (grad * cp_ref[...]).astype(BF16)
-    d_normed = rc_to_c(dot(wg_ref[...], d_gate) + dot(wp_ref[...], d_proj)) + dn_ref[...]
-    hat, rstd = hat_c(x_ref[...].astype(F32))
-    grad_x = norm_grad_c(d_normed, tile_lanes(gain_ref[...], 8), hat, rstd) + du_ref[...]
-    out_ref[...] = dot_tn(grad_x.astype(BF16), eye64()).astype(BF16).reshape(2, 16, 32, 64)
+def finish_kernel(
+    lr_ref, cg_ref, cp_ref, sides_ref, dn_ref, hat_ref, rstd_ref, du_ref, gain_ref, out_ref, tiles_ref
+):
+    tiles_ref[...] = lr_ref[...].astype(F32)
+    blocks = [tiles_ref[pl.ds(s * 512 + side * 4 + r, 64, stride=8), :] for s, side, r in SIDE_BLOCKS]
+    grad = jnp.concatenate(
+        [
+            jnp.concatenate([blocks[s * 8 + side * 4 + r] for s in range(2) for r in range(4)], axis=1)
+            for side in range(2)
+        ],
+        axis=0,
+    )
+    grad = jnp.concatenate([(grad * cg_ref[...]).astype(BF16), (grad * cp_ref[...]).astype(BF16)], axis=0)
+    d_normed = dot(sides_ref[...], grad) + dn_ref[...]
+    grad_x = norm_grad_c(d_normed, tile_lanes(gain_ref[...], 8), hat_ref[...], rstd_ref[...]) + du_ref[...]
+    out = dot_tn(grad_x.astype(BF16), eye64()).astype(BF16)
+    for s in range(2):
+        for n, i in enumerate(PIXEL_ROWS):
+            out_ref[s, i] = out[s * 512 + n * 32 : s * 512 + n * 32 + 32]
 
 
 def main_kernel(mine_ref, other_ref, wq_ref, out_ref):
     grad = (mine_ref[...] + other_ref[...]).astype(BF16)
-    out_ref[...] = dot_tn(grad, wq_ref[...]).astype(BF16).reshape(16, 32, 128)
-
-
-def call(kernel, outs, *args, flops=0):
+    out = dot_tn(grad, wq_ref[...]).astype(BF16)
+    for n, i in enumerate(PIXEL_ROWS):
+        out_ref[i] = out[n * 32 : n * 32 + 32]
+
+
+def call(kernel, outs, *args, scratch=()):
     shapes = [jax.ShapeDtypeStruct(s, t) for s, t in outs]
     nbytes = sum(a.size * a.dtype.itemsize for a in args)
     return pl.pallas_call(
@@ -361,8 +370,9 @@
         out_shape=shapes,
         in_specs=[pl.BlockSpec(memory_space=pltpu.VMEM)] * len(args),
         out_specs=[pl.BlockSpec(memory_space=pltpu.VMEM)] * len(shapes),
+        scratch_shapes=scratch,
         compiler_params=pltpu.CompilerParams(vmem_limit_bytes=24 * 1024 * 1024),
-        cost_estimate=pl.CostEstimate(flops=flops, bytes_accessed=nbytes, transcendentals=0),
+        cost_estimate=pl.CostEstimate(flops=0, bytes_accessed=nbytes, transcendentals=0),
     )(*args)
 
 
@@ -374,7 +384,7 @@
         in_specs=[pl.BlockSpec(memory_space=pl.ANY)] * len(args),
         out_specs=[pl.BlockSpec(memory_space=pltpu.VMEM)] * len(shapes),
         scratch_shapes=[pltpu.VMEM(a.shape, a.dtype) for a in args]
-        + [pltpu.SemaphoreType.DMA((len(args),))],
+        + [pltpu.VMEM((1024, 128), F32), pltpu.SemaphoreType.DMA((len(args),))],
         compiler_params=pltpu.CompilerParams(vmem_limit_bytes=24 * 1024 * 1024),
     )(*[pltpu.with_memory_space_constraint(a, pltpu.HBM) for a in args])
 
@@ -394,12 +404,12 @@
     key_weight, value_weight, query_weight, output_weight,
 ):
     gi, gm, gf = gain_in.reshape(1, 64), gain_mid.reshape(1, 64), gain_final.reshape(1, 64)
-    sides, x, normed, gat, query, grad_out, wide, kv, gm_wide, gf_wide, gi_wide, absent = call_copying(
+    sides, x, normed, gat, query, grad_out, wide, kv, gm_wide, gf_wide, gi_wide, absent, side_weights, mask = call_copying(
         front_kernel,
         [
             ((1024, 128), BF16), ((64, 1024), BF16), ((64, 1024), BF16), ((64, 1024), F32),
             ((64, 512), BF16), ((64, 512), F32), ((256, 256), BF16), ((64, 128), BF16),
-            ((256, 128), F32), ((64, 128), F32), ((64, 128), F32), ((8, 1024), F32),
+            ((256, 128), F32), ((64, 128), F32), ((64, 128), F32), ((8, 1024), F32), ((64, 256), BF16), ((8, 1024), F32),
         ],
         template_pair, pair_mask, gi, proj_a, gate_a, proj_b, gate_b, gate_out, main_pair,
         update_cotangent, query_weight.T, output_weight, proj_out, key_weight, value_weight, gm, gf,
@@ -425,13 +435,10 @@
         gat, query, grad_out, key, weights, along, stat, other,
         gm_wide, gf_wide, wide, kv, hat_m, rstd_m, out, hat_f, rstd_f,
     )
-    cg, cp, wg, wp, dn = call(
+    cg, cp, hat, rstd, dn = call(
         coef_kernel,
-        [
-            ((512, 256), F32), ((512, 256), F32), ((256, 512), BF16), ((256, 512), BF16),
-            ((64, 1024), F32),
-        ],
-        normed, pair_mask, d_gate, gate_out, proj_a, gate_a, proj_b, gate_b,
+        [((128, 1024), F32), ((128, 1024), F32), ((64, 1024), F32), ((1, 1024), F32), ((64, 1024), F32)],
+        normed, x, mask, d_gate, gate_out, side_weights,
     )
     pg = spread_chunks(pg, 4)
     (grads,) = call(triangle_kernel, [((1024, 128), BF16)], pg, a, b)
@@ -439,7 +446,9 @@
     (main_grad,) = call(main_kernel, [((16, 32, 128), BF16)], query_sum, query_other, query_weight.T)
     grads = spread_chunks(grads, 8)
     (pair_grad,) = call(
-        finish_kernel, [((2, 16, 32, 64), BF16)], grads, cg, cp, wg, wp, dn, x, d_updated, gi_wide
+        finish_kernel, [((2, 16, 32, 64), BF16)],
+        grads, cg, cp, side_weights, dn, hat, rstd, d_updated, gi_wide,
+        scratch=[pltpu.VMEM((1024, 128), F32)],
     )
     return (pair_grad, main_grad)
 

time: 91 us -> 90.1 us (level)
  Pallas kernels: 9.05 us -> 7.87 us
    pallas_call x7, Pallas kernels: 6.77 us -> 5.68 us  [call(): pl.pallas_call(kernel, out_shape=shapes, in_specs=[pl.BlockSpec(memory_sp...]
  transfers between devices with their start and end apart: 3 -> 3, of which waited for: 3 -> 3; matrix products, arithmetic and copies ran while one was open for 0% -> 0% of each run, Pallas kernels for 2% -> 1%
where the time goes in v3:
time: 90.1 us; the launch traced here: 89.3 us
  blocking collectives  57.3 us (64%)
  starting transfers between devices  12.2 us (14%)
  waiting for transfers between devices  11.2 us (12%)
  Pallas kernels  7.87 us (9%)
    all_to_all x3, blocking collectives, spread_chunks(): lax.all_to_all(v.reshape(128, rows, 128), GROUP, 0, 0, axis_index_groups=...  57.3 us
    ppermute x2, waiting for transfers between devices, exchange(): return lax.ppermute(v, 'tmpl', [(0, 1), (1, 0)])  10.5 us
    all_to_all x1, starting transfers between devices, spread_chunks(): lax.all_to_all(v.reshape(128, rows, 128), GROUP, 0, 0, axis_index_groups=...  9.25 us
    pallas_call x7, Pallas kernels, call(): pl.pallas_call(kernel, out_shape=shapes, in_specs=[pl.BlockSpec(memory_sp...  5.68 us
    ppermute x2, starting transfers between devices, exchange(): return lax.ppermute(v, 'tmpl', [(0, 1), (1, 0)])  3 us
    pallas_call x1, Pallas kernels, call_copying(): pl.pallas_call(kernel, out_shape=shapes, in_specs=[pl.BlockSpec(memory_sp...  2.19 us
  transfers between devices with their start and end apart: 3, of which 3 were waited for; matrix products, arithmetic and copies ran while one was open for 0% of the time, Pallas kernels for 1%

profile of v3, /device:TPU:6, one launch (start us, length us, event | category | flops | bytes accessed | tf_op | source)
XLA Modules:
  0.0 89.3 jit_solution(17479463614697773018)
XLA Ops:
  0.6 2.2 %shard_map.185 = (bf16[1024,128]{1,0:T(8,128)(2,1)S(1)}, bf16[64,1024]{1,0:T(8,128)(2,1)S(1)}, bf16[64,1024]{1,0:T(8,128)(2,1)S(1)}, f32[64,1024]{1,0:T(8,128)S(...) custom-call(bf16[2,16,32,64]{3,2,1,0:T(8,128)(2,1)} %x_hbm.1, ...), custom_call_target="tpu_custom_call" | custom-call | tf_op jit(solution)/shard_map/pallas_call | solution.py:381
  2.8 24.3 %all_to_all.20 = bf16[128,8,128]{2,1,0:T(8,128)(2,1)S(1)} all-to-all(bf16[128,8,128]{2,1,0:T(8,128)(2,1)S(1)} %bitcast.17), channel_id=1, replica_groups={{96,97,98,99,100,101,102,103,104,105,106,107,108,109,110,111,112,113,11..., dimensions={0} | all-to-all | bytes 524288 | tf_op jit(solution)/shard_map/all_to_all | solution.py:397
  27.2 0.6 shard_map.186
  27.8 16.6 %all_to_all.21 = bf16[128,4,128]{2,1,0:T(4,128)(2,1)S(1)} all-to-all(bf16[128,4,128]{2,1,0:T(4,128)(2,1)S(1)} %bitcast.19), channel_id=1, replica_groups={{96,97,98,99,100,101,102,103,104,105,106,107,108,109,110,111,112,113,11..., dimensions={0} | all-to-all | bytes 262144 | tf_op jit(solution)/shard_map/all_to_all | solution.py:397
  44.4 0.6 shard_map.187
  45.0 1.5 %collective-permute-start = (f32[2,4,512]{2,1,0:T(4,128)S(1)}, f32[2,4,512]{2,1,0:T(4,128)S(1)}, u32[]{:S(2)}, u32[]{:S(2)}) collective-permute-start(f32[2,4,512]{2,1,0:T(4,128)S(1)} %get-tuple-element.51.mine_ref), channel_id=1, source_target_pairs={{0,128},{128,0},{1,129},{129,1},{2,130},{130,2},{3,131},{131,3},{4... | collective-permute-start | bytes 49160 | tf_op jit(solution)/shard_map/ppermute | solution.py:393
  46.5 3.8 %collective-permute-done.other_ref = f32[2,4,512]{2,1,0:T(4,128)S(1)} collective-permute-done((f32[2,4,512]{2,1,0:T(4,128)S(1)}, f32[2,4,512]{2,1,0:T(4,128)S(1)}, u32[]{:S(2)}, u32[]{:S(2)}) %collective-permute-start) | collective-permute-done | bytes 16416 | tf_op jit(solution)/shard_map/ppermute | solution.py:393
  50.3 0.6 shard_map.188
  50.9 16.4 %all_to_all.22 = bf16[128,4,128]{2,1,0:T(4,128)(2,1)S(1)} all-to-all(bf16[128,4,128]{2,1,0:T(4,128)(2,1)S(1)} %bitcast.18), channel_id=1, replica_groups={{96,97,98,99,100,101,102,103,104,105,106,107,108,109,110,111,112,113,11..., dimensions={0} | all-to-all | bytes 262144 | tf_op jit(solution)/shard_map/all_to_all | solution.py:397
  67.3 1.3 %shard_map.189 = bf16[1024,128]{1,0:T(8,128)(2,1)} custom-call(bf16[512,128]{1,0:T(8,128)(2,1)S(1)} %bitcast.15, bf16[256,256]{1,0:T(8,128)(2,1)S(1)} %get-tuple-element.58.a_ref, bf16[256,256]{1,0:T(8,128)(2,1)S(1)} %get-tuple-element.59.b_ref), custom_call_target="tpu_custom_call" | custom-call | bytes 393216 | tf_op jit(solution)/shard_map/pallas_call | solution.py:368
  68.6 0.0 copy-start.1
  68.6 9.3 %all-to-all-start.3 = ((bf16[128,8,128]{2,1,0:T(8,128)(2,1)}), bf16[128,8,128]{2,1,0:T(8,128)(2,1)S(1)}, u32[]{:S(2)}, u32[]{:S(2)}) async-start(bf16[128,8,128]{2,1,0:T(8,128)(2,1)} %bitcast.11), calls=%async_computation.3 | async-start | bytes 524288 | tf_op jit(solution)/shard_map/all_to_all | solution.py:397
  77.9 1.5 %collective-permute-start.1 = (f32[64,512]{1,0:T(8,128)S(1)}, f32[64,512]{1,0:T(8,128)S(1)}, u32[]{:S(2)}, u32[]{:S(2)}) collective-permute-start(f32[64,512]{1,0:T(8,128)S(1)} %get-tuple-element.71.mine_ref), channel_id=1, source_target_pairs={{0,128},{128,0},{1,129},{129,1},{2,130},{130,2},{3,131},{131,3},{4... | collective-permute-start | bytes 393224 | tf_op jit(solution)/shard_map/ppermute | solution.py:393
  79.4 0.0 copy-done.1
  79.4 0.0 copy-start
  79.4 0.4 shard_map.190
  79.8 6.6 %collective-permute-done.1.other_ref = f32[64,512]{1,0:T(8,128)S(1)} collective-permute-done((f32[64,512]{1,0:T(8,128)S(1)}, f32[64,512]{1,0:T(8,128)S(1)}, u32[]{:S(2)}, u32[]{:S(2)}) %collective-permute-start.1) | collective-permute-done | bytes 131104 | tf_op jit(solution)/shard_map/ppermute | solution.py:393
  86.4 0.0 copy-done
  86.4 0.9 shard_map.192
  87.3 0.7 all-to-all-done.3
  88.0 1.3 %shard_map.191 = bf16[2,16,32,64]{3,2,1,0:T(8,128)(2,1)} custom-call(bf16[1024,128]{1,0:T(8,128)(2,1)S(1)} %bitcast.13, f32[128,1024]{1,0:T(8,128)S(1)} %get-tuple-element.64.cg_ref, f32[128,1024]{1,0:T(8,128)S(1)} %get-tuple-element.65.cp_ref, bf16[64,256]{1,0:T(8,128)(2,1)S(1)} %get-tuple-element.63.sides_ref, f32[64,1024]{1,0:T(8,128)S(1)} %get-tuple-element.66.dn_ref, ...), custom_call_target="tpu_custom_call" | custom-call | bytes 2166784 | tf_op jit(solution)/shard_map/pallas_call | solution.py:368
Async XLA Ops:
  45.0 5.3 %collective-permute-start = (f32[2,4,512]{2,1,0:T(4,128)S(1)}, f32[2,4,512]{2,1,0:T(4,128)S(1)}, u32[]{:S(2)}, u32[]{:S(2)}) collective-permute-start(f32[2,4,512]{2,1,0:T(4,128)S(1)} %get-tuple-element.51.mine_ref), channel_id=1, source_target_pairs={{0,128},{128,0},{1,129},{129,1},{2,130},{130,2},{3,131},{131,3},{4... | collective-permute-start | bytes 49160 | tf_op jit(solution)/shard_map/ppermute | solution.py:393
  68.6 10.8 %copy-start.1 = (bf16[64,64]{1,0:T(8,128)(2,1)S(1)}, bf16[64,64]{1,0:T(8,128)(2,1)}, u32[]{:S(2)}) copy-start(bf16[64,64]{1,0:T(8,128)(2,1)} %go_ref.1) | copy-start | bytes 24580
  68.6 19.4 %all-to-all-start.3 = ((bf16[128,8,128]{2,1,0:T(8,128)(2,1)}), bf16[128,8,128]{2,1,0:T(8,128)(2,1)S(1)}, u32[]{:S(2)}, u32[]{:S(2)}) async-start(bf16[128,8,128]{2,1,0:T(8,128)(2,1)} %bitcast.11), calls=%async_computation.3 | async-start | bytes 524288 | tf_op jit(solution)/shard_map/all_to_all | solution.py:397
  77.9 8.5 %collective-permute-start.1 = (f32[64,512]{1,0:T(8,128)S(1)}, f32[64,512]{1,0:T(8,128)S(1)}, u32[]{:S(2)}, u32[]{:S(2)}) collective-permute-start(f32[64,512]{1,0:T(8,128)S(1)} %get-tuple-element.71.mine_ref), channel_id=1, source_target_pairs={{0,128},{128,0},{1,129},{129,1},{2,130},{130,2},{3,131},{131,3},{4... | collective-permute-start | bytes 393224 | tf_op jit(solution)/shard_map/ppermute | solution.py:393
  79.4 7.0 %copy-start = (bf16[128,64]{0,1:T(8,128)(2,1)S(1)}, bf16[128,64]{0,1:T(8,128)(2,1)}, u32[]{:S(2)}) copy-start(bf16[128,64]{0,1:T(8,128)(2,1)} %param.34) | copy-start | bytes 49156

commit v4 on v3

--- a/solution.py
+++ b/solution.py
@@ -15,10 +15,10 @@
 HEAD_DIM = 16
 SCALE = 1.0 / math.sqrt(HEAD_DIM)
 GROUP = ("row", "col")
-TURN = 12
+TURN = 6
 SIDE_BLOCKS = [(s, side, r) for s in range(2) for side in range(2) for r in range(4)]
 PIXEL_ROWS = [4 * q + r for r in range(4) for q in range(4)]
-ORDER = [p ^ (8 * TURN) for p in range(128)]
+ORDER = [[(z ^ TURN) * 16 + core * 8 + col for z in range(8) for col in range(8)] for core in range(2)]
 
 
 def iota(shape, axis):
@@ -147,13 +147,18 @@
 
 
 def pair_up(even, odd):
-    even, odd = even.reshape(8, 8, 128), odd.reshape(8, 8, 128)
-    top = iota(even.shape, 1) < 4
-    return jnp.where(top, even, pltpu.roll(odd, 4, 1)), jnp.where(top, pltpu.roll(even, 4, 1), odd)
+    top = iota(even.shape, even.ndim - 2) < 4
+    axis = even.ndim - 2
+    return jnp.where(top, even, pltpu.roll(odd, 4, axis)), jnp.where(top, pltpu.roll(even, 4, axis), odd)
 
 
 def turn(v):
-    return jnp.concatenate([v[n ^ TURN : (n ^ TURN) + 4] for n in range(0, 16, 4)], axis=0)
+    return jnp.concatenate([v[n ^ TURN : (n ^ TURN) + 2] for n in range(0, 8, 2)], axis=0)
+
+
+def by_core(first, second):
+    core0 = (lax.axis_index("row") & 1) == 0
+    return jnp.where(core0, first, second), jnp.where(core0, second, first)
 
 
 def front_kernel(
@@ -208,24 +213,36 @@
     )
 
 
-def product_kernel(x_ref, out_ref, a_out, b_out):
-    tiles = x_ref[...].astype(F32).reshape(16, 8, 8, 128)
-    parts = [v.reshape(16, 8, 256) for v in swap_in([tiles[:, c].reshape(128, 128) for c in range(8)])]
-    rolled = [pltpu.roll(v, 4, 1) for v in parts]
-    top = iota((16, 8, 256), 1) < 4
-    a = [
-        jnp.where(top[:8], v.reshape(8, 2, 8, 256)[:, 0], w.reshape(8, 2, 8, 256)[:, 1]).reshape(64, 256)
-        for v, w in zip(parts, rolled)
-    ]
-    b = [turn(jnp.where(top, rolled[q], parts[q + 1])) for q in (0, 2)]
-    a = jnp.concatenate(a, axis=0).astype(BF16)
-    b = jnp.stack(b, axis=1).reshape(256, 256).astype(BF16)
-    a_out[...] = a
-    b_out[...] = b
-    prod = dot_nt(a, b)
-    cols = swap_out([prod[q * 64 : q * 64 + 64] for q in range(4)])
-    pairs = [jnp.stack(pair_up(cols[c], cols[c + 1]), axis=1) for c in range(0, 8, 2)]
-    out_ref[...] = jnp.stack(pairs, axis=2).reshape(512, 128).astype(BF16)
+def layout_kernel(x_ref, a_out, b_out):
+    tiles = x_ref[...].astype(F32).reshape(8, 8, 2, 8, 128)
+    parts = [v.reshape(8, 2, 8, 256) for v in swap_in([tiles[:, c].reshape(128, 128) for c in range(8)])]
+    rolled = [pltpu.roll(v.reshape(16, 8, 256), 4, 1).reshape(8, 2, 8, 256) for v in parts]
+    top = iota((8, 8, 256), 1) < 4
+    a, b = [], []
+    for e in range(2):
+        for v, w in zip(parts, rolled):
+            v, w = v[:, e].reshape(4, 2, 8, 256), w[:, e].reshape(4, 2, 8, 256)
+            a.append(jnp.where(top[:4], v[:, 0], w[:, 1]).reshape(32, 256))
+        half = [turn(jnp.where(top, rolled[q][:, e], parts[q + 1][:, e])) for q in (0, 2)]
+        b.append(jnp.stack(half, axis=1).reshape(128, 256))
+    a_out[...] = jnp.concatenate(a, axis=0).astype(BF16)
+    b_out[...] = jnp.concatenate(b, axis=0).astype(BF16)
+
+
+def product_kernel(a_ref, own_ref, other_ref, out_ref, b_out):
+    prods = []
+    for e in range(2):
+        own = own_ref[e * 128 : e * 128 + 128, :].reshape(8, 16, 256)
+        other = other_ref[e * 128 : e * 128 + 128, :].reshape(8, 16, 256)
+        b = jnp.stack(by_core(own, other), axis=1).reshape(256, 256)
+        b_out[e * 256 : e * 256 + 256, :] = b
+        prods.append(dot_nt(a_ref[e * 128 : e * 128 + 128, :], b))
+    rows = [jnp.concatenate([v[q * 32 : q * 32 + 32] for v in prods], axis=0) for q in range(4)]
+    pairs = []
+    for v in swap_out(rows):
+        v = v.reshape(2, 4, 8, 128)
+        pairs.append(jnp.stack(pair_up(v[0], v[1]), axis=1).reshape(8, 8, 128))
+    out_ref[...] = jnp.stack(pairs, axis=1).reshape(512, 128).astype(BF16)
 
 
 def heads_sum(v):
@@ -313,24 +330,40 @@
     dn_out[...] = dot(go_ref[...], dgate_ref[...])
 
 
-def triangle_kernel(pg_ref, a_ref, b_ref, out_ref):
-    tiles = pg_ref[...].astype(F32).reshape(8, 2, 4, 8, 128)
-    blocks = [
-        v.reshape(64, 128)
-        for m in range(4)
-        for v in pair_up(tiles[:, 0, m].reshape(64, 128), tiles[:, 1, m].reshape(64, 128))
-    ]
-    pg = jnp.concatenate(swap_in(blocks), axis=0).astype(BF16)
-    left = dot(pg, b_ref[...]).reshape(4, 8, 8, 256)
-    right = dot_tn(pg, a_ref[...]).reshape(16, 2, 8, 256)
-    top = iota((16, 8, 256), 1) < 4
+def right_kernel(pg_ref, a_ref, pg_out, own_out, sent_out):
+    tiles = pg_ref[...].astype(F32).reshape(8, 8, 8, 128)
+    parts = swap_in([tiles[:, c].reshape(64, 128) for c in range(8)])
+    split = [pair_up(v.reshape(4, 2, 8, 256)[:, 0], v.reshape(4, 2, 8, 256)[:, 1]) for v in parts]
+    for e in range(2):
+        pg = jnp.concatenate([v[e].reshape(32, 256) for v in split], axis=0).astype(BF16)
+        pg_out[e * 128 : e * 128 + 128, :] = pg
+        right = dot_tn(pg, a_ref[e * 128 : e * 128 + 128, :]).reshape(8, 2, 16, 256)
+        own, sent = by_core(right[:, 0], right[:, 1])
+        own_out[e * 128 : e * 128 + 128, :] = own.reshape(128, 256)
+        sent_out[e * 128 : e * 128 + 128, :] = sent.reshape(128, 256).astype(BF16)
+
+
+def left_kernel(pg_ref, b_ref, out_ref):
+    for e in range(2):
+        out_ref[e * 128 : e * 128 + 128, :] = dot(
+            pg_ref[e * 128 : e * 128 + 128, :], b_ref[e * 256 : e * 256 + 256, :]
+        )
+
+
+def triangle_kernel(left_ref, own_ref, other_ref, out_ref):
+    top = iota((8, 8, 256), 1) < 4
+    right = (own_ref[...] + other_ref[...].astype(F32)).reshape(2, 8, 2, 8, 256)
     rows = []
     for q in range(4):
-        upper = jnp.stack([left[q], pltpu.roll(left[q], 4, 1)], axis=1).reshape(16, 8, 256)
-        lower = turn(right[:, q // 2])
-        lower = lower if q & 1 else pltpu.roll(lower, 4, 1)
-        rows.append(jnp.where(top, upper, lower).reshape(128, 256))
-    cols = [v.reshape(16, 8, 128) for v in swap_out(rows)]
+        tiles = []
+        for e in range(2):
+            left = left_ref[e * 128 + q * 32 : e * 128 + q * 32 + 32, :].reshape(4, 8, 256)
+            upper = jnp.stack([left, pltpu.roll(left, 4, 1)], axis=1).reshape(8, 8, 256)
+            lower = turn(right[e, :, q // 2])
+            lower = lower if q & 1 else pltpu.roll(lower, 4, 1)
+            tiles.append(jnp.where(top, upper, lower))
+        rows.append(jnp.stack(tiles, axis=1).reshape(128, 256))
+    cols = [v.reshape(8, 2, 8, 128) for v in swap_out(rows)]
     out_ref[...] = jnp.stack(cols, axis=1).reshape(1024, 128).astype(BF16)
 
 
@@ -393,9 +426,13 @@
     return lax.ppermute(v, "tmpl", [(0, 1), (1, 0)])
 
 
+def exchange_cores(v):
+    return lax.ppermute(v, "row", [(n, n ^ 1) for n in range(16)])
+
+
 def spread_chunks(v, rows):
-    v = lax.all_to_all(v.reshape(128, rows, 128), GROUP, 0, 0, axis_index_groups=[ORDER], tiled=True)
-    return v.reshape(128 * rows, 128)
+    v = lax.all_to_all(v.reshape(64, rows, 128), GROUP, 0, 0, axis_index_groups=ORDER, tiled=True)
+    return v.reshape(64 * rows, 128)
 
 
 def body(
@@ -415,11 +452,11 @@
         update_cotangent, query_weight.T, output_weight, proj_out, key_weight, value_weight, gm, gf,
         template_mask.reshape(1, 2),
     )
-    sides = spread_chunks(sides, 8)
-    prod, a, b = call(
-        product_kernel, [((512, 128), BF16), ((256, 256), BF16), ((256, 256), BF16)], sides
-    )
-    prod = spread_chunks(prod, 4)
+    sides = spread_chunks(sides, 16)
+    a, b_own = call(layout_kernel, [((256, 256), BF16), ((256, 256), BF16)], sides)
+    b_other = exchange_cores(b_own)
+    prod, b = call(product_kernel, [((512, 128), BF16), ((512, 256), BF16)], a, b_own, b_other)
+    prod = spread_chunks(prod, 8)
     stat, weights, along, key, hat_m, rstd_m, out, hat_f, rstd_f = call(
         score_kernel,
         [
@@ -440,11 +477,16 @@
         [((128, 1024), F32), ((128, 1024), F32), ((64, 1024), F32), ((1, 1024), F32), ((64, 1024), F32)],
         normed, x, mask, d_gate, gate_out, side_weights,
     )
-    pg = spread_chunks(pg, 4)
-    (grads,) = call(triangle_kernel, [((1024, 128), BF16)], pg, a, b)
+    pg = spread_chunks(pg, 8)
+    pg, right_own, right_sent = call(
+        right_kernel, [((256, 256), BF16), ((256, 256), F32), ((256, 256), BF16)], pg, a
+    )
+    right_other = exchange_cores(right_sent)
+    (left,) = call(left_kernel, [((256, 256), F32)], pg, b)
+    (grads,) = call(triangle_kernel, [((1024, 128), BF16)], left, right_own, right_other)
     query_other = exchange(query_sum)
     (main_grad,) = call(main_kernel, [((16, 32, 128), BF16)], query_sum, query_other, query_weight.T)
-    grads = spread_chunks(grads, 8)
+    grads = spread_chunks(grads, 16)
     (pair_grad,) = call(
         finish_kernel, [((2, 16, 32, 64), BF16)],
         grads, cg, cp, side_weights, dn, hat, rstd, d_updated, gi_wide,

time: 90.1 us -> 88.4 us (0.981)
  blocking collectives: 57.3 us -> 53.8 us
  waiting for transfers between devices: 11.2 us -> 14.2 us
  starting transfers between devices: 12.2 us -> 11.2 us
    all_to_all x3, blocking collectives: 57.3 us -> 53.8 us  [spread_chunks(): lax.all_to_all(v.reshape(64, rows, 128), GROUP, 0, 0, axis_index_groups=O...]
    ppermute x0 -> x2, waiting for transfers between devices: none -> 2.48 us  [exchange_cores(): return lax.ppermute(v, 'row', [(n, n ^ 1) for n in range(16)])]
    all_to_all x1, starting transfers between devices: 9.25 us -> 7.98 us  [spread_chunks(): lax.all_to_all(v.reshape(64, rows, 128), GROUP, 0, 0, axis_index_groups=O...]
    pallas_call x7 -> x10, Pallas kernels: 5.68 us -> 6.06 us  [call(): pl.pallas_call(kernel, out_shape=shapes, in_specs=[pl.BlockSpec(memory_sp...]
  transfers between devices with their start and end apart: 3 -> 5, of which waited for: 3 -> 5; matrix products, arithmetic and copies ran while one was open for 0% -> 0% of each run, Pallas kernels for 1% -> 2%
where the time goes in v4:
time: 88.4 us; the launch traced here: 88.1 us
  blocking collectives  53.8 us (61%)
  waiting for transfers between devices  14.2 us (16%)
  starting transfers between devices  11.2 us (13%)
  Pallas kernels  8.26 us (9%)
    all_to_all x3, blocking collectives, spread_chunks(): lax.all_to_all(v.reshape(64, rows, 128), GROUP, 0, 0, axis_index_groups=O...  53.8 us
    ppermute x2, waiting for transfers between devices, exchange(): return lax.ppermute(v, 'tmpl', [(0, 1), (1, 0)])  10.5 us
    all_to_all x1, starting transfers between devices, spread_chunks(): lax.all_to_all(v.reshape(64, rows, 128), GROUP, 0, 0, axis_index_groups=O...  7.98 us
    pallas_call x10, Pallas kernels, call(): pl.pallas_call(kernel, out_shape=shapes, in_specs=[pl.BlockSpec(memory_sp...  6.06 us
    ppermute x2, starting transfers between devices, exchange(): return lax.ppermute(v, 'tmpl', [(0, 1), (1, 0)])  2.99 us
    ppermute x2, waiting for transfers between devices, exchange_cores(): return lax.ppermute(v, 'row', [(n, n ^ 1) for n in range(16)])  2.48 us
    pallas_call x1, Pallas kernels, call_copying(): pl.pallas_call(kernel, out_shape=shapes, in_specs=[pl.BlockSpec(memory_sp...  2.19 us
  transfers between devices with their start and end apart: 5, of which 5 were waited for; matrix products, arithmetic and copies ran while one was open for 0% of the time, Pallas kernels for 2%

profile of v4, /device:TPU:6, one launch (start us, length us, event | category | flops | bytes accessed | tf_op | source)
XLA Modules:
  0.0 88.1 jit_solution(14936491861333090081)
XLA Ops:
  0.6 2.2 %shard_map.185 = (bf16[1024,128]{1,0:T(8,128)(2,1)S(1)}, bf16[64,1024]{1,0:T(8,128)(2,1)S(1)}, bf16[64,1024]{1,0:T(8,128)(2,1)S(1)}, f32[64,1024]{1,0:T(8,128)S(...) custom-call(bf16[2,16,32,64]{3,2,1,0:T(8,128)(2,1)} %x_hbm.1, ...), custom_call_target="tpu_custom_call" | custom-call | tf_op jit(solution)/shard_map/pallas_call | solution.py:414
  2.8 23.3 %all_to_all.20 = bf16[64,16,128]{2,1,0:T(8,128)(2,1)S(1)} all-to-all(bf16[64,16,128]{2,1,0:T(8,128)(2,1)S(1)} %bitcast.17), channel_id=1, replica_groups={{96,97,98,99,100,101,102,103,112,113,114,115,116,117,118,119,64,65,66,6..., dimensions={0} | all-to-all | bytes 524288 | tf_op jit(solution)/shard_map/all_to_all | solution.py:434
  26.1 0.3 shard_map.186
  26.4 0.1 collective-permute-start
  26.5 1.3 %collective-permute-done.other_ref = bf16[256,256]{1,0:T(8,128)(2,1)S(1)} collective-permute-done((bf16[256,256]{1,0:T(8,128)(2,1)S(1)}, bf16[256,256]{1,0:T(8,128)(2,1)S(1)}, u32[]{:S(2)}, u32[]{:S(2)}) %collective-permute-start) | collective-permute-done | bytes 131104 | tf_op jit(solution)/shard_map/ppermute | solution.py:430
  27.9 0.4 shard_map.187
  28.3 15.5 %all_to_all.21 = bf16[64,8,128]{2,1,0:T(8,128)(2,1)S(1)} all-to-all(bf16[64,8,128]{2,1,0:T(8,128)(2,1)S(1)} %bitcast.19), channel_id=1, replica_groups={{96,97,98,99,100,101,102,103,112,113,114,115,116,117,118,119,64,65,66,6..., dimensions={0} | all-to-all | bytes 262144 | tf_op jit(solution)/shard_map/all_to_all | solution.py:434
  43.7 0.6 shard_map.188
  44.4 1.5 %collective-permute-start.1 = (f32[2,4,512]{2,1,0:T(4,128)S(1)}, f32[2,4,512]{2,1,0:T(4,128)S(1)}, u32[]{:S(2)}, u32[]{:S(2)}) collective-permute-start(f32[2,4,512]{2,1,0:T(4,128)S(1)} %get-tuple-element.57.mine_ref), channel_id=1, source_target_pairs={{0,128},{128,0},{1,129},{129,1},{2,130},{130,2},{3,131},{131,3},{4... | collective-permute-start | bytes 49160 | tf_op jit(solution)/shard_map/ppermute | solution.py:426
  45.9 3.8 %collective-permute-done.1.other_ref = f32[2,4,512]{2,1,0:T(4,128)S(1)} collective-permute-done((f32[2,4,512]{2,1,0:T(4,128)S(1)}, f32[2,4,512]{2,1,0:T(4,128)S(1)}, u32[]{:S(2)}, u32[]{:S(2)}) %collective-permute-start.1) | collective-permute-done | bytes 16416 | tf_op jit(solution)/shard_map/ppermute | solution.py:426
  49.7 0.6 shard_map.189
  50.3 15.1 %all_to_all.22 = bf16[64,8,128]{2,1,0:T(8,128)(2,1)S(1)} all-to-all(bf16[64,8,128]{2,1,0:T(8,128)(2,1)S(1)} %bitcast.18), channel_id=1, replica_groups={{96,97,98,99,100,101,102,103,112,113,114,115,116,117,118,119,64,65,66,6..., dimensions={0} | all-to-all | bytes 262144 | tf_op jit(solution)/shard_map/all_to_all | solution.py:434
  65.3 0.4 shard_map.190
  65.7 0.1 collective-permute-start.2
  65.8 0.2 shard_map.191.left_ref
  66.0 1.1 %collective-permute-done.2.other_ref = bf16[256,256]{1,0:T(8,128)(2,1)S(1)} collective-permute-done((bf16[256,256]{1,0:T(8,128)(2,1)S(1)}, bf16[256,256]{1,0:T(8,128)(2,1)S(1)}, u32[]{:S(2)}, u32[]{:S(2)}) %collective-permute-start.2) | collective-permute-done | bytes 131104 | tf_op jit(solution)/shard_map/ppermute | solution.py:430
  67.2 1.0 %shard_map.192 = bf16[1024,128]{1,0:T(8,128)(2,1)} custom-call(f32[256,256]{1,0:T(8,128)S(1)} %shard_map.191.left_ref, f32[256,256]{1,0:T(8,128)S(1)} %get-tuple-element.66.own_ref, bf16[256,256]{1,0:T(8,128)(2,1)S(1)} %collective-permute-done.2.other_ref), custom_call_target="tpu_custom_call" | custom-call | bytes 655360 | tf_op jit(solution)/shard_map/pallas_call | solution.py:401
  68.2 0.0 copy-start.1
  68.2 8.0 %all-to-all-start.3 = ((bf16[64,16,128]{2,1,0:T(8,128)(2,1)}), bf16[64,16,128]{2,1,0:T(8,128)(2,1)S(1)}, u32[]{:S(2)}, u32[]{:S(2)}) async-start(bf16[64,16,128]{2,1,0:T(8,128)(2,1)} %bitcast.11), calls=%async_computation.3 | async-start | bytes 524288 | tf_op jit(solution)/shard_map/all_to_all | solution.py:434
  76.2 1.5 %collective-permute-start.3 = (f32[64,512]{1,0:T(8,128)S(1)}, f32[64,512]{1,0:T(8,128)S(1)}, u32[]{:S(2)}, u32[]{:S(2)}) collective-permute-start(f32[64,512]{1,0:T(8,128)S(1)} %get-tuple-element.79.mine_ref), channel_id=1, source_target_pairs={{0,128},{128,0},{1,129},{129,1},{2,130},{130,2},{3,131},{131,3},{4... | collective-permute-start | bytes 393224 | tf_op jit(solution)/shard_map/ppermute | solution.py:426
  77.7 0.0 copy-done.1
  77.7 0.0 copy-start
  77.7 0.4 shard_map.193
  78.1 6.7 %collective-permute-done.3.other_ref = f32[64,512]{1,0:T(8,128)S(1)} collective-permute-done((f32[64,512]{1,0:T(8,128)S(1)}, f32[64,512]{1,0:T(8,128)S(1)}, u32[]{:S(2)}, u32[]{:S(2)}) %collective-permute-start.3) | collective-permute-done | bytes 131104 | tf_op jit(solution)/shard_map/ppermute | solution.py:426
  84.8 0.0 copy-done
  84.8 0.9 shard_map.195
  85.6 1.2 %all-to-all-done.3 = bf16[64,16,128]{2,1,0:T(8,128)(2,1)S(1)} async-done(((bf16[64,16,128]{2,1,0:T(8,128)(2,1)}), bf16[64,16,128]{2,1,0:T(8,128)(2,1)S(1)}, u32[]{:S(2)}, u32[]{:S(2)}) %all-to-all-start.3) | async-done | bytes 262176 | tf_op jit(solution)/shard_map/all_to_all | solution.py:434
  86.8 1.3 %shard_map.194 = bf16[2,16,32,64]{3,2,1,0:T(8,128)(2,1)} custom-call(bf16[1024,128]{1,0:T(8,128)(2,1)S(1)} %bitcast.13, f32[128,1024]{1,0:T(8,128)S(1)} %get-tuple-element.72.cg_ref, f32[128,1024]{1,0:T(8,128)S(1)} %get-tuple-element.73.cp_ref, bf16[64,256]{1,0:T(8,128)(2,1)S(1)} %get-tuple-element.71.sides_ref, f32[64,1024]{1,0:T(8,128)S(1)} %get-tuple-element.74.dn_ref, ...), custom_call_target="tpu_custom_call" | custom-call | bytes 2166784 | tf_op jit(solution)/shard_map/pallas_call | solution.py:401
Async XLA Ops:
  26.4 1.4 %collective-permute-start = (bf16[256,256]{1,0:T(8,128)(2,1)S(1)}, bf16[256,256]{1,0:T(8,128)(2,1)S(1)}, u32[]{:S(2)}, u32[]{:S(2)}) collective-permute-start(bf16[256,256]{1,0:T(8,128)(2,1)S(1)} %get-tuple-element.47.own_ref), channel_id=1, source_target_pairs={{0,8},{8,0},{16,24},{24,16},{32,40},{40,32},{48,56},{56,48},{64,72... | collective-permute-start | bytes 393224 | tf_op jit(solution)/shard_map/ppermute | solution.py:430
  44.4 5.3 %collective-permute-start.1 = (f32[2,4,512]{2,1,0:T(4,128)S(1)}, f32[2,4,512]{2,1,0:T(4,128)S(1)}, u32[]{:S(2)}, u32[]{:S(2)}) collective-permute-start(f32[2,4,512]{2,1,0:T(4,128)S(1)} %get-tuple-element.57.mine_ref), channel_id=1, source_target_pairs={{0,128},{128,0},{1,129},{129,1},{2,130},{130,2},{3,131},{131,3},{4... | collective-permute-start | bytes 49160 | tf_op jit(solution)/shard_map/ppermute | solution.py:426
  65.7 1.4 %collective-permute-start.2 = (bf16[256,256]{1,0:T(8,128)(2,1)S(1)}, bf16[256,256]{1,0:T(8,128)(2,1)S(1)}, u32[]{:S(2)}, u32[]{:S(2)}) collective-permute-start(bf16[256,256]{1,0:T(8,128)(2,1)S(1)} %get-tuple-element.67), channel_id=1, source_target_pairs={{0,8},{8,0},{16,24},{24,16},{32,40},{40,32},{48,56},{56,48},{64,72... | collective-permute-start | bytes 393224 | tf_op jit(solution)/shard_map/ppermute | solution.py:430
  68.2 9.5 %copy-start.1 = (bf16[64,64]{1,0:T(8,128)(2,1)S(1)}, bf16[64,64]{1,0:T(8,128)(2,1)}, u32[]{:S(2)}) copy-start(bf16[64,64]{1,0:T(8,128)(2,1)} %go_ref.1) | copy-start | bytes 24580
  68.2 18.6 %all-to-all-start.3 = ((bf16[64,16,128]{2,1,0:T(8,128)(2,1)}), bf16[64,16,128]{2,1,0:T(8,128)(2,1)S(1)}, u32[]{:S(2)}, u32[]{:S(2)}) async-start(bf16[64,16,128]{2,1,0:T(8,128)(2,1)} %bitcast.11), calls=%async_computation.3 | async-start | bytes 524288 | tf_op jit(solution)/shard_map/all_to_all | solution.py:434
  76.2 8.6 %collective-permute-start.3 = (f32[64,512]{1,0:T(8,128)S(1)}, f32[64,512]{1,0:T(8,128)S(1)}, u32[]{:S(2)}, u32[]{:S(2)}) collective-permute-start(f32[64,512]{1,0:T(8,128)S(1)} %get-tuple-element.79.mine_ref), channel_id=1, source_target_pairs={{0,128},{128,0},{1,129},{129,1},{2,130},{130,2},{3,131},{131,3},{4... | collective-permute-start | bytes 393224 | tf_op jit(solution)/shard_map/ppermute | solution.py:426
  77.7 7.1 %copy-start = (bf16[128,64]{0,1:T(8,128)(2,1)S(1)}, bf16[128,64]{0,1:T(8,128)(2,1)}, u32[]{:S(2)}) copy-start(bf16[128,64]{0,1:T(8,128)(2,1)} %param.34) | copy-start | bytes 49156

commit v5 on v4

--- a/solution.py
+++ b/solution.py
@@ -16,6 +16,7 @@
 SCALE = 1.0 / math.sqrt(HEAD_DIM)
 GROUP = ("row", "col")
 TURN = 6
+LATER = 11
 SIDE_BLOCKS = [(s, side, r) for s in range(2) for side in range(2) for r in range(4)]
 PIXEL_ROWS = [4 * q + r for r in range(4) for q in range(4)]
 ORDER = [[(z ^ TURN) * 16 + core * 8 + col for z in range(8) for col in range(8)] for core in range(2)]
@@ -162,18 +163,16 @@
 
 
 def front_kernel(
-    x_hbm, mask_hbm, gi_hbm, pa_hbm, ga_hbm, pb_hbm, gb_hbm, go_hbm, main_hbm, cot_hbm, wq_hbm, wo_hbm,
-    po_hbm, kw_hbm, vw_hbm, gm_hbm, gf_hbm, present_hbm,
-    out_ref, x_out, n_out, gat_out, q_out, g_out, wide_out_ref, kv_out, gm_out, gf_out, gi_out, absent_out, sides_out, mask_out,
-    x_ref, mask_ref, gi_ref, pa_ref, ga_ref, pb_ref, gb_ref, go_ref, main_ref, cot_ref, wq_ref, wo_ref,
-    po_ref, kw_ref, vw_ref, gm_ref, gf_ref, present_ref, tiles_ref, sems,
-):
+    x_hbm, mask_hbm, gi_hbm, pa_hbm, ga_hbm, pb_hbm, gb_hbm, *refs
+):
+    later, refs = refs[:LATER], refs[LATER:]
+    out_ref, x_out, n_out, gi_out, sides_out, mask_out = refs[:6]
+    later_out, refs = refs[6 : 6 + LATER], refs[6 + LATER :]
+    x_ref, mask_ref, gi_ref, pa_ref, ga_ref, pb_ref, gb_ref, tiles_ref, sems = refs
     pairs = [
         (x_hbm, x_ref), (gi_hbm, gi_ref), (pa_hbm, pa_ref), (ga_hbm, ga_ref), (pb_hbm, pb_ref),
-        (gb_hbm, gb_ref), (mask_hbm, mask_ref), (go_hbm, go_ref), (main_hbm, main_ref), (cot_hbm, cot_ref),
-        (wq_hbm, wq_ref), (wo_hbm, wo_ref), (po_hbm, po_ref), (kw_hbm, kw_ref), (vw_hbm, vw_ref),
-        (gm_hbm, gm_ref), (gf_hbm, gf_ref), (present_hbm, present_ref),
-    ]
+        (gb_hbm, gb_ref), (mask_hbm, mask_ref),
+    ] + list(zip(later, later_out))
     copies = [pltpu.make_async_copy(a, b, sems.at[n]) for n, (a, b) in enumerate(pairs)]
     for copy in copies:
         copy.start()
@@ -190,6 +189,7 @@
     normed = (hat * gi).astype(BF16)
     x_out[...] = x.astype(BF16)
     n_out[...] = normed
+    gi_out[...] = jnp.broadcast_to(gi, (64, 128))
     both_sides = dot_tn(weights, normed)
     both_sides = mask * jax.nn.sigmoid(both_sides[:128]) * both_sides[128:]
     for s, side, r in SIDE_BLOCKS:
@@ -197,10 +197,15 @@
             side * 64 : side * 64 + 64, s * 512 + r * 128 : s * 512 + r * 128 + 128
         ]
     out_ref[...] = tiles_ref[...].astype(BF16)
-    gi_out[...] = jnp.broadcast_to(gi, (64, 128))
     for copy in copies[7:]:
         copy.wait()
-    gat_out[...] = jax.nn.sigmoid(dot_tn(go_ref[...], normed))
+
+
+def side_kernel(
+    n_ref, go_ref, main_ref, cot_ref, wq_ref, wo_ref, po_ref, kw_ref, vw_ref, gm_ref, gf_ref, present_ref,
+    gat_out, q_out, g_out, wide_out_ref, kv_out, gm_out, gf_out, absent_out,
+):
+    gat_out[...] = jax.nn.sigmoid(dot_tn(go_ref[...], n_ref[...]))
     q_out[...] = dot_nt(wq_ref[...], jnp.concatenate([main_ref[i] for i in PIXEL_ROWS], axis=0)).astype(BF16)
     g_out[...] = dot_nt(wo_ref[...], jnp.concatenate([cot_ref[i] for i in PIXEL_ROWS], axis=0))
     wide_out_ref[...] = wide_out(po_ref[...])
@@ -292,8 +297,8 @@
 
 def grad_kernel(
     gat_ref, q_ref, g_ref, key_ref, w_ref, along_ref, mine_ref, other_ref,
-    gm_ref, gf_ref, wide_ref, kv_ref, hat_m_ref, rstd_m_ref, out_ref, hat_f_ref, rstd_f_ref,
-    pg_out, qsum_out, du_out, dgate_out,
+    gm_ref, gf_ref, wide_ref, kv_ref, hat_m_ref, rstd_m_ref, hat_f_ref, rstd_f_ref,
+    pg_out, qsum_out, du_out,
 ):
     share = jax.nn.sigmoid(mine_ref[0] - other_ref[0])
     average = share * mine_ref[1] + jax.nn.sigmoid(other_ref[0] - mine_ref[0]) * other_ref[1]
@@ -308,9 +313,7 @@
     d_updated = norm_grad_c(d_final, tile_lanes(gf_ref[...], 8), hat_f_ref[...], rstd_f_ref[...])
     gat = gat_ref[...]
     du_out[...] = d_updated
-    d_out = d_updated * gat
-    dgate_out[...] = (d_out * out_ref[...] * (1.0 - gat)).astype(BF16)
-    d_mixed = dot_tn(wide_ref[...], c_to_rc(d_out.astype(BF16)))
+    d_mixed = dot_tn(wide_ref[...], c_to_rc((d_updated * gat).astype(BF16)))
     pg = norm_grad_cr(
         d_mixed, tile_lanes(gm_ref[...], 2), hat_m_ref[...], spread_cr(rstd_m_ref[...])
     ).astype(BF16)
@@ -319,7 +322,7 @@
 
 
 def coef_kernel(
-    n_ref, x_ref, mask_ref, dgate_ref, go_ref, sides_ref, cg_out, cp_out, hat_out, rstd_out, dn_out
+    n_ref, x_ref, mask_ref, gat_ref, out_ref, du_ref, go_ref, sides_ref, cg_out, cp_out, hat_out, rstd_out, dn_out
 ):
     both_sides = dot_tn(sides_ref[...], n_ref[...])
     gate = jax.nn.sigmoid(both_sides[:128])
@@ -327,7 +330,9 @@
     cp_out[...] = scaled
     cg_out[...] = scaled * (1.0 - gate) * both_sides[128:]
     hat_out[...], rstd_out[...] = hat_c(x_ref[...].astype(F32))
-    dn_out[...] = dot(go_ref[...], dgate_ref[...])
+    gat = gat_ref[...]
+    d_gate = (du_ref[...] * gat * out_ref[...] * (1.0 - gat)).astype(BF16)
+    dn_out[...] = dot(go_ref[...], d_gate)
 
 
 def right_kernel(pg_ref, a_ref, pg_out, own_out, sent_out):
@@ -409,14 +414,16 @@
     )(*args)
 
 
-def call_copying(kernel, outs, *args):
+def call_copying(kernel, outs, now, later):
     shapes = [jax.ShapeDtypeStruct(s, t) for s, t in outs]
+    shapes += [jax.ShapeDtypeStruct(a.shape, a.dtype) for a in later]
+    args = now + later
     return pl.pallas_call(
         kernel,
         out_shape=shapes,
         in_specs=[pl.BlockSpec(memory_space=pl.ANY)] * len(args),
         out_specs=[pl.BlockSpec(memory_space=pltpu.VMEM)] * len(shapes),
-        scratch_shapes=[pltpu.VMEM(a.shape, a.dtype) for a in args]
+        scratch_shapes=[pltpu.VMEM(a.shape, a.dtype) for a in now]
         + [pltpu.VMEM((1024, 128), F32), pltpu.SemaphoreType.DMA((len(args),))],
         compiler_params=pltpu.CompilerParams(vmem_limit_bytes=24 * 1024 * 1024),
     )(*[pltpu.with_memory_space_constraint(a, pltpu.HBM) for a in args])
@@ -441,20 +448,33 @@
     key_weight, value_weight, query_weight, output_weight,
 ):
     gi, gm, gf = gain_in.reshape(1, 64), gain_mid.reshape(1, 64), gain_final.reshape(1, 64)
-    sides, x, normed, gat, query, grad_out, wide, kv, gm_wide, gf_wide, gi_wide, absent, side_weights, mask = call_copying(
+    sides, x, normed, gi_wide, side_weights, mask, *later = call_copying(
         front_kernel,
         [
-            ((1024, 128), BF16), ((64, 1024), BF16), ((64, 1024), BF16), ((64, 1024), F32),
-            ((64, 512), BF16), ((64, 512), F32), ((256, 256), BF16), ((64, 128), BF16),
-            ((256, 128), F32), ((64, 128), F32), ((64, 128), F32), ((8, 1024), F32), ((64, 256), BF16), ((8, 1024), F32),
+            ((1024, 128), BF16), ((64, 1024), BF16), ((64, 1024), BF16), ((64, 128), F32), ((64, 256), BF16),
+            ((8, 1024), F32),
         ],
-        template_pair, pair_mask, gi, proj_a, gate_a, proj_b, gate_b, gate_out, main_pair,
-        update_cotangent, query_weight.T, output_weight, proj_out, key_weight, value_weight, gm, gf,
-        template_mask.reshape(1, 2),
+        [template_pair, pair_mask, gi, proj_a, gate_a, proj_b, gate_b],
+        [
+            gate_out, main_pair, update_cotangent, query_weight.T, output_weight, proj_out, key_weight,
+            value_weight, gm, gf, template_mask.reshape(1, 2),
+        ],
     )
     sides = spread_chunks(sides, 16)
     a, b_own = call(layout_kernel, [((256, 256), BF16), ((256, 256), BF16)], sides)
     b_other = exchange_cores(b_own)
+    b_own, normed, later = lax.optimization_barrier((b_own, normed, later))
+    side = call(
+        side_kernel,
+        [
+            ((64, 1024), F32), ((64, 512), BF16), ((64, 512), F32), ((256, 256), BF16), ((64, 128), BF16),
+            ((256, 128), F32), ((64, 128), F32), ((8, 1024), F32),
+        ],
+        normed, *later,
+    )
+    b_other, (gat, query, grad_out, wide, kv, gm_wide, gf_wide, absent) = lax.optimization_barrier(
+        (b_other, side)
+    )
     prod, b = call(product_kernel, [((512, 128), BF16), ((512, 256), BF16)], a, b_own, b_other)
     prod = spread_chunks(prod, 8)
     stat, weights, along, key, hat_m, rstd_m, out, hat_f, rstd_f = call(
@@ -466,16 +486,16 @@
         x, prod, gat, query, grad_out, absent, gm_wide, gf_wide, wide, kv,
     )
     other = exchange(stat)
-    pg, query_sum, d_updated, d_gate = call(
+    pg, query_sum, d_updated = call(
         grad_kernel,
-        [((512, 128), BF16), ((64, 512), F32), ((64, 1024), F32), ((64, 1024), BF16)],
+        [((512, 128), BF16), ((64, 512), F32), ((64, 1024), F32)],
         gat, query, grad_out, key, weights, along, stat, other,
-        gm_wide, gf_wide, wide, kv, hat_m, rstd_m, out, hat_f, rstd_f,
+        gm_wide, gf_wide, wide, kv, hat_m, rstd_m, hat_f, rstd_f,
     )
     cg, cp, hat, rstd, dn = call(
         coef_kernel,
         [((128, 1024), F32), ((128, 1024), F32), ((64, 1024), F32), ((1, 1024), F32), ((64, 1024), F32)],
-        normed, x, mask, d_gate, gate_out, side_weights,
+        normed, x, mask, gat, out, d_updated, later[0], side_weights,
     )
     pg = spread_chunks(pg, 8)
     pg, right_own, right_sent = call(
@@ -485,7 +505,7 @@
     (left,) = call(left_kernel, [((256, 256), F32)], pg, b)
     (grads,) = call(triangle_kernel, [((1024, 128), BF16)], left, right_own, right_other)
     query_other = exchange(query_sum)
-    (main_grad,) = call(main_kernel, [((16, 32, 128), BF16)], query_sum, query_other, query_weight.T)
+    (main_grad,) = call(main_kernel, [((16, 32, 128), BF16)], query_sum, query_other, later[3])
     grads = spread_chunks(grads, 16)
     (pair_grad,) = call(
         finish_kernel, [((2, 16, 32, 64), BF16)],

time: 88.4 us -> 87.9 us (level)
    pallas_call x10 -> x11, Pallas kernels: 6.06 us -> 6.38 us  [call(): pl.pallas_call(kernel, out_shape=shapes, in_specs=[pl.BlockSpec(memory_sp...]
where the time goes in v5:
time: 87.9 us; the launch traced here: 87.6 us
  blocking collectives  53.8 us (61%)
  waiting for transfers between devices  13.8 us (16%)
  starting transfers between devices  11 us (13%)
  Pallas kernels  8.22 us (9%)
    all_to_all x3, blocking collectives, spread_chunks(): lax.all_to_all(v.reshape(64, rows, 128), GROUP, 0, 0, axis_index_groups=O...  53.8 us
    ppermute x2, waiting for transfers between devices, exchange(): return lax.ppermute(v, 'tmpl', [(0, 1), (1, 0)])  10.5 us
    all_to_all x1, starting transfers between devices, spread_chunks(): lax.all_to_all(v.reshape(64, rows, 128), GROUP, 0, 0, axis_index_groups=O...  7.84 us
    pallas_call x11, Pallas kernels, call(): pl.pallas_call(kernel, out_shape=shapes, in_specs=[pl.BlockSpec(memory_sp...  6.38 us
    ppermute x2, starting transfers between devices, exchange(): return lax.ppermute(v, 'tmpl', [(0, 1), (1, 0)])  2.99 us
    ppermute x2, waiting for transfers between devices, exchange_cores(): return lax.ppermute(v, 'row', [(n, n ^ 1) for n in range(16)])  2.14 us
    pallas_call x1, Pallas kernels, call_copying(): pl.pallas_call(kernel, out_shape=shapes, in_specs=[pl.BlockSpec(memory_sp...  1.85 us
  transfers between devices with their start and end apart: 5, of which 5 were waited for; matrix products, arithmetic and copies ran while one was open for 0% of the time, Pallas kernels for 2%

profile of v5, /device:TPU:6, one launch (start us, length us, event | category | flops | bytes accessed | tf_op | source)
XLA Modules:
  0.0 87.6 jit_solution(10214774561784891378)
XLA Ops:
  0.6 1.8 %shard_map.185 = (bf16[1024,128]{1,0:T(8,128)(2,1)S(1)}, bf16[64,1024]{1,0:T(8,128)(2,1)S(1)}, bf16[64,1024]{1,0:T(8,128)(2,1)S(1)}, f32[64,128]{1,0:T(8,128)S(1...) custom-call(bf16[2,16,32,64]{3,2,1,0:T(8,128)(2,1)} %x_hbm.1, ...), custom_call_target="tpu_custom_call" | custom-call | tf_op jit(solution)/shard_map/pallas_call | solution.py:421
  2.5 23.3 %all_to_all.20 = bf16[64,16,128]{2,1,0:T(8,128)(2,1)S(1)} all-to-all(bf16[64,16,128]{2,1,0:T(8,128)(2,1)S(1)} %bitcast.17), channel_id=1, replica_groups={{96,97,98,99,100,101,102,103,112,113,114,115,116,117,118,119,64,65,66,6..., dimensions={0} | all-to-all | bytes 524288 | tf_op jit(solution)/shard_map/all_to_all | solution.py:441
  25.8 0.3 shard_map.186
  26.1 0.1 collective-permute-start
  26.2 0.3 shard_map.187
  26.5 1.0 %collective-permute-done.other_ref = bf16[256,256]{1,0:T(8,128)(2,1)S(1)} collective-permute-done((bf16[256,256]{1,0:T(8,128)(2,1)S(1)}, bf16[256,256]{1,0:T(8,128)(2,1)S(1)}, u32[]{:S(2)}, u32[]{:S(2)}) %collective-permute-start) | collective-permute-done | bytes 131104 | tf_op jit(solution)/shard_map/ppermute | solution.py:437
  27.5 0.4 shard_map.188
  27.9 15.5 %all_to_all.21 = bf16[64,8,128]{2,1,0:T(8,128)(2,1)S(1)} all-to-all(bf16[64,8,128]{2,1,0:T(8,128)(2,1)S(1)} %bitcast.19), channel_id=1, replica_groups={{96,97,98,99,100,101,102,103,112,113,114,115,116,117,118,119,64,65,66,6..., dimensions={0} | all-to-all | bytes 262144 | tf_op jit(solution)/shard_map/all_to_all | solution.py:441
  43.4 0.6 shard_map.189
  44.0 1.5 %collective-permute-start.1 = (f32[2,4,512]{2,1,0:T(4,128)S(1)}, f32[2,4,512]{2,1,0:T(4,128)S(1)}, u32[]{:S(2)}, u32[]{:S(2)}) collective-permute-start(f32[2,4,512]{2,1,0:T(4,128)S(1)} %get-tuple-element.123.mine_ref), channel_id=1, source_target_pairs={{0,128},{128,0},{1,129},{129,1},{2,130},{130,2},{3,131},{131,3},{4... | collective-permute-start | bytes 49160 | tf_op jit(solution)/shard_map/ppermute | solution.py:433
  45.5 3.8 %collective-permute-done.1.other_ref = f32[2,4,512]{2,1,0:T(4,128)S(1)} collective-permute-done((f32[2,4,512]{2,1,0:T(4,128)S(1)}, f32[2,4,512]{2,1,0:T(4,128)S(1)}, u32[]{:S(2)}, u32[]{:S(2)}) %collective-permute-start.1) | collective-permute-done | bytes 16416 | tf_op jit(solution)/shard_map/ppermute | solution.py:433
  49.4 0.5 shard_map.190
  49.9 15.1 %all_to_all.22 = bf16[64,8,128]{2,1,0:T(8,128)(2,1)S(1)} all-to-all(bf16[64,8,128]{2,1,0:T(8,128)(2,1)S(1)} %bitcast.18), channel_id=1, replica_groups={{96,97,98,99,100,101,102,103,112,113,114,115,116,117,118,119,64,65,66,6..., dimensions={0} | all-to-all | bytes 262144 | tf_op jit(solution)/shard_map/all_to_all | solution.py:441
  65.0 0.4 shard_map.191
  65.4 0.1 collective-permute-start.2
  65.5 0.2 shard_map.192.left_ref
  65.7 1.1 %collective-permute-done.2.other_ref = bf16[256,256]{1,0:T(8,128)(2,1)S(1)} collective-permute-done((bf16[256,256]{1,0:T(8,128)(2,1)S(1)}, bf16[256,256]{1,0:T(8,128)(2,1)S(1)}, u32[]{:S(2)}, u32[]{:S(2)}) %collective-permute-start.2) | collective-permute-done | bytes 131104 | tf_op jit(solution)/shard_map/ppermute | solution.py:437
  66.8 1.0 %shard_map.193 = bf16[1024,128]{1,0:T(8,128)(2,1)} custom-call(f32[256,256]{1,0:T(8,128)S(1)} %shard_map.192.left_ref, f32[256,256]{1,0:T(8,128)S(1)} %get-tuple-element.131.own_ref, bf16[256,256]{1,0:T(8,128)(2,1)S(1)} %collective-permute-done.2.other_ref), custom_call_target="tpu_custom_call" | custom-call | bytes 655360 | tf_op jit(solution)/shard_map/pallas_call | solution.py:406
  67.8 7.8 %all-to-all-start.3 = ((bf16[64,16,128]{2,1,0:T(8,128)(2,1)}), bf16[64,16,128]{2,1,0:T(8,128)(2,1)S(1)}, u32[]{:S(2)}, u32[]{:S(2)}) async-start(bf16[64,16,128]{2,1,0:T(8,128)(2,1)} %bitcast.11), calls=%async_computation.3 | async-start | bytes 524288 | tf_op jit(solution)/shard_map/all_to_all | solution.py:441
  75.7 1.5 %collective-permute-start.3 = (f32[64,512]{1,0:T(8,128)S(1)}, f32[64,512]{1,0:T(8,128)S(1)}, u32[]{:S(2)}, u32[]{:S(2)}) collective-permute-start(f32[64,512]{1,0:T(8,128)S(1)} %get-tuple-element.143.mine_ref), channel_id=1, source_target_pairs={{0,128},{128,0},{1,129},{129,1},{2,130},{130,2},{3,131},{131,3},{4... | collective-permute-start | bytes 393224 | tf_op jit(solution)/shard_map/ppermute | solution.py:433
  77.2 0.4 shard_map.194
  77.6 6.7 %collective-permute-done.3.other_ref = f32[64,512]{1,0:T(8,128)S(1)} collective-permute-done((f32[64,512]{1,0:T(8,128)S(1)}, f32[64,512]{1,0:T(8,128)S(1)}, u32[]{:S(2)}, u32[]{:S(2)}) %collective-permute-start.3) | collective-permute-done | bytes 131104 | tf_op jit(solution)/shard_map/ppermute | solution.py:433
  84.3 0.9 shard_map.196
  85.1 1.2 %all-to-all-done.3 = bf16[64,16,128]{2,1,0:T(8,128)(2,1)S(1)} async-done(((bf16[64,16,128]{2,1,0:T(8,128)(2,1)}), bf16[64,16,128]{2,1,0:T(8,128)(2,1)S(1)}, u32[]{:S(2)}, u32[]{:S(2)}) %all-to-all-start.3) | async-done | bytes 262176 | tf_op jit(solution)/shard_map/all_to_all | solution.py:441
  86.3 1.3 %shard_map.195 = bf16[2,16,32,64]{3,2,1,0:T(8,128)(2,1)} custom-call(bf16[1024,128]{1,0:T(8,128)(2,1)S(1)} %bitcast.13, f32[128,1024]{1,0:T(8,128)S(1)} %get-tuple-element.137.cg_ref, f32[128,1024]{1,0:T(8,128)S(1)} %get-tuple-element.138.cp_ref, bf16[64,256]{1,0:T(8,128)(2,1)S(1)} %get-tuple-element.136.sides_ref, ...), custom_call_target="tpu_custom_call" | custom-call | bytes 2166784 | tf_op jit(solution)/shard_map/pallas_call | solution.py:406
Async XLA Ops:
  26.1 1.4 %collective-permute-start = (bf16[256,256]{1,0:T(8,128)(2,1)S(1)}, bf16[256,256]{1,0:T(8,128)(2,1)S(1)}, u32[]{:S(2)}, u32[]{:S(2)}) collective-permute-start(bf16[256,256]{1,0:T(8,128)(2,1)S(1)} %get-tuple-element.112.own_ref), channel_id=1, source_target_pairs={{0,8},{8,0},{16,24},{24,16},{32,40},{40,32},{48,56},{56,48},{64,72... | collective-permute-start | bytes 393224 | tf_op jit(solution)/shard_map/ppermute | solution.py:437
  44.0 5.3 %collective-permute-start.1 = (f32[2,4,512]{2,1,0:T(4,128)S(1)}, f32[2,4,512]{2,1,0:T(4,128)S(1)}, u32[]{:S(2)}, u32[]{:S(2)}) collective-permute-start(f32[2,4,512]{2,1,0:T(4,128)S(1)} %get-tuple-element.123.mine_ref), channel_id=1, source_target_pairs={{0,128},{128,0},{1,129},{129,1},{2,130},{130,2},{3,131},{131,3},{4... | collective-permute-start | bytes 49160 | tf_op jit(solution)/shard_map/ppermute | solution.py:433
  65.4 1.4 %collective-permute-start.2 = (bf16[256,256]{1,0:T(8,128)(2,1)S(1)}, bf16[256,256]{1,0:T(8,128)(2,1)S(1)}, u32[]{:S(2)}, u32[]{:S(2)}) collective-permute-start(bf16[256,256]{1,0:T(8,128)(2,1)S(1)} %get-tuple-element.132), channel_id=1, source_target_pairs={{0,8},{8,0},{16,24},{24,16},{32,40},{40,32},{48,56},{56,48},{64,72... | collective-permute-start | bytes 393224 | tf_op jit(solution)/shard_map/ppermute | solution.py:437
  67.8 18.5 %all-to-all-start.3 = ((bf16[64,16,128]{2,1,0:T(8,128)(2,1)}), bf16[64,16,128]{2,1,0:T(8,128)(2,1)S(1)}, u32[]{:S(2)}, u32[]{:S(2)}) async-start(bf16[64,16,128]{2,1,0:T(8,128)(2,1)} %bitcast.11), calls=%async_computation.3 | async-start | bytes 524288 | tf_op jit(solution)/shard_map/all_to_all | solution.py:441
  75.7 8.6 %collective-permute-start.3 = (f32[64,512]{1,0:T(8,128)S(1)}, f32[64,512]{1,0:T(8,128)S(1)}, u32[]{:S(2)}, u32[]{:S(2)}) collective-permute-start(f32[64,512]{1,0:T(8,128)S(1)} %get-tuple-element.143.mine_ref), channel_id=1, source_target_pairs={{0,128},{128,0},{1,129},{129,1},{2,130},{130,2},{3,131},{131,3},{4... | collective-permute-start | bytes 393224 | tf_op jit(solution)/shard_map/ppermute | solution.py:433

commit v6 on v5

--- a/solution.py
+++ b/solution.py
@@ -373,7 +373,8 @@
 
 
 def finish_kernel(
-    lr_ref, cg_ref, cp_ref, sides_ref, dn_ref, hat_ref, rstd_ref, du_ref, gain_ref, out_ref, tiles_ref
+    lr_ref, cg_ref, cp_ref, sides_ref, dn_ref, hat_ref, rstd_ref, du_ref, gain_ref,
+    mine_ref, other_ref, wq_ref, out_ref, main_out, tiles_ref,
 ):
     tiles_ref[...] = lr_ref[...].astype(F32)
     blocks = [tiles_ref[pl.ds(s * 512 + side * 4 + r, 64, stride=8), :] for s, side, r in SIDE_BLOCKS]
@@ -391,13 +392,10 @@
     for s in range(2):
         for n, i in enumerate(PIXEL_ROWS):
             out_ref[s, i] = out[s * 512 + n * 32 : s * 512 + n * 32 + 32]
-
-
-def main_kernel(mine_ref, other_ref, wq_ref, out_ref):
     grad = (mine_ref[...] + other_ref[...]).astype(BF16)
     out = dot_tn(grad, wq_ref[...]).astype(BF16)
     for n, i in enumerate(PIXEL_ROWS):
-        out_ref[i] = out[n * 32 : n * 32 + 32]
+        main_out[i] = out[n * 32 : n * 32 + 32]
 
 
 def call(kernel, outs, *args, scratch=()):
@@ -492,24 +490,26 @@
         gat, query, grad_out, key, weights, along, stat, other,
         gm_wide, gf_wide, wide, kv, hat_m, rstd_m, hat_f, rstd_f,
     )
+    pg = spread_chunks(pg, 8)
+    pg, right_own, right_sent = call(
+        right_kernel, [((256, 256), BF16), ((256, 256), F32), ((256, 256), BF16)], pg, a
+    )
+    right_other = exchange_cores(right_sent)
+    right_own, normed, gate_weight = lax.optimization_barrier((right_own, normed, later[0]))
     cg, cp, hat, rstd, dn = call(
         coef_kernel,
         [((128, 1024), F32), ((128, 1024), F32), ((64, 1024), F32), ((1, 1024), F32), ((64, 1024), F32)],
-        normed, x, mask, gat, out, d_updated, later[0], side_weights,
-    )
-    pg = spread_chunks(pg, 8)
-    pg, right_own, right_sent = call(
-        right_kernel, [((256, 256), BF16), ((256, 256), F32), ((256, 256), BF16)], pg, a
-    )
-    right_other = exchange_cores(right_sent)
+        normed, x, mask, gat, out, d_updated, gate_weight, side_weights,
+    )
+    right_other, query_other, cg, cp, hat, rstd, dn = lax.optimization_barrier(
+        (right_other, exchange(query_sum), cg, cp, hat, rstd, dn)
+    )
     (left,) = call(left_kernel, [((256, 256), F32)], pg, b)
     (grads,) = call(triangle_kernel, [((1024, 128), BF16)], left, right_own, right_other)
-    query_other = exchange(query_sum)
-    (main_grad,) = call(main_kernel, [((16, 32, 128), BF16)], query_sum, query_other, later[3])
     grads = spread_chunks(grads, 16)
-    (pair_grad,) = call(
-        finish_kernel, [((2, 16, 32, 64), BF16)],
-        grads, cg, cp, side_weights, dn, hat, rstd, d_updated, gi_wide,
+    pair_grad, main_grad = call(
+        finish_kernel, [((2, 16, 32, 64), BF16), ((16, 32, 128), BF16)],
+        grads, cg, cp, side_weights, dn, hat, rstd, d_updated, gi_wide, query_sum, query_other, later[3],
         scratch=[pltpu.VMEM((1024, 128), F32)],
     )
     return (pair_grad, main_grad)

time: 87.9 us -> 87.7 us (level)
  blocking collectives: 53.8 us -> 56.8 us
  waiting for transfers between devices: 13.8 us -> 11.4 us
    ppermute x2, waiting for transfers between devices: 10.5 us -> 3.84 us  [exchange(): return lax.ppermute(v, 'tmpl', [(0, 1), (1, 0)])]
    all_to_all x1, waiting for transfers between devices: 1.18 us -> 5.91 us  [spread_chunks(): lax.all_to_all(v.reshape(64, rows, 128), GROUP, 0, 0, axis_index_groups=O...]
    all_to_all x3, blocking collectives: 53.8 us -> 56.8 us  [spread_chunks(): lax.all_to_all(v.reshape(64, rows, 128), GROUP, 0, 0, axis_index_groups=O...]
    pallas_call x11 -> x10, Pallas kernels: 6.38 us -> 5.56 us  [call(): pl.pallas_call(kernel, out_shape=shapes, in_specs=[pl.BlockSpec(memory_sp...]
  transfers between devices with their start and end apart: 5 -> 5, of which waited for: 5 -> 4; matrix products, arithmetic and copies ran while one was open for 0% -> 0% of each run, Pallas kernels for 2% -> 2%
where the time goes in v6:
time: 87.7 us; the launch traced here: 87.4 us
  blocking collectives  56.8 us (65%)
  waiting for transfers between devices  11.4 us (13%)
  starting transfers between devices  11 us (13%)
  Pallas kernels  7.4 us (8%)
    all_to_all x3, blocking collectives, spread_chunks(): lax.all_to_all(v.reshape(64, rows, 128), GROUP, 0, 0, axis_index_groups=O...  56.8 us
    all_to_all x1, starting transfers between devices, spread_chunks(): lax.all_to_all(v.reshape(64, rows, 128), GROUP, 0, 0, axis_index_groups=O...  7.86 us
    all_to_all x1, waiting for transfers between devices, spread_chunks(): lax.all_to_all(v.reshape(64, rows, 128), GROUP, 0, 0, axis_index_groups=O...  5.91 us
    pallas_call x10, Pallas kernels, call(): pl.pallas_call(kernel, out_shape=shapes, in_specs=[pl.BlockSpec(memory_sp...  5.56 us
    ppermute x2, waiting for transfers between devices, exchange(): return lax.ppermute(v, 'tmpl', [(0, 1), (1, 0)])  3.84 us
    ppermute x2, starting transfers between devices, exchange(): return lax.ppermute(v, 'tmpl', [(0, 1), (1, 0)])  2.99 us
    pallas_call x1, Pallas kernels, call_copying(): pl.pallas_call(kernel, out_shape=shapes, in_specs=[pl.BlockSpec(memory_sp...  1.85 us
  transfers between devices with their start and end apart: 5, of which 4 were waited for; matrix products, arithmetic and copies ran while one was open for 0% of the time, Pallas kernels for 2%

profile of v6, /device:TPU:6, one launch (start us, length us, event | category | flops | bytes accessed | tf_op | source)
XLA Modules:
  0.0 87.4 jit_solution(10632439803014122569)
XLA Ops:
  0.6 1.8 %shard_map.185 = (bf16[1024,128]{1,0:T(8,128)(2,1)S(1)}, bf16[64,1024]{1,0:T(8,128)(2,1)S(1)}, bf16[64,1024]{1,0:T(8,128)(2,1)S(1)}, f32[64,128]{1,0:T(8,128)S(1...) custom-call(bf16[2,16,32,64]{3,2,1,0:T(8,128)(2,1)} %x_hbm.1, ...), custom_call_target="tpu_custom_call" | custom-call | tf_op jit(solution)/shard_map/pallas_call | solution.py:419
  2.5 23.3 %all_to_all.20 = bf16[64,16,128]{2,1,0:T(8,128)(2,1)S(1)} all-to-all(bf16[64,16,128]{2,1,0:T(8,128)(2,1)S(1)} %bitcast.18), channel_id=1, replica_groups={{96,97,98,99,100,101,102,103,112,113,114,115,116,117,118,119,64,65,66,6..., dimensions={0} | all-to-all | bytes 524288 | tf_op jit(solution)/shard_map/all_to_all | solution.py:439
  25.8 0.3 shard_map.186
  26.1 0.1 collective-permute-start
  26.2 0.3 shard_map.187
  26.5 1.0 %collective-permute-done.other_ref = bf16[256,256]{1,0:T(8,128)(2,1)S(1)} collective-permute-done((bf16[256,256]{1,0:T(8,128)(2,1)S(1)}, bf16[256,256]{1,0:T(8,128)(2,1)S(1)}, u32[]{:S(2)}, u32[]{:S(2)}) %collective-permute-start) | collective-permute-done | bytes 131104 | tf_op jit(solution)/shard_map/ppermute | solution.py:435
  27.5 0.4 shard_map.188
  27.9 15.5 %all_to_all.21 = bf16[64,8,128]{2,1,0:T(8,128)(2,1)S(1)} all-to-all(bf16[64,8,128]{2,1,0:T(8,128)(2,1)S(1)} %bitcast.19), channel_id=1, replica_groups={{96,97,98,99,100,101,102,103,112,113,114,115,116,117,118,119,64,65,66,6..., dimensions={0} | all-to-all | bytes 262144 | tf_op jit(solution)/shard_map/all_to_all | solution.py:439
  43.4 0.6 shard_map.189
  44.0 1.5 %collective-permute-start.1 = (f32[2,4,512]{2,1,0:T(4,128)S(1)}, f32[2,4,512]{2,1,0:T(4,128)S(1)}, u32[]{:S(2)}, u32[]{:S(2)}) collective-permute-start(f32[2,4,512]{2,1,0:T(4,128)S(1)} %get-tuple-element.133.mine_ref), channel_id=1, source_target_pairs={{0,128},{128,0},{1,129},{129,1},{2,130},{130,2},{3,131},{131,3},{4... | collective-permute-start | bytes 49160 | tf_op jit(solution)/shard_map/ppermute | solution.py:431
  45.5 3.8 %collective-permute-done.1.other_ref = f32[2,4,512]{2,1,0:T(4,128)S(1)} collective-permute-done((f32[2,4,512]{2,1,0:T(4,128)S(1)}, f32[2,4,512]{2,1,0:T(4,128)S(1)}, u32[]{:S(2)}, u32[]{:S(2)}) %collective-permute-start.1) | collective-permute-done | bytes 16416 | tf_op jit(solution)/shard_map/ppermute | solution.py:431
  49.4 1.2 %shard_map.190 = (bf16[512,128]{1,0:T(8,128)(2,1)}, f32[64,512]{1,0:T(8,128)S(1)}, f32[64,1024]{1,0:T(8,128)S(1)}) custom-call(f32[64,1024]{1,0:T(8,128)S(1)} %get-tuple-element.117.gat_ref, bf16[64,512]{1,0:T(8,128)(2,1)S(1)} %get-tuple-element.118.q_ref, f32[64,512]{1,0:T(8,128)S(1)} %get-tuple-element.119.g_ref, ...), custom_call_target="tpu_custom_call" | custom-call | bytes 1503232 | tf_op jit(solution)/shard_map/pallas_call | solution.py:404
  50.6 7.9 %all-to-all-start.2 = ((bf16[64,8,128]{2,1,0:T(8,128)(2,1)}), bf16[64,8,128]{2,1,0:T(8,128)(2,1)S(1)}, u32[]{:S(2)}, u32[]{:S(2)}) async-start(bf16[64,8,128]{2,1,0:T(8,128)(2,1)} %bitcast.9), calls=%async_computation.2 | async-start | bytes 262144 | tf_op jit(solution)/shard_map/all_to_all | solution.py:439
  58.4 1.5 %collective-permute-start.3 = (f32[64,512]{1,0:T(8,128)S(1)}, f32[64,512]{1,0:T(8,128)S(1)}, u32[]{:S(2)}, u32[]{:S(2)}) collective-permute-start(f32[64,512]{1,0:T(8,128)S(1)} %get-tuple-element.144.mine_ref), channel_id=1, source_target_pairs={{0,128},{128,0},{1,129},{129,1},{2,130},{130,2},{3,131},{131,3},{4... | collective-permute-start | bytes 393224 | tf_op jit(solution)/shard_map/ppermute | solution.py:431
  59.9 5.9 %all-to-all-done.2 = bf16[64,8,128]{2,1,0:T(8,128)(2,1)S(1)} async-done(((bf16[64,8,128]{2,1,0:T(8,128)(2,1)}), bf16[64,8,128]{2,1,0:T(8,128)(2,1)S(1)}, u32[]{:S(2)}, u32[]{:S(2)}) %all-to-all-start.2) | async-done | bytes 131104 | tf_op jit(solution)/shard_map/all_to_all | solution.py:439
  65.8 0.4 shard_map.191
  66.2 0.1 collective-permute-start.2
  66.3 0.2 shard_map.192.left_ref
  66.5 0.4 shard_map.193
  67.0 0.0 collective-permute-done.3.other_ref
  67.0 0.7 collective-permute-done.2.other_ref
  67.7 0.3 shard_map.194
  68.0 18.1 %all_to_all.22 = bf16[64,16,128]{2,1,0:T(8,128)(2,1)S(1)} all-to-all(bf16[64,16,128]{2,1,0:T(8,128)(2,1)S(1)} %bitcast.14), channel_id=1, replica_groups={{96,97,98,99,100,101,102,103,112,113,114,115,116,117,118,119,64,65,66,6..., dimensions={0} | all-to-all | bytes 524288 | tf_op jit(solution)/shard_map/all_to_all | solution.py:439
  86.1 1.3 %shard_map.195 = (bf16[2,16,32,64]{3,2,1,0:T(8,128)(2,1)}, bf16[16,32,128]{2,1,0:T(8,128)(2,1)}) custom-call(bf16[1024,128]{1,0:T(8,128)(2,1)S(1)} %bitcast.13, f32[128,1024]{1,0:T(8,128)S(1)} %get-tuple-element.157.cg_ref, f32[128,1024]{1,0:T(8,128)S(1)} %get-tuple-element.158.cp_ref, bf16[64,256]{1,0:T(8,128)(2,1)S(1)} %get-tuple-element.150.sides_ref, ...), custom_call_target="tpu_custom_call" | custom-call | bytes 2445312 | tf_op jit(solution)/shard_map/pallas_call | solution.py:404
Async XLA Ops:
  26.1 1.4 %collective-permute-start = (bf16[256,256]{1,0:T(8,128)(2,1)S(1)}, bf16[256,256]{1,0:T(8,128)(2,1)S(1)}, u32[]{:S(2)}, u32[]{:S(2)}) collective-permute-start(bf16[256,256]{1,0:T(8,128)(2,1)S(1)} %get-tuple-element.122.own_ref), channel_id=1, source_target_pairs={{0,8},{8,0},{16,24},{24,16},{32,40},{40,32},{48,56},{56,48},{64,72... | collective-permute-start | bytes 393224 | tf_op jit(solution)/shard_map/ppermute | solution.py:435
  44.0 5.3 %collective-permute-start.1 = (f32[2,4,512]{2,1,0:T(4,128)S(1)}, f32[2,4,512]{2,1,0:T(4,128)S(1)}, u32[]{:S(2)}, u32[]{:S(2)}) collective-permute-start(f32[2,4,512]{2,1,0:T(4,128)S(1)} %get-tuple-element.133.mine_ref), channel_id=1, source_target_pairs={{0,128},{128,0},{1,129},{129,1},{2,130},{130,2},{3,131},{131,3},{4... | collective-permute-start | bytes 49160 | tf_op jit(solution)/shard_map/ppermute | solution.py:431
  50.6 15.3 %all-to-all-start.2 = ((bf16[64,8,128]{2,1,0:T(8,128)(2,1)}), bf16[64,8,128]{2,1,0:T(8,128)(2,1)S(1)}, u32[]{:S(2)}, u32[]{:S(2)}) async-start(bf16[64,8,128]{2,1,0:T(8,128)(2,1)} %bitcast.9), calls=%async_computation.2 | async-start | bytes 262144 | tf_op jit(solution)/shard_map/all_to_all | solution.py:439
  58.4 8.5 %collective-permute-start.3 = (f32[64,512]{1,0:T(8,128)S(1)}, f32[64,512]{1,0:T(8,128)S(1)}, u32[]{:S(2)}, u32[]{:S(2)}) collective-permute-start(f32[64,512]{1,0:T(8,128)S(1)} %get-tuple-element.144.mine_ref), channel_id=1, source_target_pairs={{0,128},{128,0},{1,129},{129,1},{2,130},{130,2},{3,131},{131,3},{4... | collective-permute-start | bytes 393224 | tf_op jit(solution)/shard_map/ppermute | solution.py:431
  66.2 1.4 %collective-permute-start.2 = (bf16[256,256]{1,0:T(8,128)(2,1)S(1)}, bf16[256,256]{1,0:T(8,128)(2,1)S(1)}, u32[]{:S(2)}, u32[]{:S(2)}) collective-permute-start(bf16[256,256]{1,0:T(8,128)(2,1)S(1)} %get-tuple-element.143), channel_id=1, source_target_pairs={{0,8},{8,0},{16,24},{24,16},{32,40},{40,32},{48,56},{56,48},{64,72... | collective-permute-start | bytes 393224 | tf_op jit(solution)/shard_map/ppermute | solution.py:435

commit v7 on v6

--- a/solution.py
+++ b/solution.py
@@ -19,7 +19,9 @@
 LATER = 11
 SIDE_BLOCKS = [(s, side, r) for s in range(2) for side in range(2) for r in range(4)]
 PIXEL_ROWS = [4 * q + r for r in range(4) for q in range(4)]
-ORDER = [[(z ^ TURN) * 16 + core * 8 + col for z in range(8) for col in range(8)] for core in range(2)]
+COLS = [x * 4 + y for y in range(4) for x in range(2)]
+PLACES = [COLS.index(col) for col in range(8)]
+ORDER = [[(z ^ TURN) * 16 + core * 8 + col for z in range(8) for col in COLS] for core in range(2)]
 
 
 def iota(shape, axis):
@@ -220,7 +222,7 @@
 
 def layout_kernel(x_ref, a_out, b_out):
     tiles = x_ref[...].astype(F32).reshape(8, 8, 2, 8, 128)
-    parts = [v.reshape(8, 2, 8, 256) for v in swap_in([tiles[:, c].reshape(128, 128) for c in range(8)])]
+    parts = [v.reshape(8, 2, 8, 256) for v in swap_in([tiles[:, c].reshape(128, 128) for c in PLACES])]
     rolled = [pltpu.roll(v.reshape(16, 8, 256), 4, 1).reshape(8, 2, 8, 256) for v in parts]
     top = iota((8, 8, 256), 1) < 4
     a, b = [], []
@@ -247,7 +249,7 @@
     for v in swap_out(rows):
         v = v.reshape(2, 4, 8, 128)
         pairs.append(jnp.stack(pair_up(v[0], v[1]), axis=1).reshape(8, 8, 128))
-    out_ref[...] = jnp.stack(pairs, axis=1).reshape(512, 128).astype(BF16)
+    out_ref[...] = jnp.stack([pairs[c] for c in COLS], axis=1).reshape(512, 128).astype(BF16)
 
 
 def heads_sum(v):
@@ -296,17 +298,16 @@
 
 
 def grad_kernel(
-    gat_ref, q_ref, g_ref, key_ref, w_ref, along_ref, mine_ref, other_ref,
+    gat_ref, q_ref, g_ref, w_ref, along_ref, mine_ref, other_ref,
     gm_ref, gf_ref, wide_ref, kv_ref, hat_m_ref, rstd_m_ref, hat_f_ref, rstd_f_ref,
-    pg_out, qsum_out, du_out,
+    pg_out, slope_out, du_out,
 ):
     share = jax.nn.sigmoid(mine_ref[0] - other_ref[0])
     average = share * mine_ref[1] + jax.nn.sigmoid(other_ref[0] - mine_ref[0]) * other_ref[1]
     weights = w_ref[...] * both(share)
     slope = weights * (along_ref[...] - both(average))
     slope_wide = heads_spread(slope)
-    part = slope_wide * key_ref[...].astype(F32)
-    qsum_out[...] = (part[:, :512] + part[:, 512:]) * SCALE
+    slope_out[...] = slope
     key_grad = (slope_wide * both(q_ref[...].astype(F32) * SCALE)).astype(BF16)
     value_grad = (heads_spread(weights) * both(g_ref[...])).astype(BF16)
     d_final = dot(kv_ref[...], jnp.concatenate([key_grad, value_grad], axis=0))
@@ -321,6 +322,11 @@
     pg_out[256:, :] = pg[:, 128:]
 
 
+def query_kernel(key_ref, slope_ref, out_ref):
+    part = heads_spread(slope_ref[...]) * key_ref[...].astype(F32)
+    out_ref[...] = (part[:, :512] + part[:, 512:]) * SCALE
+
+
 def coef_kernel(
     n_ref, x_ref, mask_ref, gat_ref, out_ref, du_ref, go_ref, sides_ref, cg_out, cp_out, hat_out, rstd_out, dn_out
 ):
@@ -337,7 +343,7 @@
 
 def right_kernel(pg_ref, a_ref, pg_out, own_out, sent_out):
     tiles = pg_ref[...].astype(F32).reshape(8, 8, 8, 128)
-    parts = swap_in([tiles[:, c].reshape(64, 128) for c in range(8)])
+    parts = swap_in([tiles[:, c].reshape(64, 128) for c in PLACES])
     split = [pair_up(v.reshape(4, 2, 8, 256)[:, 0], v.reshape(4, 2, 8, 256)[:, 1]) for v in parts]
     for e in range(2):
         pg = jnp.concatenate([v[e].reshape(32, 256) for v in split], axis=0).astype(BF16)
@@ -369,7 +375,7 @@
             tiles.append(jnp.where(top, upper, lower))
         rows.append(jnp.stack(tiles, axis=1).reshape(128, 256))
     cols = [v.reshape(8, 2, 8, 128) for v in swap_out(rows)]
-    out_ref[...] = jnp.stack(cols, axis=1).reshape(1024, 128).astype(BF16)
+    out_ref[...] = jnp.stack([cols[c] for c in COLS], axis=1).reshape(1024, 128).astype(BF16)
 
 
 def finish_kernel(
@@ -484,12 +490,13 @@
         x, prod, gat, query, grad_out, absent, gm_wide, gf_wide, wide, kv,
     )
     other = exchange(stat)
-    pg, query_sum, d_updated = call(
+    pg, slope, d_updated = call(
         grad_kernel,
-        [((512, 128), BF16), ((64, 512), F32), ((64, 1024), F32)],
-        gat, query, grad_out, key, weights, along, stat, other,
+        [((512, 128), BF16), ((4, 1024), F32), ((64, 1024), F32)],
+        gat, query, grad_out, weights, along, stat, other,
         gm_wide, gf_wide, wide, kv, hat_m, rstd_m, hat_f, rstd_f,
     )
+    (query_sum,) = call(query_kernel, [((64, 512), F32)], key, slope)
     pg = spread_chunks(pg, 8)
     pg, right_own, right_sent = call(
         right_kernel, [((256, 256), BF16), ((256, 256), F32), ((256, 256), BF16)], pg, a

time: 87.7 us -> 87.4 us (level)
    pallas_call x10 -> x11, Pallas kernels: 5.56 us -> 5.57 us  [call(): pl.pallas_call(kernel, out_shape=shapes, in_specs=[pl.BlockSpec(memory_sp...]
where the time goes in v7:
time: 87.4 us; the launch traced here: 87 us
  blocking collectives  56.1 us (64%)
  starting transfers between devices  11.4 us (13%)
  waiting for transfers between devices  11.3 us (13%)
  Pallas kernels  7.42 us (8%)
    all_to_all x3, blocking collectives, spread_chunks(): lax.all_to_all(v.reshape(64, rows, 128), GROUP, 0, 0, axis_index_groups=O...  56.1 us
    all_to_all x1, starting transfers between devices, spread_chunks(): lax.all_to_all(v.reshape(64, rows, 128), GROUP, 0, 0, axis_index_groups=O...  8.23 us
    all_to_all x1, waiting for transfers between devices, spread_chunks(): lax.all_to_all(v.reshape(64, rows, 128), GROUP, 0, 0, axis_index_groups=O...  5.8 us
    pallas_call x11, Pallas kernels, call(): pl.pallas_call(kernel, out_shape=shapes, in_specs=[pl.BlockSpec(memory_sp...  5.57 us
    ppermute x2, waiting for transfers between devices, exchange(): return lax.ppermute(v, 'tmpl', [(0, 1), (1, 0)])  3.84 us
    ppermute x2, starting transfers between devices, exchange(): return lax.ppermute(v, 'tmpl', [(0, 1), (1, 0)])  2.98 us
    pallas_call x1, Pallas kernels, call_copying(): pl.pallas_call(kernel, out_shape=shapes, in_specs=[pl.BlockSpec(memory_sp...  1.85 us
  transfers between devices with their start and end apart: 5, of which 4 were waited for; matrix products, arithmetic and copies ran while one was open for 0% of the time, Pallas kernels for 2%

profile of v7, /device:TPU:6, one launch (start us, length us, event | category | flops | bytes accessed | tf_op | source)
XLA Modules:
  0.0 87.0 jit_solution(17076011194568496722)
XLA Ops:
  0.6 1.8 %shard_map.185 = (bf16[1024,128]{1,0:T(8,128)(2,1)S(1)}, bf16[64,1024]{1,0:T(8,128)(2,1)S(1)}, bf16[64,1024]{1,0:T(8,128)(2,1)S(1)}, f32[64,128]{1,0:T(8,128)S(1...) custom-call(bf16[2,16,32,64]{3,2,1,0:T(8,128)(2,1)} %x_hbm.1, ...), custom_call_target="tpu_custom_call" | custom-call | tf_op jit(solution)/shard_map/pallas_call | solution.py:425
  2.5 22.6 %all_to_all.20 = bf16[64,16,128]{2,1,0:T(8,128)(2,1)S(1)} all-to-all(bf16[64,16,128]{2,1,0:T(8,128)(2,1)S(1)} %bitcast.18), channel_id=1, replica_groups={{96,100,97,101,98,102,99,103,112,116,113,117,114,118,115,119,64,68,65,6..., dimensions={0} | all-to-all | bytes 524288 | tf_op jit(solution)/shard_map/all_to_all | solution.py:445
  25.1 0.3 shard_map.186
  25.5 0.1 collective-permute-start
  25.6 0.3 shard_map.187
  25.9 1.0 %collective-permute-done.other_ref = bf16[256,256]{1,0:T(8,128)(2,1)S(1)} collective-permute-done((bf16[256,256]{1,0:T(8,128)(2,1)S(1)}, bf16[256,256]{1,0:T(8,128)(2,1)S(1)}, u32[]{:S(2)}, u32[]{:S(2)}) %collective-permute-start) | collective-permute-done | bytes 131104 | tf_op jit(solution)/shard_map/ppermute | solution.py:441
  26.9 0.4 shard_map.188
  27.3 15.8 %all_to_all.21 = bf16[64,8,128]{2,1,0:T(8,128)(2,1)S(1)} all-to-all(bf16[64,8,128]{2,1,0:T(8,128)(2,1)S(1)} %bitcast.19), channel_id=1, replica_groups={{96,100,97,101,98,102,99,103,112,116,113,117,114,118,115,119,64,68,65,6..., dimensions={0} | all-to-all | bytes 262144 | tf_op jit(solution)/shard_map/all_to_all | solution.py:445
  43.1 0.6 shard_map.189
  43.8 1.5 %collective-permute-start.1 = (f32[2,4,512]{2,1,0:T(4,128)S(1)}, f32[2,4,512]{2,1,0:T(4,128)S(1)}, u32[]{:S(2)}, u32[]{:S(2)}) collective-permute-start(f32[2,4,512]{2,1,0:T(4,128)S(1)} %get-tuple-element.132.mine_ref), channel_id=1, source_target_pairs={{0,128},{128,0},{1,129},{129,1},{2,130},{130,2},{3,131},{131,3},{4... | collective-permute-start | bytes 49160 | tf_op jit(solution)/shard_map/ppermute | solution.py:437
  45.3 3.8 %collective-permute-done.1.other_ref = f32[2,4,512]{2,1,0:T(4,128)S(1)} collective-permute-done((f32[2,4,512]{2,1,0:T(4,128)S(1)}, f32[2,4,512]{2,1,0:T(4,128)S(1)}, u32[]{:S(2)}, u32[]{:S(2)}) %collective-permute-start.1) | collective-permute-done | bytes 16416 | tf_op jit(solution)/shard_map/ppermute | solution.py:437
  49.1 1.2 %shard_map.190 = (bf16[512,128]{1,0:T(8,128)(2,1)}, f32[4,1024]{1,0:T(4,128)S(1)}, f32[64,1024]{1,0:T(8,128)S(1)}) custom-call(f32[64,1024]{1,0:T(8,128)S(1)} %get-tuple-element.117.gat_ref, bf16[64,512]{1,0:T(8,128)(2,1)S(1)} %get-tuple-element.118.q_ref, f32[64,512]{1,0:T(8,128)S(1)} %get-tuple-element.119.g_ref, f32[4,1024]{1,0:T(4,128)S(1)} %get-tuple-element.130.w_ref, ...), custom_call_target="tpu_custom_call" | custom-call | bytes 1372160 | tf_op jit(solution)/shard_map/pallas_call | solution.py:410
  50.3 8.2 %all-to-all-start.2 = ((bf16[64,8,128]{2,1,0:T(8,128)(2,1)}), bf16[64,8,128]{2,1,0:T(8,128)(2,1)S(1)}, u32[]{:S(2)}, u32[]{:S(2)}) async-start(bf16[64,8,128]{2,1,0:T(8,128)(2,1)} %bitcast.9), calls=%async_computation.2 | async-start | bytes 262144 | tf_op jit(solution)/shard_map/all_to_all | solution.py:445
  58.6 1.5 %collective-permute-start.3 = (f32[64,512]{1,0:T(8,128)S(1)}, f32[64,512]{1,0:T(8,128)S(1)}, u32[]{:S(2)}, u32[]{:S(2)}) collective-permute-start(f32[64,512]{1,0:T(8,128)S(1)} %shard_map.193.mine_ref), channel_id=1, source_target_pairs={{0,128},{128,0},{1,129},{129,1},{2,130},{130,2},{3,131},{131,3},{4... | collective-permute-start | bytes 393224 | tf_op jit(solution)/shard_map/ppermute | solution.py:437
  60.1 5.8 %all-to-all-done.2 = bf16[64,8,128]{2,1,0:T(8,128)(2,1)S(1)} async-done(((bf16[64,8,128]{2,1,0:T(8,128)(2,1)}), bf16[64,8,128]{2,1,0:T(8,128)(2,1)S(1)}, u32[]{:S(2)}, u32[]{:S(2)}) %all-to-all-start.2) | async-done | bytes 131104 | tf_op jit(solution)/shard_map/all_to_all | solution.py:445
  65.9 0.4 shard_map.191
  66.3 0.1 collective-permute-start.2
  66.4 0.2 shard_map.192.left_ref
  66.6 0.4 shard_map.194
  67.0 0.0 collective-permute-done.3.other_ref
  67.0 0.7 collective-permute-done.2.other_ref
  67.7 0.3 shard_map.195
  68.0 17.6 %all_to_all.22 = bf16[64,16,128]{2,1,0:T(8,128)(2,1)S(1)} all-to-all(bf16[64,16,128]{2,1,0:T(8,128)(2,1)S(1)} %bitcast.14), channel_id=1, replica_groups={{96,100,97,101,98,102,99,103,112,116,113,117,114,118,115,119,64,68,65,6..., dimensions={0} | all-to-all | bytes 524288 | tf_op jit(solution)/shard_map/all_to_all | solution.py:445
  85.7 1.3 %shard_map.196 = (bf16[2,16,32,64]{3,2,1,0:T(8,128)(2,1)}, bf16[16,32,128]{2,1,0:T(8,128)(2,1)}) custom-call(bf16[1024,128]{1,0:T(8,128)(2,1)S(1)} %bitcast.13, f32[128,1024]{1,0:T(8,128)S(1)} %get-tuple-element.157.cg_ref, f32[128,1024]{1,0:T(8,128)S(1)} %get-tuple-element.158.cp_ref, bf16[64,256]{1,0:T(8,128)(2,1)S(1)} %get-tuple-element.150.sides_ref, ...), custom_call_target="tpu_custom_call" | custom-call | bytes 2445312 | tf_op jit(solution)/shard_map/pallas_call | solution.py:410
  (1 shorter events, 0.0 us)
Async XLA Ops:
  25.5 1.4 %collective-permute-start = (bf16[256,256]{1,0:T(8,128)(2,1)S(1)}, bf16[256,256]{1,0:T(8,128)(2,1)S(1)}, u32[]{:S(2)}, u32[]{:S(2)}) collective-permute-start(bf16[256,256]{1,0:T(8,128)(2,1)S(1)} %get-tuple-element.122.own_ref), channel_id=1, source_target_pairs={{0,8},{8,0},{16,24},{24,16},{32,40},{40,32},{48,56},{56,48},{64,72... | collective-permute-start | bytes 393224 | tf_op jit(solution)/shard_map/ppermute | solution.py:441
  43.8 5.3 %collective-permute-start.1 = (f32[2,4,512]{2,1,0:T(4,128)S(1)}, f32[2,4,512]{2,1,0:T(4,128)S(1)}, u32[]{:S(2)}, u32[]{:S(2)}) collective-permute-start(f32[2,4,512]{2,1,0:T(4,128)S(1)} %get-tuple-element.132.mine_ref), channel_id=1, source_target_pairs={{0,128},{128,0},{1,129},{129,1},{2,130},{130,2},{3,131},{131,3},{4... | collective-permute-start | bytes 49160 | tf_op jit(solution)/shard_map/ppermute | solution.py:437
  50.3 15.6 %all-to-all-start.2 = ((bf16[64,8,128]{2,1,0:T(8,128)(2,1)}), bf16[64,8,128]{2,1,0:T(8,128)(2,1)S(1)}, u32[]{:S(2)}, u32[]{:S(2)}) async-start(bf16[64,8,128]{2,1,0:T(8,128)(2,1)} %bitcast.9), calls=%async_computation.2 | async-start | bytes 262144 | tf_op jit(solution)/shard_map/all_to_all | solution.py:445
  58.6 8.4 %collective-permute-start.3 = (f32[64,512]{1,0:T(8,128)S(1)}, f32[64,512]{1,0:T(8,128)S(1)}, u32[]{:S(2)}, u32[]{:S(2)}) collective-permute-start(f32[64,512]{1,0:T(8,128)S(1)} %shard_map.193.mine_ref), channel_id=1, source_target_pairs={{0,128},{128,0},{1,129},{129,1},{2,130},{130,2},{3,131},{131,3},{4... | collective-permute-start | bytes 393224 | tf_op jit(solution)/shard_map/ppermute | solution.py:437
  66.3 1.4 %collective-permute-start.2 = (bf16[256,256]{1,0:T(8,128)(2,1)S(1)}, bf16[256,256]{1,0:T(8,128)(2,1)S(1)}, u32[]{:S(2)}, u32[]{:S(2)}) collective-permute-start(bf16[256,256]{1,0:T(8,128)(2,1)S(1)} %get-tuple-element.142), channel_id=1, source_target_pairs={{0,8},{8,0},{16,24},{24,16},{32,40},{40,32},{48,56},{56,48},{64,72... | collective-permute-start | bytes 393224 | tf_op jit(solution)/shard_map/ppermute | solution.py:441

commit v8 on v7

--- a/solution.py
+++ b/solution.py
@@ -236,14 +236,14 @@
     b_out[...] = jnp.concatenate(b, axis=0).astype(BF16)
 
 
-def product_kernel(a_ref, own_ref, other_ref, out_ref, b_out):
-    prods = []
-    for e in range(2):
-        own = own_ref[e * 128 : e * 128 + 128, :].reshape(8, 16, 256)
-        other = other_ref[e * 128 : e * 128 + 128, :].reshape(8, 16, 256)
-        b = jnp.stack(by_core(own, other), axis=1).reshape(256, 256)
-        b_out[e * 256 : e * 256 + 256, :] = b
-        prods.append(dot_nt(a_ref[e * 128 : e * 128 + 128, :], b))
+def whole_b(own_ref, other_ref, e):
+    own = own_ref[e * 128 : e * 128 + 128, :].reshape(8, 16, 256)
+    other = other_ref[e * 128 : e * 128 + 128, :].reshape(8, 16, 256)
+    return jnp.stack(by_core(own, other), axis=1).reshape(256, 256)
+
+
+def product_kernel(a_ref, own_ref, other_ref, out_ref):
+    prods = [dot_nt(a_ref[e * 128 : e * 128 + 128, :], whole_b(own_ref, other_ref, e)) for e in range(2)]
     rows = [jnp.concatenate([v[q * 32 : q * 32 + 32] for v in prods], axis=0) for q in range(4)]
     pairs = []
     for v in swap_out(rows):
@@ -354,10 +354,10 @@
         sent_out[e * 128 : e * 128 + 128, :] = sent.reshape(128, 256).astype(BF16)
 
 
-def left_kernel(pg_ref, b_ref, out_ref):
+def left_kernel(pg_ref, own_ref, other_ref, out_ref):
     for e in range(2):
         out_ref[e * 128 : e * 128 + 128, :] = dot(
-            pg_ref[e * 128 : e * 128 + 128, :], b_ref[e * 256 : e * 256 + 256, :]
+            pg_ref[e * 128 : e * 128 + 128, :], whole_b(own_ref, other_ref, e)
         )
 
 
@@ -479,7 +479,7 @@
     b_other, (gat, query, grad_out, wide, kv, gm_wide, gf_wide, absent) = lax.optimization_barrier(
         (b_other, side)
     )
-    prod, b = call(product_kernel, [((512, 128), BF16), ((512, 256), BF16)], a, b_own, b_other)
+    (prod,) = call(product_kernel, [((512, 128), BF16)], a, b_own, b_other)
     prod = spread_chunks(prod, 8)
     stat, weights, along, key, hat_m, rstd_m, out, hat_f, rstd_f = call(
         score_kernel,
@@ -511,7 +511,7 @@
     right_other, query_other, cg, cp, hat, rstd, dn = lax.optimization_barrier(
         (right_other, exchange(query_sum), cg, cp, hat, rstd, dn)
     )
-    (left,) = call(left_kernel, [((256, 256), F32)], pg, b)
+    (left,) = call(left_kernel, [((256, 256), F32)], pg, b_own, b_other)
     (grads,) = call(triangle_kernel, [((1024, 128), BF16)], left, right_own, right_other)
     grads = spread_chunks(grads, 16)
     pair_grad, main_grad = call(

time: 87.4 us -> 87.4 us (level)
  no operation moved by 1% of the time
where the time goes in v8:
time: 87.4 us; the launch traced here: 87 us
  blocking collectives  56.1 us (64%)
  starting transfers between devices  11.4 us (13%)
  waiting for transfers between devices  11.3 us (13%)
  Pallas kernels  7.43 us (9%)
    all_to_all x3, blocking collectives, spread_chunks(): lax.all_to_all(v.reshape(64, rows, 128), GROUP, 0, 0, axis_index_groups=O...  56.1 us
    all_to_all x1, starting transfers between devices, spread_chunks(): lax.all_to_all(v.reshape(64, rows, 128), GROUP, 0, 0, axis_index_groups=O...  8.23 us
    all_to_all x1, waiting for transfers between devices, spread_chunks(): lax.all_to_all(v.reshape(64, rows, 128), GROUP, 0, 0, axis_index_groups=O...  5.76 us
    pallas_call x11, Pallas kernels, call(): pl.pallas_call(kernel, out_shape=shapes, in_specs=[pl.BlockSpec(memory_sp...  5.58 us
    ppermute x2, waiting for transfers between devices, exchange(): return lax.ppermute(v, 'tmpl', [(0, 1), (1, 0)])  3.84 us
    ppermute x2, starting transfers between devices, exchange(): return lax.ppermute(v, 'tmpl', [(0, 1), (1, 0)])  2.99 us
    pallas_call x1, Pallas kernels, call_copying(): pl.pallas_call(kernel, out_shape=shapes, in_specs=[pl.BlockSpec(memory_sp...  1.85 us
  transfers between devices with their start and end apart: 5, of which 4 were waited for; matrix products, arithmetic and copies ran while one was open for 0% of the time, Pallas kernels for 2%

profile of v8, /device:TPU:6, one launch (start us, length us, event | category | flops | bytes accessed | tf_op | source)
XLA Modules:
  0.0 87.0 jit_solution(8129462845780936971)
XLA Ops:
  0.6 1.8 %shard_map.185 = (bf16[1024,128]{1,0:T(8,128)(2,1)S(1)}, bf16[64,1024]{1,0:T(8,128)(2,1)S(1)}, bf16[64,1024]{1,0:T(8,128)(2,1)S(1)}, f32[64,128]{1,0:T(8,128)S(1...) custom-call(bf16[2,16,32,64]{3,2,1,0:T(8,128)(2,1)} %x_hbm.1, ...), custom_call_target="tpu_custom_call" | custom-call | tf_op jit(solution)/shard_map/pallas_call | solution.py:425
  2.5 22.6 %all_to_all.20 = bf16[64,16,128]{2,1,0:T(8,128)(2,1)S(1)} all-to-all(bf16[64,16,128]{2,1,0:T(8,128)(2,1)S(1)} %bitcast.19), channel_id=1, replica_groups={{96,100,97,101,98,102,99,103,112,116,113,117,114,118,115,119,64,68,65,6..., dimensions={0} | all-to-all | bytes 524288 | tf_op jit(solution)/shard_map/all_to_all | solution.py:445
  25.1 0.3 shard_map.186
  25.5 0.1 collective-permute-start
  25.6 0.3 shard_map.187
  25.9 1.0 %collective-permute-done.other_ref = bf16[256,256]{1,0:T(8,128)(2,1)S(1)} collective-permute-done((bf16[256,256]{1,0:T(8,128)(2,1)S(1)}, bf16[256,256]{1,0:T(8,128)(2,1)S(1)}, u32[]{:S(2)}, u32[]{:S(2)}) %collective-permute-start) | collective-permute-done | bytes 131104 | tf_op jit(solution)/shard_map/ppermute | solution.py:441
  26.9 0.4 shard_map.188
  27.3 15.8 %all_to_all.21 = bf16[64,8,128]{2,1,0:T(8,128)(2,1)S(1)} all-to-all(bf16[64,8,128]{2,1,0:T(8,128)(2,1)S(1)} %bitcast.17), channel_id=1, replica_groups={{96,100,97,101,98,102,99,103,112,116,113,117,114,118,115,119,64,68,65,6..., dimensions={0} | all-to-all | bytes 262144 | tf_op jit(solution)/shard_map/all_to_all | solution.py:445
  43.1 0.6 shard_map.189
  43.8 1.5 %collective-permute-start.1 = (f32[2,4,512]{2,1,0:T(4,128)S(1)}, f32[2,4,512]{2,1,0:T(4,128)S(1)}, u32[]{:S(2)}, u32[]{:S(2)}) collective-permute-start(f32[2,4,512]{2,1,0:T(4,128)S(1)} %get-tuple-element.129.mine_ref), channel_id=1, source_target_pairs={{0,128},{128,0},{1,129},{129,1},{2,130},{130,2},{3,131},{131,3},{4... | collective-permute-start | bytes 49160 | tf_op jit(solution)/shard_map/ppermute | solution.py:437
  45.3 3.8 %collective-permute-done.1.other_ref = f32[2,4,512]{2,1,0:T(4,128)S(1)} collective-permute-done((f32[2,4,512]{2,1,0:T(4,128)S(1)}, f32[2,4,512]{2,1,0:T(4,128)S(1)}, u32[]{:S(2)}, u32[]{:S(2)}) %collective-permute-start.1) | collective-permute-done | bytes 16416 | tf_op jit(solution)/shard_map/ppermute | solution.py:437
  49.1 1.2 %shard_map.190 = (bf16[512,128]{1,0:T(8,128)(2,1)}, f32[4,1024]{1,0:T(4,128)S(1)}, f32[64,1024]{1,0:T(8,128)S(1)}) custom-call(f32[64,1024]{1,0:T(8,128)S(1)} %get-tuple-element.115.gat_ref, bf16[64,512]{1,0:T(8,128)(2,1)S(1)} %get-tuple-element.116.q_ref, f32[64,512]{1,0:T(8,128)S(1)} %get-tuple-element.117.g_ref, f32[4,1024]{1,0:T(4,128)S(1)} %get-tuple-element.127.w_ref, ...), custom_call_target="tpu_custom_call" | custom-call | bytes 1372160 | tf_op jit(solution)/shard_map/pallas_call | solution.py:410
  50.3 8.2 %all-to-all-start.2 = ((bf16[64,8,128]{2,1,0:T(8,128)(2,1)}), bf16[64,8,128]{2,1,0:T(8,128)(2,1)S(1)}, u32[]{:S(2)}, u32[]{:S(2)}) async-start(bf16[64,8,128]{2,1,0:T(8,128)(2,1)} %bitcast.9), calls=%async_computation.2 | async-start | bytes 262144 | tf_op jit(solution)/shard_map/all_to_all | solution.py:445
  58.6 1.5 %collective-permute-start.3 = (f32[64,512]{1,0:T(8,128)S(1)}, f32[64,512]{1,0:T(8,128)S(1)}, u32[]{:S(2)}, u32[]{:S(2)}) collective-permute-start(f32[64,512]{1,0:T(8,128)S(1)} %shard_map.193.mine_ref), channel_id=1, source_target_pairs={{0,128},{128,0},{1,129},{129,1},{2,130},{130,2},{3,131},{131,3},{4... | collective-permute-start | bytes 393224 | tf_op jit(solution)/shard_map/ppermute | solution.py:437
  60.1 5.8 %all-to-all-done.2 = bf16[64,8,128]{2,1,0:T(8,128)(2,1)S(1)} async-done(((bf16[64,8,128]{2,1,0:T(8,128)(2,1)}), bf16[64,8,128]{2,1,0:T(8,128)(2,1)S(1)}, u32[]{:S(2)}, u32[]{:S(2)}) %all-to-all-start.2) | async-done | bytes 131104 | tf_op jit(solution)/shard_map/all_to_all | solution.py:445
  65.8 0.4 shard_map.191
  66.2 0.1 collective-permute-start.2
  66.3 0.2 shard_map.192.left_ref
  66.5 0.4 shard_map.194
  67.0 0.0 collective-permute-done.3.other_ref
  67.0 0.7 collective-permute-done.2.other_ref
  67.7 0.3 shard_map.195
  68.0 17.7 %all_to_all.22 = bf16[64,16,128]{2,1,0:T(8,128)(2,1)S(1)} all-to-all(bf16[64,16,128]{2,1,0:T(8,128)(2,1)S(1)} %bitcast.14), channel_id=1, replica_groups={{96,100,97,101,98,102,99,103,112,116,113,117,114,118,115,119,64,68,65,6..., dimensions={0} | all-to-all | bytes 524288 | tf_op jit(solution)/shard_map/all_to_all | solution.py:445
  85.7 1.3 %shard_map.196 = (bf16[2,16,32,64]{3,2,1,0:T(8,128)(2,1)}, bf16[16,32,128]{2,1,0:T(8,128)(2,1)}) custom-call(bf16[1024,128]{1,0:T(8,128)(2,1)S(1)} %bitcast.13, f32[128,1024]{1,0:T(8,128)S(1)} %get-tuple-element.153.cg_ref, f32[128,1024]{1,0:T(8,128)S(1)} %get-tuple-element.154.cp_ref, bf16[64,256]{1,0:T(8,128)(2,1)S(1)} %get-tuple-element.146.sides_ref, ...), custom_call_target="tpu_custom_call" | custom-call | bytes 2445312 | tf_op jit(solution)/shard_map/pallas_call | solution.py:410
  (1 shorter events, 0.0 us)
Async XLA Ops:
  25.5 1.4 %collective-permute-start = (bf16[256,256]{1,0:T(8,128)(2,1)S(1)}, bf16[256,256]{1,0:T(8,128)(2,1)S(1)}, u32[]{:S(2)}, u32[]{:S(2)}) collective-permute-start(bf16[256,256]{1,0:T(8,128)(2,1)S(1)} %get-tuple-element.120.own_ref), channel_id=1, source_target_pairs={{0,8},{8,0},{16,24},{24,16},{32,40},{40,32},{48,56},{56,48},{64,72... | collective-permute-start | bytes 393224 | tf_op jit(solution)/shard_map/ppermute | solution.py:441
  43.8 5.3 %collective-permute-start.1 = (f32[2,4,512]{2,1,0:T(4,128)S(1)}, f32[2,4,512]{2,1,0:T(4,128)S(1)}, u32[]{:S(2)}, u32[]{:S(2)}) collective-permute-start(f32[2,4,512]{2,1,0:T(4,128)S(1)} %get-tuple-element.129.mine_ref), channel_id=1, source_target_pairs={{0,128},{128,0},{1,129},{129,1},{2,130},{130,2},{3,131},{131,3},{4... | collective-permute-start | bytes 49160 | tf_op jit(solution)/shard_map/ppermute | solution.py:437
  50.3 15.5 %all-to-all-start.2 = ((bf16[64,8,128]{2,1,0:T(8,128)(2,1)}), bf16[64,8,128]{2,1,0:T(8,128)(2,1)S(1)}, u32[]{:S(2)}, u32[]{:S(2)}) async-start(bf16[64,8,128]{2,1,0:T(8,128)(2,1)} %bitcast.9), calls=%async_computation.2 | async-start | bytes 262144 | tf_op jit(solution)/shard_map/all_to_all | solution.py:445
  58.6 8.4 %collective-permute-start.3 = (f32[64,512]{1,0:T(8,128)S(1)}, f32[64,512]{1,0:T(8,128)S(1)}, u32[]{:S(2)}, u32[]{:S(2)}) collective-permute-start(f32[64,512]{1,0:T(8,128)S(1)} %shard_map.193.mine_ref), channel_id=1, source_target_pairs={{0,128},{128,0},{1,129},{129,1},{2,130},{130,2},{3,131},{131,3},{4... | collective-permute-start | bytes 393224 | tf_op jit(solution)/shard_map/ppermute | solution.py:437
  66.2 1.4 %collective-permute-start.2 = (bf16[256,256]{1,0:T(8,128)(2,1)S(1)}, bf16[256,256]{1,0:T(8,128)(2,1)S(1)}, u32[]{:S(2)}, u32[]{:S(2)}) collective-permute-start(bf16[256,256]{1,0:T(8,128)(2,1)S(1)} %get-tuple-element.138), channel_id=1, source_target_pairs={{0,8},{8,0},{16,24},{24,16},{32,40},{40,32},{48,56},{56,48},{64,72... | collective-permute-start | bytes 393224 | tf_op jit(solution)/shard_map/ppermute | solution.py:441
